TPU v7x, 32 devices: a whole 2x2x4 slice. The times are simulated.
32 devices in a mesh: groups: 2 (over y), strip: 4 (over z), angle: 2 (over x), depth: 2 (over core).
Axes of the slice: x: 2, y: 2, z: 4, core: 2. Of those that a mesh axis runs over, the one named last changes fastest.
Arguments:
- crystal: bfloat16 [16, 2, 512, 384], P(('groups', 'depth'), None, 'strip'), parts along dimension 0, may hold values from -4 to 4
- probe: bfloat16 [2, 256, 256], replicated, may hold values from -5 to 5
- amplitude: bfloat16 [4, 2048, 256], P('angle', ('groups', 'strip', 'depth')), parts along dimension 1, may hold values from 0.5 to 8
- shear: int32 [16, 8], P(('groups', 'angle'), 'depth'), parts along dimension 0, may hold values from 0 to 15
- scan_x: int32 [4, 4, 2], P(('groups', 'angle')), parts along dimension 0, may hold values from 0 to 112
- scan_y: int32 [4, 4, 2], P(('groups', 'angle')), parts along dimension 0, may hold values from 0 to 128
- slot_angle: int32 [4, 4, 2], P(('groups', 'angle')), parts along dimension 0, may hold values from 0 to 3
- owner_slot: int32 [4, 4, 2], P(('groups', 'angle')), parts along dimension 0, may hold values from 0 to 1, each once within a row
- counts: int32 [4, 4], P(('groups', 'angle')), parts along dimension 0, may hold values from 1 to 2
Outputs:
- gradient: float32 [16, 2, 512, 384], P(('groups', 'depth'), None, ('strip', 'angle')), parts along dimension 0
There are 2 independent parts, one for each index of `groups`. A program takes and returns all parts, laid end to end along the dimension named above; an argument that names none is the same for every part. Nothing has to cross between parts.
Inputs may be any that keep to these rules, and one draw needn't show every extreme that they name: `owner_slot`: for each angle group and home strip, the 2 entries are a permutation of 0 to 1.
All inputs are finite; a program needn't handle non-finite values.
Results may differ from a plain program's by a relative error of at most 0.02.
Values may be sent and summed in bfloat16 or wider, within the bound.
No kernel may reach another device: no remote copies, remote signals or barrier semaphores. Data moves between devices by JAX's collectives and lax.ppermute only.
A program may use at most 64 MiB of HBM per device.

v0:
```python
import math

import jax
import jax.numpy as jnp
from jax import lax
from jax.sharding import PartitionSpec as P

FRAME = 256
WX = 128
SHEAR = 16
BAND = 144


def spot(*values):
    return tuple((jnp.asarray(value, jnp.int32) for value in values))


def dft_parts():
    index_row = jnp.arange(FRAME, dtype=jnp.int32)
    wound = index_row[:, None] * index_row[None, :] % FRAME
    phase = wound.astype(jnp.float32) * (2.0 * math.pi / FRAME)
    scaling = 1.0 / math.sqrt(FRAME)
    return (
        (jnp.cos(phase) * scaling).astype(jnp.bfloat16),
        (-jnp.sin(phase) * scaling).astype(jnp.bfloat16),
    )


def complex_times(left, right, sign):
    left_re = left[..., 0, :, :]
    left_im = left[..., 1, :, :]
    right_re = right[..., 0, :, :]
    right_im = right[..., 1, :, :]
    out_re = left_re * right_re - sign * left_im * right_im
    out_im = left_re * right_im + sign * left_im * right_re
    return jnp.stack([out_re, out_im], axis=-3)


def right_product(block, table_re, table_im, sign):
    part_re = block[..., 0, :, :]
    part_im = block[..., 1, :, :]

    def multiply(left, table):
        return jnp.einsum("...b,bc->...c", left, table, preferred_element_type=jnp.float32)

    first = multiply(part_re, table_re)
    second = multiply(part_im, table_im)
    third = multiply(part_re, table_im)
    fourth = multiply(part_im, table_re)
    return jnp.stack([first - sign * second, sign * third + fourth], axis=-3)


def body(crystal, probe, amplitude, shear, scan_x, scan_y, slot_angle, owner_slot, counts):
    strips = lax.axis_size("strip")
    strip_here = lax.axis_index("strip")
    layer_count = crystal.shape[0]
    slot_count = owner_slot.shape[2]
    quarter = strips // 4
    lanes = slot_count // quarter
    table_re, table_im = dft_parts()
    pad_re = jnp.pad(table_re, ((BAND, BAND), (0, 0)))
    pad_im = jnp.pad(table_im, ((BAND, BAND), (0, 0)))
    probe_pad = jnp.pad(probe, ((0, 0), (BAND, BAND), (0, 0)))
    offsets = scan_x[0]
    columns = scan_y[0]
    angles = slot_angle[0]
    owners = owner_slot[0]
    limits = counts[0]
    slot_ids = jnp.arange(slot_count, dtype=jnp.int32)
    reaches = jnp.arange(3, dtype=jnp.int32)
    home_rows = strip_here - reaches
    home_valid = (home_rows >= 0) & (home_rows <= strips - 3)
    home_safe = jnp.clip(home_rows, 0, strips - 1)
    sent_quota = owners[home_safe]
    sent_lane = sent_quota // quarter
    sent_alive = home_valid[:, None] & (slot_ids[None, :] < limits[home_safe][:, None])
    owner_strip = (home_safe[:, None] + 4 * (sent_quota % quarter) + 1) % strips
    destination = jnp.where(sent_alive, owner_strip * lanes + sent_lane, strips * lanes).reshape(-1)
    lift_rows = shear[angles[home_safe]].reshape(3 * slot_count, layer_count)
    corners = columns[home_safe].reshape(-1)
    crystal_pad = jnp.pad(crystal, ((0, 0), (0, 0), (SHEAR, SHEAR), (0, 0)))

    def project(lift_row, corner):
        gathered = jnp.zeros((2, BAND, FRAME), jnp.float32)
        for layer_index in range(layer_count):
            window = lax.dynamic_slice(
                crystal_pad[layer_index], spot(0, lift_row[layer_index], corner), (2, BAND, FRAME)
            )
            gathered = gathered + window.astype(jnp.float32)
        return gathered.astype(jnp.bfloat16)

    slab_bands = jax.vmap(project)(lift_rows, corners)
    outgoing = (
        jnp.zeros((strips * lanes, 2, BAND, FRAME), jnp.bfloat16)
        .at[destination]
        .set(slab_bands, mode="drop")
    )
    arrived = lax.all_to_all(outgoing, "strip", split_axis=0, concat_axis=0, tiled=True)
    quotas = jnp.arange(slot_count, dtype=jnp.int32)
    owned_lane = quotas // quarter
    source_home = (strip_here - 1 - 4 * (quotas % quarter)) % strips
    source_valid = source_home <= strips - 3
    matches = owners[source_home] == quotas[:, None]
    chosen = jnp.sum(jnp.where(matches, slot_ids[None, :], 0), axis=1)
    owned_alive = source_valid & (chosen < limits[source_home])
    owned_offset = offsets[source_home, chosen]
    row_starts = reaches[None, :] * WX - owned_offset[:, None] - SHEAR + BAND
    senders = (source_home[:, None] + reaches[None, :]) % strips
    sender_slots = senders * lanes + owned_lane[:, None]
    received = arrived[sender_slots]

    def take_rows(table, axis_pick):
        return jax.vmap(
            jax.vmap(lambda first_row: lax.dynamic_slice_in_dim(table, first_row, BAND, axis_pick))
        )(row_starts)

    rows_re = take_rows(pad_re, 0)
    rows_im = take_rows(pad_im, 0)
    probe_rows = take_rows(probe_pad, 1).astype(jnp.float32)
    exit_band = complex_times(probe_rows, received.astype(jnp.float32), 1.0).astype(jnp.bfloat16)
    section = right_product(exit_band, table_re, table_im, 1.0).astype(jnp.bfloat16)
    part_re = rows_re
    part_im = rows_im

    def multiply(table, block):
        return jnp.einsum("qkic,qkib->cqb", table, block, preferred_element_type=jnp.float32)

    spec_re = multiply(part_re, section[:, :, 0]) - multiply(part_im, section[:, :, 1])
    spec_im = multiply(part_im, section[:, :, 0]) + multiply(part_re, section[:, :, 1])
    spectrum = lax.psum_scatter(
        jnp.stack([spec_re, spec_im], axis=1).astype(jnp.bfloat16),
        "depth",
        scatter_dimension=0,
        tiled=True,
    ).astype(jnp.float32)
    spec_re = spectrum[:, 0]
    spec_im = spectrum[:, 1]
    magnitude = jnp.sqrt(spec_re * spec_re + spec_im * spec_im)
    measured = jnp.swapaxes(amplitude, 0, 1).astype(jnp.float32)
    factor = (1.0 - measured / jnp.maximum(magnitude, 1.0)) * owned_alive[None, :, None].astype(
        jnp.float32
    )
    residual = (spectrum * factor[:, None]).astype(jnp.bfloat16)
    inverse_rows = right_product(residual, table_re, table_im, -1.0).astype(jnp.bfloat16)
    half_rows = inverse_rows.shape[0]
    column_start = lax.axis_index("depth") * half_rows
    home_owned = jnp.where(owned_alive[:, None], sender_slots, strips * lanes).reshape(-1)
    share_rows = BAND // lax.axis_size("depth")
    first_row = jnp.int32(0)
    part_re = lax.dynamic_slice(
        rows_re,
        spot(0, 0, first_row, column_start),
        (slot_count, 3, lax.axis_size("depth") * share_rows, half_rows),
    )
    part_im = lax.dynamic_slice(
        rows_im,
        spot(0, 0, first_row, column_start),
        (slot_count, 3, lax.axis_size("depth") * share_rows, half_rows),
    )

    def multiply(table, block):
        return jnp.einsum("qkic,cqb->qkib", table, block, preferred_element_type=jnp.float32)

    wave_re = multiply(part_re, inverse_rows[:, 0]) + multiply(part_im, inverse_rows[:, 1])
    wave_im = multiply(part_re, inverse_rows[:, 1]) - multiply(part_im, inverse_rows[:, 0])
    pieces = lax.psum_scatter(
        jnp.moveaxis(
            complex_times(probe_rows, jnp.stack([wave_re, wave_im], axis=2), -1.0), 3, 0
        ).astype(jnp.bfloat16),
        "depth",
        scatter_dimension=0,
        tiled=True,
    ).astype(jnp.float32)
    pieces = (
        jnp.moveaxis(pieces, 0, 3)
        .astype(jnp.bfloat16)
        .reshape(slot_count * 3, 2, share_rows, FRAME)
    )
    returning = (
        jnp.zeros((strips * lanes, 2, share_rows, FRAME), jnp.bfloat16)
        .at[home_owned]
        .set(pieces, mode="drop")
    )
    returned = lax.all_to_all(returning, "strip", split_axis=0, concat_axis=0, tiled=True)
    returned = lax.all_gather(returned, "depth", axis=2, tiled=True)
    back_bands = returned[(owner_strip * lanes + sent_lane).reshape(-1)]
    weights = sent_alive.reshape(-1).astype(jnp.float32)

    def deposit(item_index, gradient_pad):
        contribution = back_bands[item_index].astype(jnp.float32) * weights[item_index]
        lift_row = lift_rows[item_index]
        corner = corners[item_index]
        for layer_index in range(layer_count):
            position = spot(layer_index, 0, lift_row[layer_index], corner)
            current = lax.dynamic_slice(gradient_pad, position, (1, 2, BAND, FRAME))
            gradient_pad = lax.dynamic_update_slice(
                gradient_pad, current + contribution[None], position
            )
        return gradient_pad

    start_pad = jnp.zeros((layer_count, 2, WX + 2 * SHEAR, crystal.shape[3]), jnp.float32)
    gradient_pad = lax.fori_loop(0, 3 * slot_count, deposit, start_pad)
    gradient = gradient_pad[:, :, SHEAR : SHEAR + WX].astype(jnp.bfloat16)
    angle_count = lax.axis_size("angle")
    scaling = 1.0 / (shear.shape[0] * angle_count)
    shared = lax.psum_scatter(gradient, "angle", scatter_dimension=2, tiled=True).astype(
        jnp.float32
    )
    return shared * scaling


def solution(mesh):
    placed = (
        P(("groups", "depth"), None, "strip", None),
        P(),
        P("angle", ("groups", "strip", "depth"), None),
        P(("groups", "angle"), "depth"),
        P(("groups", "angle"), None, None),
        P(("groups", "angle"), None, None),
        P(("groups", "angle"), None, None),
        P(("groups", "angle"), None, None),
        P(("groups", "angle"), None),
    )
    return jax.shard_map(
        body,
        mesh=mesh,
        in_specs=placed,
        out_specs=P(("groups", "depth"), None, ("strip", "angle"), None),
        check_vma=False,
    )
```

profile of v0, /device:TPU:17, one launch (start us, length us, event | category | flops | bytes accessed | tf_op | source)
XLA Modules:
  0.0 371.5 jit_solution(13340963413556306195)
XLA Ops:
  11.7 12.6 %while.21 = (s32[]{:T(128)}, bf16[2,160,384]{2,1,0:T(8,128)(2,1)S(1)}, s32[6,3]{1,0:T(8,128)S(1)}, bf16[6,2,144,256]{3,2,1,0:T(8,128)(2,1)S(1)}, s32[]{:T(128)}) while((s32[]{:T(128)}, bf16[2,160,384]{2,1,0:T(8,128)(2,1)S(1)}, s32[6,3]{1,0:T(8,128)S(1)}, bf16[6,2,144,256]{3,2,1,0:T(8,128)(2,1)S(1)}, s32[]{:T(128)}) %tuple.156), condition=%wide.while_cond.1, body=%wide.while_body.1.sunk | while | flops 2 | bytes 295029 | solution.py:86
  12.4 1.4 bitcast_dynamic-update-slice_fusion.13
  14.5 1.4 bitcast_dynamic-update-slice_fusion.13
  16.6 1.4 bitcast_dynamic-update-slice_fusion.13
  18.7 1.4 bitcast_dynamic-update-slice_fusion.13
  20.8 1.4 bitcast_dynamic-update-slice_fusion.13
  22.9 1.4 bitcast_dynamic-update-slice_fusion.13
  24.4 12.9 %while.22 = (s32[]{:T(128)}, bf16[2,160,384]{2,1,0:T(8,128)(2,1)S(1)}, s32[6,3]{1,0:T(8,128)S(1)}, bf16[6,2,144,256]{3,2,1,0:T(8,128)(2,1)S(1)}, s32[]{:T(128)}) while((s32[]{:T(128)}, bf16[2,160,384]{2,1,0:T(8,128)(2,1)S(1)}, s32[6,3]{1,0:T(8,128)S(1)}, bf16[6,2,144,256]{3,2,1,0:T(8,128)(2,1)S(1)}, s32[]{:T(128)}) %tuple.153), condition=%wide.while_cond.2, body=%wide.while_body.2.sunk | while | flops 2 | bytes 295029 | solution.py:86
  25.0 1.4 bitcast_dynamic-update-slice_fusion.14
  27.2 1.4 bitcast_dynamic-update-slice_fusion.14
  29.3 1.4 bitcast_dynamic-update-slice_fusion.14
  31.5 1.4 bitcast_dynamic-update-slice_fusion.14
  33.6 1.4 bitcast_dynamic-update-slice_fusion.14
  35.8 1.4 bitcast_dynamic-update-slice_fusion.14
  37.3 12.4 %while.23 = (s32[]{:T(128)}, bf16[2,160,384]{2,1,0:T(8,128)(2,1)S(1)}, s32[6,3]{1,0:T(8,128)S(1)}, bf16[6,2,144,256]{3,2,1,0:T(8,128)(2,1)S(1)}, s32[]{:T(128)}) while((s32[]{:T(128)}, bf16[2,160,384]{2,1,0:T(8,128)(2,1)S(1)}, s32[6,3]{1,0:T(8,128)S(1)}, bf16[6,2,144,256]{3,2,1,0:T(8,128)(2,1)S(1)}, s32[]{:T(128)}) %tuple.150), condition=%wide.while_cond.3, body=%wide.while_body.3.sunk | while | flops 2 | bytes 295029 | solution.py:86
  50.8 15.6 %while.24 = (s32[]{:T(128)}, bf16[2,160,384]{2,1,0:T(8,128)(2,1)S(1)}, s32[6,3]{1,0:T(8,128)S(1)}, bf16[6,2,144,256]{3,2,1,0:T(8,128)(2,1)}, s32[]{:T(128)}) while((s32[]{:T(128)}, bf16[2,160,384]{2,1,0:T(8,128)(2,1)S(1)}, s32[6,3]{1,0:T(8,128)S(1)}, bf16[6,2,144,256]{3,2,1,0:T(8,128)(2,1)}, s32[]{:T(128)}) %tuple.147), condition=%wide.while_cond.4, body=%wide.while_body.4.sunk | while | flops 2 | bytes 296553 | solution.py:86
  51.5 1.9 bitcast_dynamic-update-slice_fusion.16
  54.1 2.0 bitcast_dynamic-update-slice_fusion.16
  56.7 2.0 bitcast_dynamic-update-slice_fusion.16
  59.3 2.0 bitcast_dynamic-update-slice_fusion.16
  61.9 2.0 bitcast_dynamic-update-slice_fusion.16
  64.5 1.9 bitcast_dynamic-update-slice_fusion.16
  69.4 1.9 add_convert_fusion
  72.3 2.8 scatter_fusion
  75.1 4.9 %all-to-all-start = ((bf16[8,2,144,256]{3,2,1,0:T(8,128)(2,1)}), bf16[8,2,144,256]{3,2,1,0:T(8,128)(2,1)}, u32[]{:S(2)}, u32[]{:S(2)}) async-start(bf16[8,2,144,256]{3,2,1,0:T(8,128)(2,1)} %scatter_fusion), calls=%async_computation | async-start | bytes 2359296 | tf_op jit(solution)/shard_map/all_to_all | solution.py:98
  83.2 7.5 %while.25 = (s32[]{:T(128)}, bf16[544,256]{1,0:T(8,128)(2,1)S(1)}, s32[6,2]{0,1:T(2,128)S(1)}, bf16[6,144,256]{2,1,0:T(8,128)(2,1)S(1)}, s32[]{:T(128)}) while((s32[]{:T(128)}, bf16[544,256]{1,0:T(8,128)(2,1)S(1)}, s32[6,2]{0,1:T(2,128)S(1)}, bf16[6,144,256]{2,1,0:T(8,128)(2,1)S(1)}, s32[]{:T(128)}) %tuple.162), condition=%wide.while_cond.5, body=%wide.while_body.5.sunk | while | flops 2 | bytes 147553 | solution.py:114
  91.6 2.7 gather_fusion.6
  96.2 7.3 %while.20 = (s32[]{:T(128)}, bf16[544,256]{1,0:T(8,128)(2,1)S(1)}, s32[6,2]{0,1:T(2,128)S(1)}, bf16[6,144,256]{2,1,0:T(8,128)(2,1)S(1)}, s32[]{:T(128)}) while((s32[]{:T(128)}, bf16[544,256]{1,0:T(8,128)(2,1)S(1)}, s32[6,2]{0,1:T(2,128)S(1)}, bf16[6,144,256]{2,1,0:T(8,128)(2,1)S(1)}, s32[]{:T(128)}) %tuple.176), condition=%wide.while_cond, body=%wide.while_body.sunk | while | flops 2 | bytes 147553 | solution.py:114
  103.5 1.6 all-to-all-done
  105.1 2.0 gather_fusion.9
  116.2 10.5 %reduce-scatter.10.cloned.1.call-done = bf16[128,1024]{1,0:T(8,128)(2,1)} async-done(((bf16[256,1024]{1,0:T(8,128)(2,1)}), bf16[128,1024]{1,0:T(8,128)(2,1)}) %reduce-scatter.10.cloned.1.call-update) | async-done | bytes 262160
  134.8 2.1 reshape.729
  137.5 9.2 %reduce-scatter.12.cloned.1.call-done = bf16[72,3072]{1,0:T(8,128)(2,1)} async-done(((bf16[144,3072]{1,0:T(8,128)(2,1)}), bf16[72,3072]{1,0:T(8,128)(2,1)}) %reduce-scatter.12.cloned.1.call-update) | async-done | bytes 442384
  146.6 1.7 reshape.730
  149.6 17.8 %all_to_all.10 = bf16[8,2,72,256]{3,2,1,0:T(8,128)(2,1)} all-to-all(bf16[8,2,72,256]{3,2,1,0:T(8,128)(2,1)S(1)} %scatter_fusion.1), channel_id=1, replica_groups=mesh['groups'=2,'strip'=4,'angle'=2,'depth'=2] {'strip'}, dimensions={0} | all-to-all | bytes 1179648 | tf_op jit(solution)/shard_map/all_to_all | solution.py:184
  167.9 11.2 %all-gather.2.cloned.1.call-done = bf16[8,2,144,256]{3,2,1,0:T(8,128)(2,1)} async-done(((bf16[8,2,72,256]{3,2,1,0:T(8,128)(2,1)}), bf16[8,2,144,256]{3,2,1,0:T(8,128)(2,1)}) %all-gather.2.cloned.1.call-update) | async-done | bytes 1179664 | tf_op jit(solution)/shard_map/all_gather | solution.py:185
  179.2 1.9 gather_fusion.10
  181.2 157.3 %while.19 = (s32[]{:T(128)}, f32[4,2,160,384]{3,2,1,0:T(8,128)S(1)}, s32[6,4]{1,0:T(8,128)S(1)}, s32[6]{0:T(128)S(1)}, bf16[6,2,144,256]{3,2,1,0:T(8,128)(2,1)S(...) while((s32[]{:T(128)}, ...), condition=%wide.region_6.7_spmd, body=%wide.region_5.6_spmd.sunk | while | flops 884753 | bytes 5308875 | solution.py:202
  188.2 3.0 dynamic_update_slice.32
  193.9 3.0 dynamic_update_slice.33
  199.6 3.0 dynamic_update_slice.34
  205.3 3.0 dynamic_update_slice.35
  215.3 3.0 dynamic_update_slice.32
  221.0 3.0 dynamic_update_slice.33
  226.7 3.0 dynamic_update_slice.34
  232.4 3.0 dynamic_update_slice.35
  242.4 3.0 dynamic_update_slice.32
  248.1 3.0 dynamic_update_slice.33
  253.8 3.0 dynamic_update_slice.34
  259.5 3.0 dynamic_update_slice.35
  269.6 3.0 dynamic_update_slice.32
  275.3 3.0 dynamic_update_slice.33
  281.0 3.0 dynamic_update_slice.34
  286.7 3.0 dynamic_update_slice.35
  296.7 1.6 dynamic_update_slice.32
  301.0 1.6 dynamic_update_slice.33
  305.4 1.6 dynamic_update_slice.34
  309.8 1.6 dynamic_update_slice.35
  318.4 3.0 dynamic_update_slice.32
  324.1 3.0 dynamic_update_slice.33
  329.8 3.0 dynamic_update_slice.34
  335.5 3.0 dynamic_update_slice.35
  339.5 23.5 %reduce-scatter.8.cloned.1.call-done = bf16[4,2,64,384]{3,2,1,0:T(8,128)(2,1)} async-done(((bf16[4,2,128,384]{3,2,1,0:T(8,128)(2,1)}), bf16[4,2,64,384]{3,2,1,0:T(8,128)(2,1)}) %reduce-scatter.8.cloned.1.call-update) | async-done | bytes 393232 | tf_op jit(solution)/shard_map/reduce_scatter | solution.py:206
  363.0 1.9 convert_multiply_fusion.1
  (271 shorter events, 107.2 us)
Async XLA Ops:
  6.5 4.4 %copy-start = (s32[4,4]{1,0:T(4,128)S(1)}, s32[4,4]{1,0:T(4,128)}, u32[]{:S(2)}) copy-start(s32[4,4]{1,0:T(4,128)} %param.14) | copy-start | bytes 196
  37.3 29.1 %copy-start.1 = (s32[1,4]{1,0:T(1,128)S(1)}, s32[1,4]{1,0:T(1,128)}, u32[]{:S(2)}) copy-start(s32[1,4]{1,0:T(1,128)} %param.19) | copy-start | bytes 52
  49.7 19.6 %copy-start.3 = (bf16[6,2,144,256]{3,2,1,0:T(8,128)(2,1)}, bf16[6,2,144,256]{3,2,1,0:T(8,128)(2,1)S(1)}, u32[]{:S(2)}) copy-start(bf16[6,2,144,256]{3,2,1,0:T(8,128)(2,1)S(1)} %get-tuple-element.146) | copy-start | bytes 2654212
  49.7 18.1 %copy-start.9 = (s32[1,4,2]{1,2,0:T(2,128)S(1)}, s32[1,4,2]{1,2,0:T(2,128)}, u32[]{:S(2)}) copy-start(s32[1,4,2]{1,2,0:T(2,128)} %param.18) | copy-start | bytes 100
  75.1 7.2 %copy-start.2 = (s32[1,4,2]{1,2,0:T(2,128)S(1)}, s32[1,4,2]{1,2,0:T(2,128)}, u32[]{:S(2)}) copy-start(s32[1,4,2]{1,2,0:T(2,128)} %param.15) | copy-start | bytes 100
  75.1 30.0 %all-to-all-start = ((bf16[8,2,144,256]{3,2,1,0:T(8,128)(2,1)}), bf16[8,2,144,256]{3,2,1,0:T(8,128)(2,1)}, u32[]{:S(2)}, u32[]{:S(2)}) async-start(bf16[8,2,144,256]{3,2,1,0:T(8,128)(2,1)} %scatter_fusion), calls=%async_computation | async-start | bytes 2359296 | tf_op jit(solution)/shard_map/all_to_all | solution.py:98
  80.1 10.9 %copy-start.4 = (bf16[2,256,256]{2,1,0:T(8,128)(2,1)S(1)}, bf16[2,256,256]{2,1,0:T(8,128)(2,1)}, u32[]{:S(2)}) copy-start(bf16[2,256,256]{2,1,0:T(8,128)(2,1)} %param.12) | copy-start | bytes 786436
  80.1 46.6 %reduce-scatter.10.cloned.1.call-start = ((), (), s32[]{:S(2)}) async-start(), calls=%async_computation.7 | async-start | bytes 786432
  81.1 10.5 %copy-start.7 = (s32[1024]{0:T(1024)}, s32[1024]{0:T(1024)S(1)}, u32[]{:S(2)}) copy-start(s32[1024]{0:T(1024)S(1)} %pad_clamp_fusion.2) | copy-start | bytes 12292
  81.8 0.6 copy-start.10
  114.0 2.1 copy-start.11
  114.1 13.9 %copy-start.5 = (bf16[2,128,256]{2,1,0:T(8,128)(2,1)S(1)}, bf16[2,128,256]{2,1,0:T(8,128)(2,1)}, u32[]{:S(2)}) copy-start(bf16[2,128,256]{2,1,0:T(8,128)(2,1)} %param.13) | copy-start | bytes 393220
  115.1 31.5 %reduce-scatter.12.cloned.1.call-start = ((), (), s32[]{:S(2)}) async-start(), calls=%async_computation.8 | async-start | bytes 1327104
  137.0 42.2 %all-gather.2.cloned.1.call-start = ((), (), s32[]{:S(2)}) async-start(), calls=%async_computation.5 | async-start | bytes 1769472 | tf_op jit(solution)/shard_map/all_gather | solution.py:185
  148.5 19.3 %copy-start.6 = (f32[3,2]{1,0:T(4,128)S(1)}, f32[3,2]{1,0:T(4,128)}, u32[]{:S(2)}) copy-start(f32[3,2]{1,0:T(4,128)} %get-tuple-element.313) | copy-start | bytes 76
  148.6 19.4 %copy-start.8 = (s32[6]{0:T(128)S(1)}, s32[6]{0:T(128)}, u32[]{:S(2)}) copy-start(s32[6]{0:T(128)} %get-tuple-element.251) | copy-start | bytes 76
  167.4 195.6 %reduce-scatter.8.cloned.1.call-start = ((), (), s32[]{:S(2)}) async-start(), calls=%async_computation.6 | async-start | bytes 1179648 | tf_op jit(solution)/shard_map/reduce_scatter | solution.py:206
Sparse Core Ops, SparseCore 0:
  115.2 11.4 reduce-scatter.9
  137.1 9.4 reduce-scatter.11
  167.6 11.5 all-gather.1
  339.6 23.3 reduce-scatter.7
where the time goes:
time: 375 us; the launch traced here: 371 us
  local copies, waits for them, and re-layouts  177 us (47%)
  loops' own time  60.1 us (16%)
  waiting for transfers between devices  56.1 us (15%)
  other arithmetic  29.5 us (8%)
  blocking collectives  17.8 us (5%)
  between operations  13.7 us (4%)
  matrix products  12.1 us (3%)
  starting transfers between devices  5.52 us (1%)
    gather x108, local copies, waits for them, and re-layouts  67.2 us
    dynamic_update_slice x24, local copies, waits for them, and re-layouts, deposit(): lax.dynamic_update_slice(gradient_pad, current + contribution[None], posi...  65.9 us
    another operation x1, loops' own time, body(): gradient_pad = lax.fori_loop(0, 3 * slot_count, deposit, start_pad)  59.2 us
    reduce_scatter x1, waiting for transfers between devices, body(): lax.psum_scatter(gradient, 'angle', scatter_dimension=2, tiled=True)  23.5 us
    add x24, other arithmetic, deposit(): current + contribution[None]  20.2 us
    unnamed x6, waiting for transfers between devices  19.8 us
    all_to_all x1, blocking collectives, body(): lax.all_to_all(returning, 'strip', split_axis=0, concat_axis=0, tiled=True)  17.8 us
    all_gather x1, waiting for transfers between devices, body(): returned = lax.all_gather(returned, 'depth', axis=2, tiled=True)  11.2 us
  transfers between devices with their start and end apart: 5, of which 5 were waited for; matrix products, arithmetic and copies ran while one was open for 6% of the time, Pallas kernels for 0%

commit v1 on v0

v1 whole, which is shorter than its diff:
```python
import functools
import math

import jax
import jax.numpy as jnp
import ml_dtypes
import numpy as np
from jax import lax
from jax.experimental import pallas as pl
from jax.experimental.pallas import tpu as pltpu
from jax.sharding import PartitionSpec as P

BF = jnp.bfloat16
F32 = jnp.float32
VMEM_BYTES = 48 * 2**20
MAX_SHEAR = 16


def dft_table(n):
    index = np.arange(n, dtype=np.int64)
    phase = (index[:, None] * index[None, :] % n).astype(np.float64) * (2.0 * math.pi / n)
    scale = 1.0 / math.sqrt(n)
    table = np.stack([np.cos(phase) * scale, -np.sin(phase) * scale])
    return table.astype(np.float32).astype(ml_dtypes.bfloat16)


def dot(left, right):
    return jnp.dot(left, right, preferred_element_type=F32)


def band_matrix(rows, cols, offset):
    gap = lax.broadcasted_iota(jnp.int32, (rows, cols), 1) - lax.broadcasted_iota(
        jnp.int32, (rows, cols), 0
    )
    return jnp.where(gap == offset, 1.0, 0.0).astype(BF)


def clip(value, top):
    return jnp.minimum(jnp.maximum(value, 0), top)


def slot_of(owner_at, slots, quota):
    found = jnp.int32(0)
    for slot in range(slots):
        found = jnp.where(owner_at(slot) == quota, slot, found)
    return found


def project_kernel(strips, slots, mine, *refs):
    shear, scan_x, scan_y, slot_angle, owner, crystal = refs[:6]
    layers, _, wx, ny = crystal.shape
    if mine:
        arrived, moving, middle, table = refs[6:]
    else:
        (out,) = refs[6:]
    strip = lax.axis_index("strip")
    depth = lax.axis_index("depth")
    half = depth if mine else 1 - depth
    if mine:
        place = 0
        for i in range(shear.shape[0]):
            for z in range(layers):
                table[place] = shear[i, z]
                place += 1
        for ref in (scan_y, slot_angle, owner):
            for i in range(strips):
                for m in range(slots):
                    table[place] = ref[0, i, m]
                    place += 1
    bricks = [
        jnp.concatenate([crystal[z, part] for z in range(layers)], axis=0) for part in range(2)
    ]
    frame = out.shape[-1] if not mine else moving.shape[-1]
    for kind in range(2):
        home = clip(strip - (2 * half if kind == 0 else 1), strips - 1)
        back = wx * half if kind == 0 else wx * (1 - half)
        for quota in range(slots):
            slot = slot_of(lambda m: owner[0, home, m], slots, quota)
            start = scan_x[0, home, slot] - back
            angle = slot_angle[0, home, slot]
            rows = jnp.concatenate(
                [band_matrix(wx, wx, start + shear[angle, z]) for z in range(layers)], axis=1
            )
            columns = band_matrix(ny, frame, -scan_y[0, home, slot])
            for part in range(2):
                lifted = dot(rows, bricks[part]).astype(BF)
                band = dot(lifted, columns)
                if mine:
                    band = band + arrived[kind, quota, part].astype(F32)
                    (moving if kind == 0 else middle)[quota, part] = band.astype(BF)
                else:
                    out[kind, quota, part] = band.astype(BF)


def transform_kernel(strips, angles, slots, window, *refs):
    scan_x, owner, counts = refs[:3]
    moved, moved_far, middle, middle_far, near, far, probe, tab = refs[3:11]
    outs = refs[11 : 11 + 2 * angles]
    waves, levels = refs[11 + 2 * angles :]
    quarter = strips // 4
    strip = lax.axis_index("strip")
    plane = lax.axis_index("angle")
    depth = lax.axis_index("depth")
    half = moved.shape[2]
    frame = moved.shape[3]
    f_re = tab[0]
    f_im = tab[1]
    n_im = -f_im
    for quota in range(slots):
        home = lax.rem(strip + (strips - 1) + 4 * (strips - quota % quarter), strips)
        slot = slot_of(lambda m: owner[0, home, m], slots, quota)
        alive = jnp.logical_and(home <= strips - 3, slot < counts[0, home])
        alive = jnp.where(alive, 1.0, 0.0).astype(F32)
        for side, (a_ref, m_ref) in enumerate(((moved, middle), (moved_far, middle_far))):
            row = pl.multiple_of((depth if side == 0 else 1 - depth) * half, half)
            w_re = a_ref[quota, 0].astype(F32) + m_ref[quota, 0].astype(F32)
            w_im = a_ref[quota, 1].astype(F32) + m_ref[quota, 1].astype(F32)
            p_re = probe[0, pl.ds(row, half)].astype(F32)
            p_im = probe[1, pl.ds(row, half)].astype(F32)
            waves[quota, pl.ds(row, half), :frame] = (p_re * w_re - p_im * w_im).astype(BF)
            waves[quota, pl.ds(row, half), frame:] = (p_re * w_im + p_im * w_re).astype(BF)
        exit_wave = waves[quota]
        section = jnp.concatenate(
            [
                dot(exit_wave, jnp.concatenate([f_re, n_im], axis=0)).astype(BF),
                dot(exit_wave, jnp.concatenate([f_im, f_re], axis=0)).astype(BF),
            ],
            axis=0,
        )
        s_re = dot(jnp.concatenate([f_re, n_im], axis=1), section)
        s_im = dot(jnp.concatenate([f_im, f_re], axis=1), section)
        magnitude = jnp.maximum(jnp.sqrt(s_re * s_re + s_im * s_im), 1.0)
        for side, a_ref in enumerate((near, far)):
            row = pl.multiple_of((depth if side == 0 else 1 - depth) * half, half)
            levels[quota, pl.ds(row, half)] = a_ref[quota]
        measured = levels[quota].astype(F32)
        factor = (1.0 - measured / magnitude) * alive
        residual = jnp.concatenate(
            [(s_re * factor).astype(BF), (s_im * factor).astype(BF)], axis=1
        )
        inverse = jnp.concatenate(
            [
                dot(residual, jnp.concatenate([f_re, f_im], axis=0)).astype(BF),
                dot(residual, jnp.concatenate([n_im, f_re], axis=0)).astype(BF),
            ],
            axis=0,
        )
        b_re = dot(jnp.concatenate([f_re, f_im], axis=1), inverse)
        b_im = dot(jnp.concatenate([n_im, f_re], axis=1), inverse)
        p_re = probe[0].astype(F32)
        p_im = probe[1].astype(F32)
        back = jnp.concatenate(
            [
                (p_re * b_re + p_im * b_im).astype(BF),
                (p_re * b_im - p_im * b_re).astype(BF),
            ],
            axis=1,
        )
        offset = scan_x[0, home, slot]
        share = window - MAX_SHEAR
        for shift in range(angles):
            target = lax.rem(plane + shift, angles)
            for kind in range(2):
                reach = 2 * depth if kind == 0 else 1
                first = reach * (share * angles) + share * target - offset - MAX_SHEAR
                cut = dot(band_matrix(window, frame, first), back).astype(BF)
                outs[2 * shift + kind][quota, 0] = cut[:, :frame]
                outs[2 * shift + kind][quota, 1] = cut[:, frame:]


def deposit_kernel(strips, angles, slots, scale, *refs):
    tables = refs[:angles]
    blocks = refs[angles : angles + 3 * angles]
    (out,) = refs[4 * angles :]
    layers, _, share, ny = out.shape
    window, frame = blocks[0].shape[2:]
    strip = lax.axis_index("strip")
    depth = lax.axis_index("depth")
    count = strips * slots
    rows = []
    values = ([], [])
    for shift in range(angles):
        table = tables[shift]
        base = table.shape[0] - 3 * count
        for kind in range(3):
            reach = (2 * depth, 2 - 2 * depth, 1)[kind]
            home = clip(strip - reach, strips - 1)
            block = blocks[3 * shift + kind]
            for quota in range(slots):
                slot = slot_of(
                    lambda m: table[base + 2 * count + home * slots + m], slots, quota
                )
                column = table[base + home * slots + slot]
                angle = table[base + count + home * slots + slot]
                rows.append(
                    jnp.concatenate(
                        [
                            band_matrix(share, window, MAX_SHEAR - table[angle * layers + z])
                            for z in range(layers)
                        ],
                        axis=0,
                    )
                )
                columns = band_matrix(frame, ny, column)
                for part in range(2):
                    values[part].append(dot(block[quota, part], columns).astype(BF))
    left = jnp.concatenate(rows, axis=1)
    for part in range(2):
        total = dot(left, jnp.concatenate(values[part], axis=0)) * scale
        for z in range(layers):
            out[z, part] = total[z * share : (z + 1) * share]


def body(mesh_shape, crystal, probe, amplitude, shear, scan_x, scan_y, slot_angle, owner_slot, counts):
    strips, angles, depths = (mesh_shape[n] for n in ("strip", "angle", "depth"))
    slots = owner_slot.shape[2]
    quarter = strips // 4
    lanes = slots // quarter
    layers, _, wx, ny = crystal.shape
    frame = probe.shape[-1]
    share = wx // angles
    window = share + MAX_SHEAR
    half = amplitude.shape[1]
    axes = ("strip", "angle", "depth")
    params = pltpu.CompilerParams(vmem_limit_bytes=VMEM_BYTES)
    smem = pl.BlockSpec(memory_space=pltpu.SMEM)
    vmem = pl.BlockSpec(memory_space=pltpu.VMEM)

    def swap(x):
        return lax.ppermute(x, "depth", [(d, (d + 1) % depths) for d in range(depths)])

    def permute(x, move):
        pairs = []
        for s in range(strips):
            for a in range(angles):
                for d in range(depths):
                    to = move(s, a, d)
                    if to is not None:
                        pairs.append(
                            (
                                (s * angles + a) * depths + d,
                                (to[0] * angles + to[1]) * depths + to[2],
                            )
                        )
        return lax.ppermute(x, axes, pairs)

    def ring(x, turn, lap):
        def move(s, a, d):
            a = (a + lap) % angles
            way = turn if d == 0 else -turn
            if 0 <= s + way < strips:
                return s + way, a, d
            return s, a, 1 - d

        return permute(x, move)

    def far(x, way, lap, hops, forward):
        def move(s, a, d):
            reach = 2 * d if way else 1
            home = s - reach if forward else (s - 1 - 4 * hops) % strips
            if not 0 <= home <= strips - 3:
                return None
            to = (home + 1 + 4 * hops) % strips if forward else home + reach
            return to, (a + lap) % angles, d

        return permute(x, move)

    amplitude_far = swap(amplitude)
    ints = (shear, scan_x, scan_y, slot_angle, owner_slot)
    halves = jax.ShapeDtypeStruct((slots, 2, half, frame), BF)
    sent = pl.pallas_call(
        functools.partial(project_kernel, strips, slots, False),
        out_shape=jax.ShapeDtypeStruct((2, slots, 2, half, frame), BF),
        in_specs=[smem] * 5 + [vmem],
        out_specs=vmem,
        compiler_params=params,
        name="project_far",
    )(*ints, crystal)
    arrived = swap(sent)
    entries = shear.shape[0] * layers + 3 * strips * slots
    moving, middle, table = pl.pallas_call(
        functools.partial(project_kernel, strips, slots, True),
        out_shape=[halves, halves, jax.ShapeDtypeStruct((entries,), jnp.int32)],
        in_specs=[smem] * 5 + [vmem] * 2,
        out_specs=[vmem, vmem, smem],
        compiler_params=params,
        name="project_near",
    )(*ints, crystal, arrived)
    tables = [table] + [
        lax.ppermute(table, "angle", [(a, (a + t) % angles) for a in range(angles)])
        for t in range(1, angles)
    ]

    def by_hops(x, near, beyond):
        if quarter == 1:
            return near(x)
        pieces = []
        for hops in range(quarter):
            piece = x[hops::quarter]
            pieces.append(near(piece) if hops == 0 else beyond(piece, hops))
        return jnp.stack(pieces, axis=1).reshape(x.shape)

    moved = by_hops(moving, lambda x: ring(x, 1, 0), lambda x, n: far(x, 1, 0, n, True))
    middle = by_hops(middle, lambda x: x, lambda x, n: far(x, 0, 0, n, True))
    middle_far = swap(middle)
    moved_far = swap(moved)
    cuts = pl.pallas_call(
        functools.partial(transform_kernel, strips, angles, slots, window),
        out_shape=[jax.ShapeDtypeStruct((slots, 2, window, frame), BF)] * (2 * angles),
        in_specs=[smem] * 3 + [vmem] * 8,
        out_specs=[vmem] * (2 * angles),
        scratch_shapes=[
            pltpu.VMEM((slots, frame, 2 * frame), BF),
            pltpu.VMEM((slots, frame, frame), BF),
        ],
        compiler_params=params,
        name="transform",
    )(
        scan_x, owner_slot, counts, moved, moved_far, middle, middle_far,
        amplitude, amplitude_far, probe, jnp.asarray(dft_table(frame)),
    )
    blocks = []
    for lap in range(angles):
        outer = by_hops(
            cuts[2 * lap],
            lambda x: ring(x, -1, lap),
            lambda x, n: far(x, 1, lap, n, False),
        )
        inner = by_hops(
            cuts[2 * lap + 1],
            lambda x: x
            if lap == 0
            else lax.ppermute(x, "angle", [(a, (a + lap) % angles) for a in range(angles)]),
            lambda x, n: far(x, 0, lap, n, False),
        )
        blocks += [outer, swap(outer), inner]
    scale = 1.0 / (shear.shape[0] * angles)
    return pl.pallas_call(
        functools.partial(deposit_kernel, strips, angles, slots, scale),
        out_shape=jax.ShapeDtypeStruct((layers, 2, share, ny), F32),
        in_specs=[smem] * angles + [vmem] * (3 * angles),
        out_specs=vmem,
        compiler_params=params,
        name="deposit",
    )(*tables, *blocks)


def solution(mesh):
    placed = (
        P(("groups", "depth"), None, "strip", None),
        P(),
        P("angle", ("groups", "strip", "depth"), None),
        P(("groups", "angle"), "depth"),
        P(("groups", "angle"), None, None),
        P(("groups", "angle"), None, None),
        P(("groups", "angle"), None, None),
        P(("groups", "angle"), None, None),
        P(("groups", "angle"), None),
    )
    return jax.shard_map(
        functools.partial(body, dict(mesh.shape)),
        mesh=mesh,
        in_specs=placed,
        out_specs=P(("groups", "depth"), None, ("strip", "angle"), None),
        check_vma=False,
    )
```

time: 375 us -> 39.5 us (0.11)
  the two profiles are of different devices: /device:TPU:17 before, /device:TPU:0 now
where the time goes in v1:
time: 39.5 us; the launch traced here: 39.2 us
  waiting for transfers between devices  13.7 us (35%)
  Pallas kernels  11.2 us (28%)
  starting transfers between devices  10.3 us (26%)
  local copies, waits for them, and re-layouts  3.98 us (10%)
    ppermute x3, waiting for transfers between devices, permute(): return lax.ppermute(x, axes, pairs)  9.38 us
    ppermute x3, starting transfers between devices, permute(): return lax.ppermute(x, axes, pairs)  6.44 us
    unnamed x22, local copies, waits for them, and re-layouts  3.98 us
    pallas_call x1, Pallas kernels, body(): pl.pallas_call(functools.partial(transform_kernel, strips, angles, slots,...  3.61 us
    pallas_call x1, Pallas kernels, body(): pl.pallas_call(functools.partial(deposit_kernel, strips, angles, slots, s...  2.9 us
    ppermute x6, waiting for transfers between devices, swap(): lax.ppermute(x, 'depth', [(d, (d + 1) % depths) for d in range(depths)])  2.76 us
    pallas_call x1, Pallas kernels, body(): pl.pallas_call(functools.partial(project_kernel, strips, slots, True), ou...  2.51 us
    ppermute x1, starting transfers between devices, body(): lax.ppermute(table, 'angle', [(a, (a + t) % angles) for a in range(angles)])  2.3 us
  transfers between devices with their start and end apart: 11, of which 6 were waited for; matrix products, arithmetic and copies ran while one was open for 0% of the time, Pallas kernels for 0%

profile of v1, /device:TPU:0, one launch (start us, length us, event | category | flops | bytes accessed | tf_op | source)
XLA Modules:
  0.0 39.2 jit_solution(8610659425956030707)
XLA Ops:
  0.0 0.0 copy-start.6
  0.0 0.8 %copy.15.refs_1_.refs_0_ = s32[1,4,2]{2,1,0:T(4,128)S(1)} copy(s32[1,4,2]{1,2,0:T(2,128)} %param.14) | data formatting | bytes 64 | tf_op args[4]
  0.8 0.0 copy-done.6
  0.8 0.0 copy-start.7
  0.8 0.1 copy.18.refs_4_.refs_1_
  0.9 0.6 %copy-done.7 = s32[1,4,2]{1,2,0:T(2,128)S(1)} copy-done((s32[1,4,2]{1,2,0:T(2,128)S(1)}, s32[1,4,2]{1,2,0:T(2,128)}, u32[]{:S(2)}) %copy-start.7) | copy-done | bytes 56
  1.5 0.0 copy-start.8
  1.5 0.1 copy.16.refs_2_
  1.6 0.6 %copy-done.8 = s32[1,4,2]{1,2,0:T(2,128)S(1)} copy-done((s32[1,4,2]{1,2,0:T(2,128)S(1)}, s32[1,4,2]{1,2,0:T(2,128)}, u32[]{:S(2)}) %copy-start.8) | copy-done | bytes 56
  2.1 0.0 copy-start.4
  2.1 0.1 copy.17.refs_3_
  2.2 0.6 %copy-done.4 = s32[4,4]{1,0:T(4,128)S(1)} copy-done((s32[4,4]{1,0:T(4,128)S(1)}, s32[4,4]{1,0:T(4,128)}, u32[]{:S(2)}) %copy-start.4) | copy-done | bytes 88
  2.8 0.0 copy-start
  2.8 1.1 %copy-done = bf16[4,2,128,384]{3,2,1,0:T(8,128)(2,1)S(1)} copy-done((bf16[4,2,128,384]{3,2,1,0:T(8,128)(2,1)S(1)}, bf16[4,2,128,384]{3,2,1,0:T(8,128)(2,1)}, u32[]{:S(2)}) %copy-start) | copy-done | bytes 786456
  4.0 2.2 %project_far.1 = bf16[2,2,2,128,256]{4,3,2,1,0:T(8,128)(2,1)S(1)} custom-call(s32[4,4]{1,0:T(4,128)S(1)} %copy-done.4, s32[1,4,2]{2,1,0:T(4,128)S(1)} %copy.15.refs_1_.refs_0_, s32[1,4,2]{2,1,0:T(4,128)S(1)} %copy.16.refs_2_, s32[1,4,2]{2,1,0:T(4,128)S(1)} %copy.17.refs_3_, s32[1,4,2]{2,1,0:T(4,128)S(1)} %copy.18.refs_4_.refs_1_, ...), custom_call_target="tpu_custom_call" | custom-call | tf_op jit(solution)/shard_map/project_far/pallas_call | solution.py:271
  6.2 0.0 copy-start.3
  6.2 0.0 copy-start.1
  6.2 0.0 copy-start.2
  6.2 0.5 %collective-permute-start = (bf16[2,2,2,128,256]{4,3,2,1,0:T(8,128)(2,1)S(1)}, bf16[2,2,2,128,256]{4,3,2,1,0:T(8,128)(2,1)S(1)}, u32[]{:S(2)}, u32[]{:S(2)}) collective-permute-start(bf16[2,2,2,128,256]{4,3,2,1,0:T(8,128)(2,1)S(1)} %project_far.1), channel_id=1, source_target_pairs={{0,1},{1,0},{2,3},{3,2},{4,5},{5,4},{6,7},{7,6},{8,9},{9,8},{10,11... | collective-permute-start | bytes 1572872 | tf_op jit(solution)/shard_map/ppermute | solution.py:230
  6.7 1.5 %collective-permute-done.refs_6_ = bf16[2,2,2,128,256]{4,3,2,1,0:T(8,128)(2,1)S(1)} collective-permute-done((bf16[2,2,2,128,256]{4,3,2,1,0:T(8,128)(2,1)S(1)}, bf16[2,2,2,128,256]{4,3,2,1,0:T(8,128)(2,1)S(1)}, u32[]{:S(2)}, u32[]{:S(2)}) %collective-permute-start) | collective-permute-done | bytes 524320 | tf_op jit(solution)/shard_map/ppermute | solution.py:230
  8.2 2.5 %project_near.1 = (bf16[2,2,128,256]{3,2,1,0:T(8,128)(2,1)S(1)}, bf16[2,2,128,256]{3,2,1,0:T(8,128)(2,1)S(1)}, s32[40]{0:T(128)S(1)}) custom-call(s32[4,4]{1,0:T(4,128)S(1)} %copy-done.4, s32[1,4,2]{2,1,0:T(4,128)S(1)} %copy.15.refs_1_.refs_0_, s32[1,4,2]{2,1,0:T(4,128)S(1)} %copy.16.refs_2_, s32[1,4,2]{2,1,0:T(4,128)S(1)} %copy.17.refs_3_, ...), custom_call_target="tpu_custom_call" | custom-call | tf_op jit(solution)/shard_map/project_near/pallas_call | solution.py:281
  10.8 0.0 copy-start.5
  10.8 3.0 %collective-permute-start.2 = (bf16[2,2,128,256]{3,2,1,0:T(8,128)(2,1)S(1)}, bf16[2,2,128,256]{3,2,1,0:T(8,128)(2,1)S(1)}, u32[]{:S(2)}, u32[]{:S(2)}) collective-permute-start(bf16[2,2,128,256]{3,2,1,0:T(8,128)(2,1)S(1)} %get-tuple-element.13), channel_id=1, source_target_pairs={{0,4},{1,0},{2,6},{3,2},{4,8},{5,1},{6,10},{7,3},{8,12},{9,5},{10,... | collective-permute-start | bytes 786440 | tf_op jit(solution)/shard_map/ppermute | solution.py:245
  13.7 0.0 collective-permute-start.4
  13.7 3.9 %collective-permute-done.2.refs_3_ = bf16[2,2,128,256]{3,2,1,0:T(8,128)(2,1)S(1)} collective-permute-done((bf16[2,2,128,256]{3,2,1,0:T(8,128)(2,1)S(1)}, bf16[2,2,128,256]{3,2,1,0:T(8,128)(2,1)S(1)}, u32[]{:S(2)}, u32[]{:S(2)}) %collective-permute-start.2) | collective-permute-done | bytes 262176 | tf_op jit(solution)/shard_map/ppermute | solution.py:245
  17.6 0.0 collective-permute-start.3
  17.6 0.0 copy-done.3
  17.6 0.5 %collective-permute-start.5 = (bf16[2,128,256]{2,1,0:T(8,128)(2,1)S(1)}, bf16[2,128,256]{2,1,0:T(8,128)(2,1)S(1)}, u32[]{:S(2)}, u32[]{:S(2)}) collective-permute-start(bf16[2,128,256]{2,1,0:T(8,128)(2,1)S(1)} %copy-done.3), channel_id=1, source_target_pairs={{0,1},{1,0},{2,3},{3,2},{4,5},{5,4},{6,7},{7,6},{8,9},{9,8},{10,11... | collective-permute-start | bytes 393224 | tf_op jit(solution)/shard_map/ppermute | solution.py:230
  18.1 1.2 %collective-permute-done.5.refs_8_ = bf16[2,128,256]{2,1,0:T(8,128)(2,1)S(1)} collective-permute-done((bf16[2,128,256]{2,1,0:T(8,128)(2,1)S(1)}, bf16[2,128,256]{2,1,0:T(8,128)(2,1)S(1)}, u32[]{:S(2)}, u32[]{:S(2)}) %collective-permute-start.5) | collective-permute-done | bytes 131104 | tf_op jit(solution)/shard_map/ppermute | solution.py:230
  19.3 0.0 collective-permute-done.4.refs_6_
  19.4 0.0 collective-permute-done.3.refs_4_
  19.4 0.0 copy-done.1
  19.4 0.0 copy-done.2
  19.4 0.0 copy-done.5
  19.4 3.6 %transform.1 = (bf16[2,2,80,256]{3,2,1,0:T(8,128)(2,1)S(1)}, bf16[2,2,80,256]{3,2,1,0:T(8,128)(2,1)S(1)}, bf16[2,2,80,256]{3,2,1,0:T(8,128)(2,1)S(1)}, bf16[2,2,80,256]{3,2,1,0:T(8,128)(2,1)S(1)}) custom-call(s32[1,4,2]{2,1,0:T(4,128)S(1)} %copy.15.refs_1_.refs_0_, s32[1,4,2]{2,1,0:T(4,128)S(1)} %copy.18.refs_4_.refs_1_, s32[1,4]{1,0:T(1,128)S(1)} %copy-done.5, ...), custom_call_target="tpu_custom_call" | custom-call | tf_op jit(solution)/shard_map/transform/pallas_call | solution.py:307
  23.0 0.2 collective-permute-start.6
  23.2 3.3 %collective-permute-start.8 = (bf16[2,2,80,256]{3,2,1,0:T(8,128)(2,1)S(1)}, bf16[2,2,80,256]{3,2,1,0:T(8,128)(2,1)S(1)}, u32[]{:S(2)}, u32[]{:S(2)}) collective-permute-start(bf16[2,2,80,256]{3,2,1,0:T(8,128)(2,1)S(1)} %get-tuple-element.17), channel_id=1, source_target_pairs={{0,3},{1,7},{2,1},{3,5},{4,2},{5,11},{6,0},{7,9},{8,6},{9,15},{10,... | collective-permute-start | bytes 491528 | tf_op jit(solution)/shard_map/ppermute | solution.py:245
  26.5 0.5 %collective-permute-start.10 = (bf16[2,2,80,256]{3,2,1,0:T(8,128)(2,1)S(1)}, bf16[2,2,80,256]{3,2,1,0:T(8,128)(2,1)S(1)}, u32[]{:S(2)}, u32[]{:S(2)}) collective-permute-start(bf16[2,2,80,256]{3,2,1,0:T(8,128)(2,1)S(1)} %get-tuple-element.18), channel_id=1, source_target_pairs={{0,2},{2,0},{1,3},{3,1},{4,6},{6,4},{5,7},{7,5},{8,10},{10,8},{9,1... | collective-permute-start | bytes 491528 | tf_op jit(solution)/shard_map/ppermute | solution.py:333
  27.0 1.8 %collective-permute-done.6.refs_2_ = bf16[2,2,80,256]{3,2,1,0:T(8,128)(2,1)S(1)} collective-permute-done((bf16[2,2,80,256]{3,2,1,0:T(8,128)(2,1)S(1)}, bf16[2,2,80,256]{3,2,1,0:T(8,128)(2,1)S(1)}, u32[]{:S(2)}, u32[]{:S(2)}) %collective-permute-start.6) | collective-permute-done | bytes 163872 | tf_op jit(solution)/shard_map/ppermute | solution.py:245
  28.8 0.0 collective-permute-start.7
  28.8 3.7 %collective-permute-done.8.refs_5_ = bf16[2,2,80,256]{3,2,1,0:T(8,128)(2,1)S(1)} collective-permute-done((bf16[2,2,80,256]{3,2,1,0:T(8,128)(2,1)S(1)}, bf16[2,2,80,256]{3,2,1,0:T(8,128)(2,1)S(1)}, u32[]{:S(2)}, u32[]{:S(2)}) %collective-permute-start.8) | collective-permute-done | bytes 163872 | tf_op jit(solution)/shard_map/ppermute | solution.py:245
  32.5 0.0 collective-permute-start.9
  32.5 2.3 %collective-permute-start.1 = (s32[40]{0:T(128)S(1)}, s32[40]{0:T(128)S(1)}, u32[]{:S(2)}, u32[]{:S(2)}) collective-permute-start(s32[40]{0:T(128)S(1)} %get-tuple-element.12.refs_0_), channel_id=1, source_target_pairs={{0,2},{2,0},{1,3},{3,1},{4,6},{6,4},{5,7},{7,5},{8,10},{10,8},{9,1... | collective-permute-start | bytes 488 | tf_op jit(solution)/shard_map/ppermute | solution.py:290
  34.8 1.5 %collective-permute-done.1.refs_1_ = s32[40]{0:T(128)S(1)} collective-permute-done((s32[40]{0:T(128)S(1)}, s32[40]{0:T(128)S(1)}, u32[]{:S(2)}, u32[]{:S(2)}) %collective-permute-start.1) | collective-permute-done | bytes 192 | tf_op jit(solution)/shard_map/ppermute | solution.py:290
  36.3 0.0 collective-permute-done.10.refs_7_
  36.3 0.0 collective-permute-done.7.refs_3_
  36.3 0.0 collective-permute-done.9.refs_6_
  36.3 2.9 %deposit.1 = f32[4,2,64,384]{3,2,1,0:T(8,128)} custom-call(s32[40]{0:T(128)S(1)} %get-tuple-element.12.refs_0_, s32[40]{0:T(128)S(1)} %collective-permute-done.1.refs_1_, bf16[2,2,80,256]{3,2,1,0:T(8,128)(2,1)S(1)} %collective-permute-done.6.refs_2_, bf16[2,2,80,256]{3,2,1,0:T(8,128)(2,1)S(1)} %collective-permute-done.7.refs_3_, ...), custom_call_target="tpu_custom_call" | custom-call | tf_op jit(solution)/shard_map/deposit/pallas_call | solution.py:338
Async XLA Ops:
  0.0 0.8 %copy-start.6 = (s32[1,4,2]{1,2,0:T(2,128)S(1)}, s32[1,4,2]{1,2,0:T(2,128)}, u32[]{:S(2)}) copy-start(s32[1,4,2]{1,2,0:T(2,128)} %param.17) | copy-start | bytes 100
  0.8 0.7 %copy-start.7 = (s32[1,4,2]{1,2,0:T(2,128)S(1)}, s32[1,4,2]{1,2,0:T(2,128)}, u32[]{:S(2)}) copy-start(s32[1,4,2]{1,2,0:T(2,128)} %param.15) | copy-start | bytes 100
  1.5 0.7 %copy-start.8 = (s32[1,4,2]{1,2,0:T(2,128)S(1)}, s32[1,4,2]{1,2,0:T(2,128)}, u32[]{:S(2)}) copy-start(s32[1,4,2]{1,2,0:T(2,128)} %param.16) | copy-start | bytes 100
  2.1 0.7 %copy-start.4 = (s32[4,4]{1,0:T(4,128)S(1)}, s32[4,4]{1,0:T(4,128)}, u32[]{:S(2)}) copy-start(s32[4,4]{1,0:T(4,128)} %refs_0_.4) | copy-start | bytes 196
  2.8 1.1 %copy-start = (bf16[4,2,128,384]{3,2,1,0:T(8,128)(2,1)S(1)}, bf16[4,2,128,384]{3,2,1,0:T(8,128)(2,1)}, u32[]{:S(2)}) copy-start(bf16[4,2,128,384]{3,2,1,0:T(8,128)(2,1)} %refs_5_.3) | copy-start | bytes 2359300
  6.2 11.5 %copy-start.3 = (bf16[2,128,256]{2,1,0:T(8,128)(2,1)S(1)}, bf16[2,128,256]{2,1,0:T(8,128)(2,1)}, u32[]{:S(2)}) copy-start(bf16[2,128,256]{2,1,0:T(8,128)(2,1)} %refs_7_.1) | copy-start | bytes 393220
  6.2 13.2 %copy-start.1 = (bf16[2,256,256]{2,1,0:T(8,128)(2,1)S(1)}, bf16[2,256,256]{2,1,0:T(8,128)(2,1)}, u32[]{:S(2)}) copy-start(bf16[2,256,256]{2,1,0:T(8,128)(2,1)} %refs_9_.1) | copy-start | bytes 786436
  6.2 13.2 %copy-start.2 = (bf16[2,256,256]{2,1,0:T(8,128)(2,1)S(1)}, bf16[2,256,256]{2,1,0:T(8,128)(2,1)}, u32[]{:S(2)}) copy-start(bf16[2,256,256]{2,1,0:T(8,128)(2,1)} %constant.2.clone.refs_10_) | copy-start | bytes 786436
  6.2 2.0 %collective-permute-start = (bf16[2,2,2,128,256]{4,3,2,1,0:T(8,128)(2,1)S(1)}, bf16[2,2,2,128,256]{4,3,2,1,0:T(8,128)(2,1)S(1)}, u32[]{:S(2)}, u32[]{:S(2)}) collective-permute-start(bf16[2,2,2,128,256]{4,3,2,1,0:T(8,128)(2,1)S(1)} %project_far.1), channel_id=1, source_target_pairs={{0,1},{1,0},{2,3},{3,2},{4,5},{5,4},{6,7},{7,6},{8,9},{9,8},{10,11... | collective-permute-start | bytes 1572872 | tf_op jit(solution)/shard_map/ppermute | solution.py:230
  10.8 8.6 %copy-start.5 = (s32[1,4]{1,0:T(1,128)S(1)}, s32[1,4]{1,0:T(1,128)}, u32[]{:S(2)}) copy-start(s32[1,4]{1,0:T(1,128)} %refs_2_.3) | copy-start | bytes 52
  10.8 6.9 %collective-permute-start.2 = (bf16[2,2,128,256]{3,2,1,0:T(8,128)(2,1)S(1)}, bf16[2,2,128,256]{3,2,1,0:T(8,128)(2,1)S(1)}, u32[]{:S(2)}, u32[]{:S(2)}) collective-permute-start(bf16[2,2,128,256]{3,2,1,0:T(8,128)(2,1)S(1)} %get-tuple-element.13), channel_id=1, source_target_pairs={{0,4},{1,0},{2,6},{3,2},{4,8},{5,1},{6,10},{7,3},{8,12},{9,5},{10,... | collective-permute-start | bytes 786440 | tf_op jit(solution)/shard_map/ppermute | solution.py:245
  13.7 5.6 %collective-permute-start.4 = (bf16[2,2,128,256]{3,2,1,0:T(8,128)(2,1)S(1)}, bf16[2,2,128,256]{3,2,1,0:T(8,128)(2,1)S(1)}, u32[]{:S(2)}, u32[]{:S(2)}) collective-permute-start(bf16[2,2,128,256]{3,2,1,0:T(8,128)(2,1)S(1)} %get-tuple-element.14.refs_5_), channel_id=1, source_target_pairs={{0,1},{1,0},{2,3},{3,2},{4,5},{5,4},{6,7},{7,6},{8,9},{9,8},{10,11... | collective-permute-start | bytes 786440 | tf_op jit(solution)/shard_map/ppermute | solution.py:230
  17.6 1.7 %collective-permute-start.3 = (bf16[2,2,128,256]{3,2,1,0:T(8,128)(2,1)S(1)}, bf16[2,2,128,256]{3,2,1,0:T(8,128)(2,1)S(1)}, u32[]{:S(2)}, u32[]{:S(2)}) collective-permute-start(bf16[2,2,128,256]{3,2,1,0:T(8,128)(2,1)S(1)} %collective-permute-done.2.refs_3_), channel_id=1, source_target_pairs={{0,1},{1,0},{2,3},{3,2},{4,5},{5,4},{6,7},{7,6},{8,9},{9,8},{10,11... | collective-permute-start | bytes 786440 | tf_op jit(solution)/shard_map/ppermute | solution.py:230
  17.6 1.7 %collective-permute-start.5 = (bf16[2,128,256]{2,1,0:T(8,128)(2,1)S(1)}, bf16[2,128,256]{2,1,0:T(8,128)(2,1)S(1)}, u32[]{:S(2)}, u32[]{:S(2)}) collective-permute-start(bf16[2,128,256]{2,1,0:T(8,128)(2,1)S(1)} %copy-done.3), channel_id=1, source_target_pairs={{0,1},{1,0},{2,3},{3,2},{4,5},{5,4},{6,7},{7,6},{8,9},{9,8},{10,11... | collective-permute-start | bytes 393224 | tf_op jit(solution)/shard_map/ppermute | solution.py:230
  23.0 5.8 %collective-permute-start.6 = (bf16[2,2,80,256]{3,2,1,0:T(8,128)(2,1)S(1)}, bf16[2,2,80,256]{3,2,1,0:T(8,128)(2,1)S(1)}, u32[]{:S(2)}, u32[]{:S(2)}) collective-permute-start(bf16[2,2,80,256]{3,2,1,0:T(8,128)(2,1)S(1)} %get-tuple-element.15), channel_id=1, source_target_pairs={{0,1},{1,5},{2,3},{3,7},{4,0},{5,9},{6,2},{7,11},{8,4},{9,13},{10,... | collective-permute-start | bytes 491528 | tf_op jit(solution)/shard_map/ppermute | solution.py:245
  23.2 9.3 %collective-permute-start.8 = (bf16[2,2,80,256]{3,2,1,0:T(8,128)(2,1)S(1)}, bf16[2,2,80,256]{3,2,1,0:T(8,128)(2,1)S(1)}, u32[]{:S(2)}, u32[]{:S(2)}) collective-permute-start(bf16[2,2,80,256]{3,2,1,0:T(8,128)(2,1)S(1)} %get-tuple-element.17), channel_id=1, source_target_pairs={{0,3},{1,7},{2,1},{3,5},{4,2},{5,11},{6,0},{7,9},{8,6},{9,15},{10,... | collective-permute-start | bytes 491528 | tf_op jit(solution)/shard_map/ppermute | solution.py:245
  26.5 9.9 %collective-permute-start.10 = (bf16[2,2,80,256]{3,2,1,0:T(8,128)(2,1)S(1)}, bf16[2,2,80,256]{3,2,1,0:T(8,128)(2,1)S(1)}, u32[]{:S(2)}, u32[]{:S(2)}) collective-permute-start(bf16[2,2,80,256]{3,2,1,0:T(8,128)(2,1)S(1)} %get-tuple-element.18), channel_id=1, source_target_pairs={{0,2},{2,0},{1,3},{3,1},{4,6},{6,4},{5,7},{7,5},{8,10},{10,8},{9,1... | collective-permute-start | bytes 491528 | tf_op jit(solution)/shard_map/ppermute | solution.py:333
  28.8 7.5 %collective-permute-start.7 = (bf16[2,2,80,256]{3,2,1,0:T(8,128)(2,1)S(1)}, bf16[2,2,80,256]{3,2,1,0:T(8,128)(2,1)S(1)}, u32[]{:S(2)}, u32[]{:S(2)}) collective-permute-start(bf16[2,2,80,256]{3,2,1,0:T(8,128)(2,1)S(1)} %collective-permute-done.6.refs_2_), channel_id=1, source_target_pairs={{0,1},{1,0},{2,3},{3,2},{4,5},{5,4},{6,7},{7,6},{8,9},{9,8},{10,11... | collective-permute-start | bytes 491528 | tf_op jit(solution)/shard_map/ppermute | solution.py:230
  32.5 3.8 %collective-permute-start.9 = (bf16[2,2,80,256]{3,2,1,0:T(8,128)(2,1)S(1)}, bf16[2,2,80,256]{3,2,1,0:T(8,128)(2,1)S(1)}, u32[]{:S(2)}, u32[]{:S(2)}) collective-permute-start(bf16[2,2,80,256]{3,2,1,0:T(8,128)(2,1)S(1)} %collective-permute-done.8.refs_5_), channel_id=1, source_target_pairs={{0,1},{1,0},{2,3},{3,2},{4,5},{5,4},{6,7},{7,6},{8,9},{9,8},{10,11... | collective-permute-start | bytes 491528 | tf_op jit(solution)/shard_map/ppermute | solution.py:230
  32.5 3.8 %collective-permute-start.1 = (s32[40]{0:T(128)S(1)}, s32[40]{0:T(128)S(1)}, u32[]{:S(2)}, u32[]{:S(2)}) collective-permute-start(s32[40]{0:T(128)S(1)} %get-tuple-element.12.refs_0_), channel_id=1, source_target_pairs={{0,2},{2,0},{1,3},{3,1},{4,6},{6,4},{5,7},{7,5},{8,10},{10,8},{9,1... | collective-permute-start | bytes 488 | tf_op jit(solution)/shard_map/ppermute | solution.py:290

commit v2 on v1

v2 whole, which is shorter than its diff:
```python
import functools
import math

import jax
import jax.numpy as jnp
import ml_dtypes
import numpy as np
from jax import lax
from jax.experimental import pallas as pl
from jax.experimental.pallas import tpu as pltpu
from jax.sharding import PartitionSpec as P

BF = jnp.bfloat16
F32 = jnp.float32
VMEM_BYTES = 48 * 2**20
MAX_SHEAR = 16


def dft_table(n):
    index = np.arange(n, dtype=np.int64)
    phase = (index[:, None] * index[None, :] % n).astype(np.float64) * (2.0 * math.pi / n)
    scale = 1.0 / math.sqrt(n)
    table = np.stack([np.cos(phase) * scale, -np.sin(phase) * scale])
    return table.astype(np.float32).astype(ml_dtypes.bfloat16)


def dot(left, right):
    return jnp.dot(left, right, preferred_element_type=F32)


def band_matrix(rows, cols, offset):
    gap = lax.broadcasted_iota(jnp.int32, (rows, cols), 1) - lax.broadcasted_iota(
        jnp.int32, (rows, cols), 0
    )
    return jnp.where(gap == offset, 1.0, 0.0).astype(BF)


def clip(value, top):
    return jnp.minimum(jnp.maximum(value, 0), top)


class Table:
    def __init__(self, ref, strips, slots, layers):
        self.ref, self.slots, self.layers = ref, slots, layers
        self.count = strips * slots
        self.base = ref.shape[0] - 4 * self.count - strips

    def pick(self, which, home, slot):
        return self.ref[self.base + which * self.count + home * self.slots + slot]

    def column(self, home, slot):
        return self.pick(0, home, slot)

    def shears(self, home, slot):
        angle = self.pick(1, home, slot)
        return [self.ref[angle * self.layers + z] for z in range(self.layers)]

    def slot(self, home, quota):
        found = jnp.int32(0)
        for slot in range(self.slots):
            found = jnp.where(self.pick(2, home, slot) == quota, slot, found)
        return found

    def offset(self, home, slot):
        return self.pick(3, home, slot)

    def alive(self, home, slot):
        return slot < self.ref[self.base + 4 * self.count + home]


def fill_table(table, shear, by_slot, counts):
    place = 0
    for i in range(shear.shape[0]):
        for z in range(shear.shape[1]):
            table[place] = shear[i, z]
            place += 1
    _, slots, strips = by_slot[0].shape
    for ref in by_slot:
        for home in range(strips):
            for slot in range(slots):
                table[place] = ref[0, slot, home]
                place += 1
    for home in range(strips):
        table[place] = counts[0, home]
        place += 1


def project_kernel(strips, slots, mine, *refs):
    strip = lax.axis_index("strip")
    depth = lax.axis_index("depth")
    half = depth if mine else 1 - depth
    if mine:
        table, crystal, *parts = refs
    else:
        shear, scan_x, scan_y, slot_angle, owner, counts, crystal, *parts, table = refs
        fill_table(table, shear, (scan_y, slot_angle, owner, scan_x), counts)
    layers, _, wx, ny = crystal.shape
    ints = Table(table, strips, slots, layers)
    frame = parts[0].shape[-1]
    rows = []
    columns = []
    for kind, out in enumerate(parts):
        home = clip(strip - (2 * half if kind == 0 else 1), strips - 1)
        back = wx * half if kind == 0 else wx
        for quota in range(slots):
            slot = ints.slot(home, quota)
            start = ints.offset(home, slot) - back
            rows.append(
                jnp.concatenate(
                    [
                        band_matrix(out.shape[2], wx, start + shear)
                        for shear in ints.shears(home, slot)
                    ],
                    axis=1,
                )
            )
            columns.append(band_matrix(ny, frame, -ints.column(home, slot)))
    rows = jnp.concatenate(rows, axis=0)
    lifted = [
        dot(rows, jnp.concatenate([crystal[z, part] for z in range(layers)], axis=0)).astype(BF)
        for part in range(2)
    ]
    place = 0
    for kind, out in enumerate(parts):
        tall = out.shape[2]
        for quota in range(slots):
            both = jnp.concatenate([x[place : place + tall] for x in lifted], axis=0)
            band = dot(both, columns[kind * slots + quota]).astype(out.dtype)
            out[quota, 0] = band[:tall]
            out[quota, 1] = band[tall:]
            place += tall


def add_kernel(near, far, out):
    out[...] = (near[...] + far[...].astype(F32)).astype(out.dtype)


def transform_kernel(strips, angles, slots, layers, window, *refs):
    table, moved, moved_far, middle, middle_far, near, far, probe, tab = refs[:9]
    ints = Table(table, strips, slots, layers)
    outs = refs[9 : 9 + 2 * angles]
    waves, levels = refs[9 + 2 * angles :]
    quarter = strips // 4
    strip = lax.axis_index("strip")
    plane = lax.axis_index("angle")
    depth = lax.axis_index("depth")
    half = moved.shape[2]
    frame = moved.shape[3]
    f_re = tab[0]
    f_im = tab[1]
    n_im = -f_im
    homes = []
    places = []
    for quota in range(slots):
        home = lax.rem(strip + (strips - 1) + 4 * (strips - quota % quarter), strips)
        homes.append(home)
        places.append(ints.slot(home, quota))
        for side, (a_ref, level) in enumerate(((moved, near), (moved_far, far))):
            row = pl.multiple_of((depth if side == 0 else 1 - depth) * half, half)
            here = pl.ds(row, half)
            w_re, w_im = (
                a_ref[quota, part].astype(F32)
                + middle[quota, part, here].astype(F32)
                + middle_far[quota, part, here].astype(F32)
                for part in range(2)
            )
            p_re = probe[0, here].astype(F32)
            p_im = probe[1, here].astype(F32)
            to = pl.ds(row + quota * frame, half)
            waves[to, :frame] = (p_re * w_re - p_im * w_im).astype(BF)
            waves[to, frame:] = (p_re * w_im + p_im * w_re).astype(BF)
            levels[quota, here] = level[quota]

    def side_by_side(x, dtype=BF):
        return jnp.concatenate(
            [
                jnp.concatenate(
                    [
                        x[q * frame : (q + 1) * frame, p * frame : (p + 1) * frame]
                        for q in range(slots)
                    ],
                    axis=1,
                )
                for p in range(2)
            ],
            axis=0,
        ).astype(dtype)

    def blocks(re, im, low):
        return jnp.concatenate(
            [jnp.concatenate([re, im], axis=1), jnp.concatenate([low, re], axis=1)], axis=0
        )

    ahead = blocks(f_re, f_im, n_im)
    behind = blocks(f_re, n_im, f_im)
    section = side_by_side(dot(waves[...], ahead))
    spectrum = dot(behind, section)
    p_re = probe[0].astype(F32)
    p_im = probe[1].astype(F32)
    residuals = []
    for quota in range(slots):
        alive = jnp.logical_and(
            homes[quota] <= strips - 3, ints.alive(homes[quota], places[quota])
        )
        alive = jnp.where(alive, 1.0, 0.0).astype(F32)
        s_re = spectrum[:frame, quota * frame : (quota + 1) * frame]
        s_im = spectrum[frame:, quota * frame : (quota + 1) * frame]
        magnitude = jnp.maximum(jnp.sqrt(s_re * s_re + s_im * s_im), 1.0)
        factor = (1.0 - levels[quota].astype(F32) / magnitude) * alive
        residuals.append(jnp.concatenate([s_re * factor, s_im * factor], axis=1).astype(BF))
    inverse = side_by_side(dot(jnp.concatenate(residuals, axis=0), behind))
    wave = dot(ahead, inverse)
    share = window - MAX_SHEAR
    for quota in range(slots):
        b_re = wave[:frame, quota * frame : (quota + 1) * frame]
        b_im = wave[frame:, quota * frame : (quota + 1) * frame]
        back = jnp.concatenate(
            [p_re * b_re + p_im * b_im, p_re * b_im - p_im * b_re], axis=1
        ).astype(BF)
        offset = ints.offset(homes[quota], places[quota])
        picks = []
        for shift in range(angles):
            target = lax.rem(plane + shift, angles)
            for kind in range(2):
                reach = 2 * depth if kind == 0 else 1
                first = reach * (share * angles) + share * target - offset - MAX_SHEAR
                picks.append(band_matrix(window, frame, first))
        cut = dot(jnp.concatenate(picks, axis=0), back).astype(BF)
        for place, out in enumerate(outs):
            rows = cut[place * window : (place + 1) * window]
            held = out.shape[0]
            if held == slots:
                out[quota, 0] = rows[:, :frame]
                out[quota, 1] = rows[:, frame:]
                continue

            @pl.when(depth == quota // held)
            def _():
                out[quota % held, 0] = rows[:, :frame]
                out[quota % held, 1] = rows[:, frame:]


def deposit_kernel(strips, slots, items, before, last, scale, *refs):
    laps = sorted({lap for lap, _ in items})
    tables = dict(zip(laps, refs))
    refs = refs[len(laps) :]
    blocks, refs = refs[: len(items)], refs[len(items) :]
    sums = refs[0] if before else None
    out = refs[1] if before else refs[0]
    total, sems = refs[-2:] if last else (out, None)
    layers, _, share, ny = out.shape
    window, frame = blocks[0].shape[2:]
    strip = lax.axis_index("strip")
    depth = lax.axis_index("depth")
    rows = []
    values = ([], [])
    for (lap, kind), block in zip(items, blocks):
        ints = Table(tables[lap], strips, slots, layers)
        reach = (2 * depth, 2 - 2 * depth, 1, 1)[kind]
        home = clip(strip - reach, strips - 1)
        held = block.shape[0]
        for place in range(held):
            quota = place
            if held < slots:
                quota = place + held * (depth if kind == 2 else 1 - depth)
            slot = ints.slot(home, quota)
            rows.append(
                jnp.concatenate(
                    [
                        band_matrix(share, window, MAX_SHEAR - shear)
                        for shear in ints.shears(home, slot)
                    ],
                    axis=0,
                )
            )
            columns = band_matrix(frame, ny, ints.column(home, slot))
            both = jnp.concatenate([block[place, 0], block[place, 1]], axis=0)
            placed = dot(both, columns).astype(BF)
            values[0].append(placed[:window])
            values[1].append(placed[window:])
    left = jnp.concatenate(rows, axis=1)
    copies = []
    for part in range(2):
        grown = dot(left, jnp.concatenate(values[part], axis=0)) * scale
        for z in range(layers):
            piece = grown[z * share : (z + 1) * share]
            total[z, part] = piece if sums is None else piece + sums[z, part]
            if last:
                copies.append(
                    pltpu.make_async_copy(total.at[z, part], out.at[z, part], sems.at[z, part])
                )
                copies[-1].start()
    for copy in copies:
        copy.wait()


def body(mesh_shape, crystal, probe, amplitude, shear, scan_x, scan_y, slot_angle, owner_slot, counts):
    strips, angles, depths = (mesh_shape[n] for n in ("strip", "angle", "depth"))
    slots = owner_slot.shape[2]
    quarter = strips // 4
    lanes = slots // quarter
    layers, _, wx, ny = crystal.shape
    frame = probe.shape[-1]
    share = wx // angles
    window = share + MAX_SHEAR
    half = amplitude.shape[1]
    axes = ("strip", "angle", "depth")
    params = pltpu.CompilerParams(vmem_limit_bytes=VMEM_BYTES)
    smem = pl.BlockSpec(memory_space=pltpu.SMEM)
    vmem = pl.BlockSpec(memory_space=pltpu.VMEM)

    def cost(micros):
        return pl.CostEstimate(flops=int(micros * 8e8), bytes_accessed=0, transcendentals=0)

    def swap(x):
        return lax.ppermute(x, "depth", [(d, (d + 1) % depths) for d in range(depths)])

    def permute(x, move):
        pairs = []
        for s in range(strips):
            for a in range(angles):
                for d in range(depths):
                    to = move(s, a, d)
                    if to is not None:
                        pairs.append(
                            (
                                (s * angles + a) * depths + d,
                                (to[0] * angles + to[1]) * depths + to[2],
                            )
                        )
        return lax.ppermute(x, axes, pairs)

    def ring(x, turn, lap):
        def move(s, a, d):
            way = turn if d == 0 else -turn
            if 0 <= s + way < strips:
                return s + way, (a + lap) % angles, d
            return s, a, 1 - d

        return permute(x, move)

    def far(x, way, lap, hops, forward):
        def move(s, a, d):
            reach = 2 * d if way else 1
            home = s - reach if forward else (s - 1 - 4 * hops) % strips
            if not 0 <= home <= strips - 3:
                return None
            to = (home + 1 + 4 * hops) % strips if forward else home + reach
            return to, (a + lap) % angles, d

        return permute(x, move)

    amplitude_far = swap(amplitude)
    flat = [jnp.swapaxes(x, 1, 2) for x in (scan_x, scan_y, slot_angle, owner_slot)]
    ints = (shear, *flat, counts)
    entries = shear.shape[0] * layers + 4 * strips * slots + strips
    sent, table = pl.pallas_call(
        functools.partial(project_kernel, strips, slots, False),
        out_shape=[
            jax.ShapeDtypeStruct((slots, 2, half, frame), BF),
            jax.ShapeDtypeStruct((entries,), jnp.int32),
        ],
        in_specs=[smem] * 6 + [vmem],
        out_specs=[vmem, smem],
        compiler_params=params,
        cost_estimate=cost(1.5),
        name="project_far",
    )(*ints, crystal)
    arrived = swap(sent)
    tables = [table] + [
        lax.ppermute(table, "angle", [(a, (a + t) % angles) for a in range(angles)])
        for t in range(1, angles)
    ]
    moving, middle = pl.pallas_call(
        functools.partial(project_kernel, strips, slots, True),
        out_shape=[
            jax.ShapeDtypeStruct((slots, 2, half, frame), F32),
            jax.ShapeDtypeStruct((slots, 2, frame, frame), BF),
        ],
        in_specs=[smem, vmem],
        out_specs=[vmem, vmem],
        compiler_params=params,
        cost_estimate=cost(2.5),
        name="project_near",
    )(table, crystal)
    moving = pl.pallas_call(
        add_kernel,
        out_shape=jax.ShapeDtypeStruct(moving.shape, BF),
        in_specs=[vmem] * 2,
        out_specs=vmem,
        compiler_params=params,
        cost_estimate=cost(0.5),
        name="add",
    )(moving, arrived)

    def by_hops(x, near, beyond):
        if quarter == 1:
            return near(x)
        pieces = []
        for hops in range(quarter):
            piece = x[hops::quarter]
            pieces.append(near(piece) if hops == 0 else beyond(piece, hops))
        return jnp.stack(pieces, axis=1).reshape(x.shape)

    moved = by_hops(moving, lambda x: ring(x, 1, 0), lambda x, n: far(x, 1, 0, n, True))
    middle = by_hops(middle, lambda x: x, lambda x, n: far(x, 0, 0, n, True))
    middle_far = swap(middle)
    moved, tables, amplitude_far = lax.optimization_barrier((moved, tables, amplitude_far))
    moved_far = swap(moved)
    split = quarter == 1 and slots % depths == 0
    held = slots // depths if split else slots
    cuts = pl.pallas_call(
        functools.partial(transform_kernel, strips, angles, slots, layers, window),
        out_shape=[
            jax.ShapeDtypeStruct((held if i > 1 and i % 2 else slots, 2, window, frame), BF)
            for i in range(2 * angles)
        ],
        in_specs=[smem] + [vmem] * 8,
        out_specs=[vmem] * (2 * angles),
        scratch_shapes=[
            pltpu.VMEM((slots * frame, 2 * frame), BF),
            pltpu.VMEM((slots, frame, frame), BF),
        ],
        compiler_params=params,
        cost_estimate=cost(3),
        name="transform",
    )(
        table, moved, moved_far, middle, middle_far,
        amplitude, amplitude_far, probe, jnp.asarray(dft_table(frame)),
    )
    blocks = {}
    for lap in range(angles):
        blocks[lap, 0] = by_hops(
            cuts[2 * lap],
            lambda x: ring(x, -1, lap),
            lambda x, n: far(x, 1, lap, n, False),
        )
        blocks[lap, 2] = by_hops(
            cuts[2 * lap + 1],
            lambda x: x
            if lap == 0
            else lax.ppermute(x, "angle", [(a, (a + lap) % angles) for a in range(angles)]),
            lambda x, n: far(x, 0, lap, n, False),
        )
    scale = 1.0 / (shear.shape[0] * angles)

    def deposit(items, sums, last):
        laps = sorted({lap for lap, _ in items})
        sums = [] if sums is None else [sums]
        shape = (layers, 2, share, ny)
        return pl.pallas_call(
            functools.partial(deposit_kernel, strips, slots, items, bool(sums), last, scale),
            out_shape=jax.ShapeDtypeStruct(shape, F32),
            in_specs=[smem] * len(laps) + [vmem] * (len(items) + len(sums)),
            out_specs=pl.BlockSpec(memory_space=pltpu.HBM) if last else vmem,
            scratch_shapes=[pltpu.VMEM(shape, F32), pltpu.SemaphoreType.DMA((layers, 2))]
            if last
            else [],
            compiler_params=params,
            cost_estimate=cost(0.05),
            name="deposit",
        )(*(tables[lap] for lap in laps), *(blocks[item] for item in items), *sums)

    later = range(1, angles)
    keys = [(lap, 0) for lap in range(angles)] + [(lap, 2) for lap in later]
    blocks.update(zip(keys, lax.optimization_barrier([blocks[key] for key in keys])))
    shared = {0: 1, 2: 3} if split else {0: 1}
    others = [(lap, shared[kind]) for lap, kind in keys if kind in shared]
    blocks.update({(lap, shared[kind]): swap(blocks[lap, kind]) for lap, kind in keys if kind in shared})
    return deposit(others, deposit(keys + [(0, 2)], None, False), True)


def solution(mesh):
    placed = (
        P(("groups", "depth"), None, "strip", None),
        P(),
        P("angle", ("groups", "strip", "depth"), None),
        P(("groups", "angle"), "depth"),
        P(("groups", "angle"), None, None),
        P(("groups", "angle"), None, None),
        P(("groups", "angle"), None, None),
        P(("groups", "angle"), None, None),
        P(("groups", "angle"), None),
    )
    return jax.shard_map(
        functools.partial(body, dict(mesh.shape)),
        mesh=mesh,
        in_specs=placed,
        out_specs=P(("groups", "depth"), None, ("strip", "angle"), None),
        check_vma=False,
    )
```

time: 39.5 us -> 31.1 us (0.79)
  the two profiles are of different devices: /device:TPU:0 before, /device:TPU:17 now
where the time goes in v2:
time: 31.1 us; the launch traced here: 30.9 us
  waiting for transfers between devices  11 us (35%)
  Pallas kernels  9.75 us (31%)
  starting transfers between devices  8.17 us (26%)
  local copies, waits for them, and re-layouts  1.87 us (6%)
    ppermute x1, waiting for transfers between devices, body(): lax.ppermute(x, 'angle', [(a, (a + lap) % angles) for a in range(angles)])  7.14 us
    ppermute x7, starting transfers between devices, swap(): lax.ppermute(x, 'depth', [(d, (d + 1) % depths) for d in range(depths)])  3.92 us
    pallas_call x2, Pallas kernels, deposit(): pl.pallas_call(functools.partial(deposit_kernel, strips, slots, items, bo...  3.45 us
    pallas_call x1, Pallas kernels, body(): pl.pallas_call(functools.partial(transform_kernel, strips, angles, slots,...  2.9 us
    ppermute x3, starting transfers between devices, permute(): return lax.ppermute(x, axes, pairs)  2.78 us
    pallas_call x1, Pallas kernels, body(): pl.pallas_call(functools.partial(project_kernel, strips, slots, True), ou...  1.94 us
    unnamed x22, local copies, waits for them, and re-layouts  1.87 us
    ppermute x1, waiting for transfers between devices, body(): lax.ppermute(table, 'angle', [(a, (a + t) % angles) for a in range(angles)])  1.47 us
  transfers between devices with their start and end apart: 12, of which 4 were waited for; matrix products, arithmetic and copies ran while one was open for 0% of the time, Pallas kernels for 11%

profile of v2, /device:TPU:17, one launch (start us, length us, event | category | flops | bytes accessed | tf_op | source)
XLA Modules:
  0.0 30.9 jit_solution(11490200421881135134)
XLA Ops:
  0.0 0.0 copy-start.8
  0.0 0.0 copy-start.6
  0.0 0.0 copy-start.7
  0.0 0.0 copy-start.4
  0.0 0.0 copy-start.5
  0.0 0.0 copy-start.9
  0.0 0.6 %copy-done.8 = s32[1,4,2]{1,2,0:T(2,128)S(1)} copy-done((s32[1,4,2]{1,2,0:T(2,128)S(1)}, s32[1,4,2]{1,2,0:T(2,128)}, u32[]{:S(2)}) %copy-start.8) | copy-done | bytes 56
  0.7 0.0 copy-done.6
  0.7 0.0 copy-done.7
  0.7 0.0 copy-done.4
  0.7 0.0 copy-done.5
  0.7 0.0 copy-done.9
  0.7 0.0 copy-start
  0.7 1.1 %copy-done = bf16[4,2,128,384]{3,2,1,0:T(8,128)(2,1)S(1)} copy-done((bf16[4,2,128,384]{3,2,1,0:T(8,128)(2,1)S(1)}, bf16[4,2,128,384]{3,2,1,0:T(8,128)(2,1)}, u32[]{:S(2)}) %copy-start) | copy-done | bytes 786456
  1.9 0.0 copy-start.1
  1.9 1.4 %project_far.1 = (bf16[2,2,128,256]{3,2,1,0:T(8,128)(2,1)S(1)}, s32[52]{0:T(128)S(1)}) custom-call(s32[4,4]{1,0:T(4,128)S(1)} %copy-done.4, s32[1,2,4]{2,1,0:T(2,128)S(1)} %bitcast.4, s32[1,2,4]{2,1,0:T(2,128)S(1)} %bitcast.5, s32[1,2,4]{2,1,0:T(2,128)S(1)} %bitcast.6, s32[1,2,4]{2,1,0:T(2,128)S(1)} %bitcast.7, s32[1,4]{1,0:T(1,128)S(1)} %copy-done.9, ...), custom_call_target="tpu_custom_call" | custom-call | flops 1200000000 | tf_op jit(solution)/shard_map/project_far/pallas_call | solution.py:357
  3.3 0.7 %collective-permute-start = (bf16[2,2,128,256]{3,2,1,0:T(8,128)(2,1)S(1)}, bf16[2,2,128,256]{3,2,1,0:T(8,128)(2,1)S(1)}, u32[]{:S(2)}, u32[]{:S(2)}) collective-permute-start(bf16[2,2,128,256]{3,2,1,0:T(8,128)(2,1)S(1)} %get-tuple-element.22), channel_id=1, source_target_pairs={{0,1},{1,0},{2,3},{3,2},{4,5},{5,4},{6,7},{7,6},{8,9},{9,8},{10,11... | collective-permute-start | bytes 786440 | tf_op jit(solution)/shard_map/ppermute | solution.py:316
  4.0 0.0 copy-done.1
  4.0 1.9 %project_near.1 = (f32[2,2,128,256]{3,2,1,0:T(8,128)S(1)}, bf16[2,2,256,256]{3,2,1,0:T(8,128)(2,1)S(1)}) custom-call(s32[52]{0:T(128)S(1)} %get-tuple-element.23.refs_0_, bf16[4,2,128,384]{3,2,1,0:T(8,128)(2,1)S(1)} %copy-done.1), custom_call_target="tpu_custom_call" | custom-call | flops 2000000000 | tf_op jit(solution)/shard_map/project_near/pallas_call | solution.py:374
  6.0 0.0 collective-permute-done.far
  6.0 0.0 copy-start.3
  6.0 0.0 copy-start.2
  6.0 0.0 copy-start.10
  6.0 0.1 add.1
  6.1 0.2 collective-permute-start.1
  6.3 1.4 %collective-permute-start.5 = (bf16[2,2,256,256]{3,2,1,0:T(8,128)(2,1)S(1)}, bf16[2,2,256,256]{3,2,1,0:T(8,128)(2,1)S(1)}, u32[]{:S(2)}, u32[]{:S(2)}) collective-permute-start(bf16[2,2,256,256]{3,2,1,0:T(8,128)(2,1)S(1)} %get-tuple-element.26.refs_3_), channel_id=1, source_target_pairs={{0,1},{1,0},{2,3},{3,2},{4,5},{5,4},{6,7},{7,6},{8,9},{9,8},{10,11... | collective-permute-start | bytes 1572872 | tf_op jit(solution)/shard_map/ppermute | solution.py:316
  7.7 0.0 copy-done.3
  7.7 0.0 collective-permute-start.3
  7.7 1.2 %collective-permute-start.2 = (s32[52]{0:T(128)S(1)}, s32[52]{0:T(128)S(1)}, u32[]{:S(2)}, u32[]{:S(2)}) collective-permute-start(s32[52]{0:T(128)S(1)} %get-tuple-element.23.refs_0_), channel_id=1, source_target_pairs={{0,2},{2,0},{1,3},{3,1},{4,6},{6,4},{5,7},{7,5},{8,10},{10,8},{9,1... | collective-permute-start | bytes 632 | tf_op jit(solution)/shard_map/ppermute | solution.py:371
  8.9 1.5 %collective-permute-done.2.refs_1_ = s32[52]{0:T(128)S(1)} collective-permute-done((s32[52]{0:T(128)S(1)}, s32[52]{0:T(128)S(1)}, u32[]{:S(2)}, u32[]{:S(2)}) %collective-permute-start.2) | collective-permute-done | bytes 240 | tf_op jit(solution)/shard_map/ppermute | solution.py:371
  10.4 0.0 collective-permute-done.3.refs_6_
  10.4 1.2 %collective-permute-done.1.refs_1_ = bf16[2,2,128,256]{3,2,1,0:T(8,128)(2,1)S(1)} collective-permute-done((bf16[2,2,128,256]{3,2,1,0:T(8,128)(2,1)S(1)}, bf16[2,2,128,256]{3,2,1,0:T(8,128)(2,1)S(1)}, u32[]{:S(2)}, u32[]{:S(2)}) %collective-permute-start.1) | collective-permute-done | bytes 262176 | tf_op jit(solution)/shard_map/ppermute | solution.py:331
  11.6 0.9 %collective-permute-start.4 = (bf16[2,2,128,256]{3,2,1,0:T(8,128)(2,1)S(1)}, bf16[2,2,128,256]{3,2,1,0:T(8,128)(2,1)S(1)}, u32[]{:S(2)}, u32[]{:S(2)}) collective-permute-start(bf16[2,2,128,256]{3,2,1,0:T(8,128)(2,1)S(1)} %collective-permute-done.1.refs_1_), channel_id=1, source_target_pairs={{0,1},{1,0},{2,3},{3,2},{4,5},{5,4},{6,7},{7,6},{8,9},{9,8},{10,11... | collective-permute-start | bytes 786440 | tf_op jit(solution)/shard_map/ppermute | solution.py:316
  12.5 0.0 collective-permute-done.5.refs_4_
  12.5 1.2 %collective-permute-done.4.refs_2_ = bf16[2,2,128,256]{3,2,1,0:T(8,128)(2,1)S(1)} collective-permute-done((bf16[2,2,128,256]{3,2,1,0:T(8,128)(2,1)S(1)}, bf16[2,2,128,256]{3,2,1,0:T(8,128)(2,1)S(1)}, u32[]{:S(2)}, u32[]{:S(2)}) %collective-permute-start.4) | collective-permute-done | bytes 262176 | tf_op jit(solution)/shard_map/ppermute | solution.py:316
  13.7 0.0 copy-done.2
  13.7 0.0 copy-done.10
  13.7 2.9 %transform.1 = (bf16[2,2,80,256]{3,2,1,0:T(8,128)(2,1)S(1)}, bf16[2,2,80,256]{3,2,1,0:T(8,128)(2,1)S(1)}, bf16[2,2,80,256]{3,2,1,0:T(8,128)(2,1)S(1)}, bf16[1,2,80,256]{3,2,1,0:T(8,128)(2,1)S(1)}) custom-call(s32[52]{0:T(128)S(1)} %get-tuple-element.23.refs_0_, bf16[2,2,128,256]{3,2,1,0:T(8,128)(2,1)S(1)} %collective-permute-done.1.refs_1_, ...), custom_call_target="tpu_custom_call" | custom-call | flops 2400000000 | tf_op jit(solution)/shard_map/transform/pallas_call | solution.py:412
  16.6 1.3 %collective-permute-start.6 = (bf16[2,2,80,256]{3,2,1,0:T(8,128)(2,1)S(1)}, bf16[2,2,80,256]{3,2,1,0:T(8,128)(2,1)S(1)}, u32[]{:S(2)}, u32[]{:S(2)}) collective-permute-start(bf16[2,2,80,256]{3,2,1,0:T(8,128)(2,1)S(1)} %get-tuple-element.28), channel_id=1, source_target_pairs={{0,1},{1,5},{2,3},{3,7},{4,0},{5,9},{6,2},{7,11},{8,4},{9,13},{10,... | collective-permute-start | bytes 491528 | tf_op jit(solution)/shard_map/ppermute | solution.py:331
  17.9 1.3 %collective-permute-start.7 = (bf16[2,2,80,256]{3,2,1,0:T(8,128)(2,1)S(1)}, bf16[2,2,80,256]{3,2,1,0:T(8,128)(2,1)S(1)}, u32[]{:S(2)}, u32[]{:S(2)}) collective-permute-start(bf16[2,2,80,256]{3,2,1,0:T(8,128)(2,1)S(1)} %get-tuple-element.29), channel_id=1, source_target_pairs={{0,1},{1,7},{2,3},{3,5},{4,2},{5,11},{6,0},{7,9},{8,6},{9,15},{10,... | collective-permute-start | bytes 491528 | tf_op jit(solution)/shard_map/ppermute | solution.py:331
  19.2 0.3 collective-permute-start.8
  19.4 7.1 %collective-permute-done.8.refs_4_ = bf16[1,2,80,256]{3,2,1,0:T(8,128)(2,1)S(1)} collective-permute-done((bf16[1,2,80,256]{3,2,1,0:T(8,128)(2,1)S(1)}, bf16[1,2,80,256]{3,2,1,0:T(8,128)(2,1)S(1)}, u32[]{:S(2)}, u32[]{:S(2)}) %collective-permute-start.8) | collective-permute-done | bytes 81952 | tf_op jit(solution)/shard_map/ppermute | solution.py:442
  26.5 0.0 collective-permute-done.6.refs_2_
  26.6 0.0 collective-permute-done.7.refs_3_
  26.6 0.4 %collective-permute-start.9 = (bf16[2,2,80,256]{3,2,1,0:T(8,128)(2,1)S(1)}, bf16[2,2,80,256]{3,2,1,0:T(8,128)(2,1)S(1)}, u32[]{:S(2)}, u32[]{:S(2)}) collective-permute-start(bf16[2,2,80,256]{3,2,1,0:T(8,128)(2,1)S(1)} %collective-permute-done.6.refs_2_), channel_id=1, source_target_pairs={{0,1},{1,0},{2,3},{3,2},{4,5},{5,4},{6,7},{7,6},{8,9},{9,8},{10,11... | collective-permute-start | bytes 491528 | tf_op jit(solution)/shard_map/ppermute | solution.py:316
  27.0 0.1 collective-permute-start.10
  27.1 0.4 %collective-permute-start.11 = (bf16[1,2,80,256]{3,2,1,0:T(8,128)(2,1)S(1)}, bf16[1,2,80,256]{3,2,1,0:T(8,128)(2,1)S(1)}, u32[]{:S(2)}, u32[]{:S(2)}) collective-permute-start(bf16[1,2,80,256]{3,2,1,0:T(8,128)(2,1)S(1)} %collective-permute-done.8.refs_4_), channel_id=1, source_target_pairs={{0,1},{1,0},{2,3},{3,2},{4,5},{5,4},{6,7},{7,6},{8,9},{9,8},{10,11... | collective-permute-start | bytes 245768 | tf_op jit(solution)/shard_map/ppermute | solution.py:316
  27.5 1.4 %deposit.2.refs_5_ = f32[4,2,64,384]{3,2,1,0:T(8,128)S(1)} custom-call(s32[52]{0:T(128)S(1)} %get-tuple-element.23.refs_0_, s32[52]{0:T(128)S(1)} %collective-permute-done.2.refs_1_, bf16[2,2,80,256]{3,2,1,0:T(8,128)(2,1)S(1)} %collective-permute-done.6.refs_2_, bf16[2,2,80,256]{3,2,1,0:T(8,128)(2,1)S(1)} %collective-permute-done.7.refs_3_, ...), custom_call_target="tpu_custom_call" | custom-call | flops 40000000 | tf_op jit(solution)/shard_map/deposit/pallas_call | solution.py:451
  28.9 0.0 collective-permute-done.11.refs_4_
  28.9 0.0 collective-permute-done.9.refs_2_
  28.9 0.0 collective-permute-done.10.refs_3_
  28.9 2.0 %deposit.3 = f32[4,2,64,384]{3,2,1,0:T(8,128)} custom-call(s32[52]{0:T(128)S(1)} %get-tuple-element.23.refs_0_, s32[52]{0:T(128)S(1)} %collective-permute-done.2.refs_1_, bf16[2,2,80,256]{3,2,1,0:T(8,128)(2,1)S(1)} %collective-permute-done.9.refs_2_, bf16[2,2,80,256]{3,2,1,0:T(8,128)(2,1)S(1)} %collective-permute-done.10.refs_3_, ...), custom_call_target="tpu_custom_call" | custom-call | flops 40000000 | tf_op jit(solution)/shard_map/deposit/pallas_call | solution.py:451
Async XLA Ops:
  0.0 0.7 %copy-start.8 = (s32[1,4,2]{1,2,0:T(2,128)S(1)}, s32[1,4,2]{1,2,0:T(2,128)}, u32[]{:S(2)}) copy-start(s32[1,4,2]{1,2,0:T(2,128)} %param.17) | copy-start | bytes 100
  0.0 0.7 %copy-start.6 = (s32[1,4,2]{1,2,0:T(2,128)S(1)}, s32[1,4,2]{1,2,0:T(2,128)}, u32[]{:S(2)}) copy-start(s32[1,4,2]{1,2,0:T(2,128)} %param.15) | copy-start | bytes 100
  0.0 0.7 %copy-start.7 = (s32[1,4,2]{1,2,0:T(2,128)S(1)}, s32[1,4,2]{1,2,0:T(2,128)}, u32[]{:S(2)}) copy-start(s32[1,4,2]{1,2,0:T(2,128)} %param.16) | copy-start | bytes 100
  0.0 0.7 %copy-start.4 = (s32[4,4]{1,0:T(4,128)S(1)}, s32[4,4]{1,0:T(4,128)}, u32[]{:S(2)}) copy-start(s32[4,4]{1,0:T(4,128)} %refs_0_.1) | copy-start | bytes 196
  0.0 0.7 %copy-start.5 = (s32[1,4,2]{1,2,0:T(2,128)S(1)}, s32[1,4,2]{1,2,0:T(2,128)}, u32[]{:S(2)}) copy-start(s32[1,4,2]{1,2,0:T(2,128)} %param.14) | copy-start | bytes 100
  0.0 0.7 %copy-start.9 = (s32[1,4]{1,0:T(1,128)S(1)}, s32[1,4]{1,0:T(1,128)}, u32[]{:S(2)}) copy-start(s32[1,4]{1,0:T(1,128)} %refs_5_.2) | copy-start | bytes 52
  0.7 1.1 %copy-start = (bf16[4,2,128,384]{3,2,1,0:T(8,128)(2,1)S(1)}, bf16[4,2,128,384]{3,2,1,0:T(8,128)(2,1)}, u32[]{:S(2)}) copy-start(bf16[4,2,128,384]{3,2,1,0:T(8,128)(2,1)} %refs_1_.1) | copy-start | bytes 2359300
  1.9 2.1 %copy-start.1 = (bf16[4,2,128,384]{3,2,1,0:T(8,128)(2,1)S(1)}, bf16[4,2,128,384]{3,2,1,0:T(8,128)(2,1)}, u32[]{:S(2)}) copy-start(bf16[4,2,128,384]{3,2,1,0:T(8,128)(2,1)} %refs_1_.1) | copy-start | bytes 2359300
  3.3 2.7 %collective-permute-start = (bf16[2,2,128,256]{3,2,1,0:T(8,128)(2,1)S(1)}, bf16[2,2,128,256]{3,2,1,0:T(8,128)(2,1)S(1)}, u32[]{:S(2)}, u32[]{:S(2)}) collective-permute-start(bf16[2,2,128,256]{3,2,1,0:T(8,128)(2,1)S(1)} %get-tuple-element.22), channel_id=1, source_target_pairs={{0,1},{1,0},{2,3},{3,2},{4,5},{5,4},{6,7},{7,6},{8,9},{9,8},{10,11... | collective-permute-start | bytes 786440 | tf_op jit(solution)/shard_map/ppermute | solution.py:316
  6.0 1.7 %copy-start.3 = (bf16[2,128,256]{2,1,0:T(8,128)(2,1)S(1)}, bf16[2,128,256]{2,1,0:T(8,128)(2,1)}, u32[]{:S(2)}) copy-start(bf16[2,128,256]{2,1,0:T(8,128)(2,1)} %refs_5_.3) | copy-start | bytes 393220
  6.0 7.7 %copy-start.2 = (bf16[2,256,256]{2,1,0:T(8,128)(2,1)S(1)}, bf16[2,256,256]{2,1,0:T(8,128)(2,1)}, u32[]{:S(2)}) copy-start(bf16[2,256,256]{2,1,0:T(8,128)(2,1)} %refs_7_.1) | copy-start | bytes 786436
  6.0 7.6 %copy-start.10 = (bf16[2,256,256]{2,1,0:T(8,128)(2,1)S(1)}, bf16[2,256,256]{2,1,0:T(8,128)(2,1)}, u32[]{:S(2)}) copy-start(bf16[2,256,256]{2,1,0:T(8,128)(2,1)} %constant.2.clone.refs_8_) | copy-start | bytes 786436
  6.1 5.5 %collective-permute-start.1 = (bf16[2,2,128,256]{3,2,1,0:T(8,128)(2,1)S(1)}, bf16[2,2,128,256]{3,2,1,0:T(8,128)(2,1)S(1)}, u32[]{:S(2)}, u32[]{:S(2)}) collective-permute-start(bf16[2,2,128,256]{3,2,1,0:T(8,128)(2,1)S(1)} %add.1), channel_id=1, source_target_pairs={{0,4},{1,0},{2,6},{3,2},{4,8},{5,1},{6,10},{7,3},{8,12},{9,5},{10,... | collective-permute-start | bytes 786440 | tf_op jit(solution)/shard_map/ppermute | solution.py:331
  6.3 6.2 %collective-permute-start.5 = (bf16[2,2,256,256]{3,2,1,0:T(8,128)(2,1)S(1)}, bf16[2,2,256,256]{3,2,1,0:T(8,128)(2,1)S(1)}, u32[]{:S(2)}, u32[]{:S(2)}) collective-permute-start(bf16[2,2,256,256]{3,2,1,0:T(8,128)(2,1)S(1)} %get-tuple-element.26.refs_3_), channel_id=1, source_target_pairs={{0,1},{1,0},{2,3},{3,2},{4,5},{5,4},{6,7},{7,6},{8,9},{9,8},{10,11... | collective-permute-start | bytes 1572872 | tf_op jit(solution)/shard_map/ppermute | solution.py:316
  7.7 2.7 %collective-permute-start.3 = (bf16[2,128,256]{2,1,0:T(8,128)(2,1)S(1)}, bf16[2,128,256]{2,1,0:T(8,128)(2,1)S(1)}, u32[]{:S(2)}, u32[]{:S(2)}) collective-permute-start(bf16[2,128,256]{2,1,0:T(8,128)(2,1)S(1)} %copy-done.3), channel_id=1, source_target_pairs={{0,1},{1,0},{2,3},{3,2},{4,5},{5,4},{6,7},{7,6},{8,9},{9,8},{10,11... | collective-permute-start | bytes 393224 | tf_op jit(solution)/shard_map/ppermute | solution.py:316
  7.7 2.7 %collective-permute-start.2 = (s32[52]{0:T(128)S(1)}, s32[52]{0:T(128)S(1)}, u32[]{:S(2)}, u32[]{:S(2)}) collective-permute-start(s32[52]{0:T(128)S(1)} %get-tuple-element.23.refs_0_), channel_id=1, source_target_pairs={{0,2},{2,0},{1,3},{3,1},{4,6},{6,4},{5,7},{7,5},{8,10},{10,8},{9,1... | collective-permute-start | bytes 632 | tf_op jit(solution)/shard_map/ppermute | solution.py:371
  11.6 2.0 %collective-permute-start.4 = (bf16[2,2,128,256]{3,2,1,0:T(8,128)(2,1)S(1)}, bf16[2,2,128,256]{3,2,1,0:T(8,128)(2,1)S(1)}, u32[]{:S(2)}, u32[]{:S(2)}) collective-permute-start(bf16[2,2,128,256]{3,2,1,0:T(8,128)(2,1)S(1)} %collective-permute-done.1.refs_1_), channel_id=1, source_target_pairs={{0,1},{1,0},{2,3},{3,2},{4,5},{5,4},{6,7},{7,6},{8,9},{9,8},{10,11... | collective-permute-start | bytes 786440 | tf_op jit(solution)/shard_map/ppermute | solution.py:316
  16.6 10.0 %collective-permute-start.6 = (bf16[2,2,80,256]{3,2,1,0:T(8,128)(2,1)S(1)}, bf16[2,2,80,256]{3,2,1,0:T(8,128)(2,1)S(1)}, u32[]{:S(2)}, u32[]{:S(2)}) collective-permute-start(bf16[2,2,80,256]{3,2,1,0:T(8,128)(2,1)S(1)} %get-tuple-element.28), channel_id=1, source_target_pairs={{0,1},{1,5},{2,3},{3,7},{4,0},{5,9},{6,2},{7,11},{8,4},{9,13},{10,... | collective-permute-start | bytes 491528 | tf_op jit(solution)/shard_map/ppermute | solution.py:331
  17.9 8.7 %collective-permute-start.7 = (bf16[2,2,80,256]{3,2,1,0:T(8,128)(2,1)S(1)}, bf16[2,2,80,256]{3,2,1,0:T(8,128)(2,1)S(1)}, u32[]{:S(2)}, u32[]{:S(2)}) collective-permute-start(bf16[2,2,80,256]{3,2,1,0:T(8,128)(2,1)S(1)} %get-tuple-element.29), channel_id=1, source_target_pairs={{0,1},{1,7},{2,3},{3,5},{4,2},{5,11},{6,0},{7,9},{8,6},{9,15},{10,... | collective-permute-start | bytes 491528 | tf_op jit(solution)/shard_map/ppermute | solution.py:331
  19.2 7.4 %collective-permute-start.8 = (bf16[1,2,80,256]{3,2,1,0:T(8,128)(2,1)S(1)}, bf16[1,2,80,256]{3,2,1,0:T(8,128)(2,1)S(1)}, u32[]{:S(2)}, u32[]{:S(2)}) collective-permute-start(bf16[1,2,80,256]{3,2,1,0:T(8,128)(2,1)S(1)} %get-tuple-element.30), channel_id=1, source_target_pairs={{0,2},{2,0},{1,3},{3,1},{4,6},{6,4},{5,7},{7,5},{8,10},{10,8},{9,1... | collective-permute-start | bytes 245768 | tf_op jit(solution)/shard_map/ppermute | solution.py:442
  26.6 2.4 %collective-permute-start.9 = (bf16[2,2,80,256]{3,2,1,0:T(8,128)(2,1)S(1)}, bf16[2,2,80,256]{3,2,1,0:T(8,128)(2,1)S(1)}, u32[]{:S(2)}, u32[]{:S(2)}) collective-permute-start(bf16[2,2,80,256]{3,2,1,0:T(8,128)(2,1)S(1)} %collective-permute-done.6.refs_2_), channel_id=1, source_target_pairs={{0,1},{1,0},{2,3},{3,2},{4,5},{5,4},{6,7},{7,6},{8,9},{9,8},{10,11... | collective-permute-start | bytes 491528 | tf_op jit(solution)/shard_map/ppermute | solution.py:316
  27.0 2.0 %collective-permute-start.10 = (bf16[2,2,80,256]{3,2,1,0:T(8,128)(2,1)S(1)}, bf16[2,2,80,256]{3,2,1,0:T(8,128)(2,1)S(1)}, u32[]{:S(2)}, u32[]{:S(2)}) collective-permute-start(bf16[2,2,80,256]{3,2,1,0:T(8,128)(2,1)S(1)} %collective-permute-done.7.refs_3_), channel_id=1, source_target_pairs={{0,1},{1,0},{2,3},{3,2},{4,5},{5,4},{6,7},{7,6},{8,9},{9,8},{10,11... | collective-permute-start | bytes 491528 | tf_op jit(solution)/shard_map/ppermute | solution.py:316
  27.1 1.8 %collective-permute-start.11 = (bf16[1,2,80,256]{3,2,1,0:T(8,128)(2,1)S(1)}, bf16[1,2,80,256]{3,2,1,0:T(8,128)(2,1)S(1)}, u32[]{:S(2)}, u32[]{:S(2)}) collective-permute-start(bf16[1,2,80,256]{3,2,1,0:T(8,128)(2,1)S(1)} %collective-permute-done.8.refs_4_), channel_id=1, source_target_pairs={{0,1},{1,0},{2,3},{3,2},{4,5},{5,4},{6,7},{7,6},{8,9},{9,8},{10,11... | collective-permute-start | bytes 245768 | tf_op jit(solution)/shard_map/ppermute | solution.py:316

commit v3 on v2

--- a/solution.py
+++ b/solution.py
@@ -13,15 +13,17 @@
 BF = jnp.bfloat16
 F32 = jnp.float32
 VMEM_BYTES = 48 * 2**20
+FILL_VMEM_BYTES = 54 * 2**20
 MAX_SHEAR = 16
 
 
-def dft_table(n):
+def dft_tables(n):
     index = np.arange(n, dtype=np.int64)
     phase = (index[:, None] * index[None, :] % n).astype(np.float64) * (2.0 * math.pi / n)
     scale = 1.0 / math.sqrt(n)
-    table = np.stack([np.cos(phase) * scale, -np.sin(phase) * scale])
-    return table.astype(np.float32).astype(ml_dtypes.bfloat16)
+    re, im = np.cos(phase) * scale, -np.sin(phase) * scale
+    tables = np.stack([np.block([[re, im], [-im, re]]), np.block([[re, -im], [im, re]])])
+    return tables.astype(np.float32).astype(ml_dtypes.bfloat16)
 
 
 def dot(left, right):
@@ -68,14 +70,14 @@
         return slot < self.ref[self.base + 4 * self.count + home]
 
 
-def fill_table(table, shear, by_slot, counts):
+def fill_kernel(shear, scan_x, scan_y, slot_angle, owner, counts, table):
     place = 0
     for i in range(shear.shape[0]):
         for z in range(shear.shape[1]):
             table[place] = shear[i, z]
             place += 1
-    _, slots, strips = by_slot[0].shape
-    for ref in by_slot:
+    _, slots, strips = scan_x.shape
+    for ref in (scan_y, slot_angle, owner, scan_x):
         for home in range(strips):
             for slot in range(slots):
                 table[place] = ref[0, slot, home]
@@ -89,11 +91,7 @@
     strip = lax.axis_index("strip")
     depth = lax.axis_index("depth")
     half = depth if mine else 1 - depth
-    if mine:
-        table, crystal, *parts = refs
-    else:
-        shear, scan_x, scan_y, slot_angle, owner, counts, crystal, *parts, table = refs
-        fill_table(table, shear, (scan_y, slot_angle, owner, scan_x), counts)
+    table, crystal, *parts = refs
     layers, _, wx, ny = crystal.shape
     ints = Table(table, strips, slots, layers)
     frame = parts[0].shape[-1]
@@ -135,26 +133,36 @@
     out[...] = (near[...] + far[...].astype(F32)).astype(out.dtype)
 
 
-def transform_kernel(strips, angles, slots, layers, window, *refs):
-    table, moved, moved_far, middle, middle_far, near, far, probe, tab = refs[:9]
+def cut_kernel(strips, angles, slots, layers, window, table, picks, alive):
     ints = Table(table, strips, slots, layers)
-    outs = refs[9 : 9 + 2 * angles]
-    waves, levels = refs[9 + 2 * angles :]
     quarter = strips // 4
     strip = lax.axis_index("strip")
     plane = lax.axis_index("angle")
     depth = lax.axis_index("depth")
+    share = window - MAX_SHEAR
+    for quota in range(slots):
+        home = lax.rem(strip + (strips - 1) + 4 * (strips - quota % quarter), strips)
+        slot = ints.slot(home, quota)
+        live = jnp.logical_and(home <= strips - 3, ints.alive(home, slot))
+        alive[quota] = jnp.full(alive.shape[1:], jnp.where(live, 1.0, 0.0), F32)
+        offset = ints.offset(home, slot)
+        for shift in range(angles):
+            target = lax.rem(plane + shift, angles)
+            for kind in range(2):
+                reach = 2 * depth if kind == 0 else 1
+                first = reach * (share * angles) + share * target - offset - MAX_SHEAR
+                place = (2 * shift + kind) * window
+                picks[quota, place : place + window] = band_matrix(window, picks.shape[2], first)
+
+
+def transform_kernel(angles, slots, window, *refs):
+    moved, moved_far, middle, middle_far, near, far, probe, tab, picks, alive = refs[:10]
+    outs = refs[10 : 10 + 2 * angles]
+    waves, levels = refs[10 + 2 * angles :]
+    depth = lax.axis_index("depth")
     half = moved.shape[2]
     frame = moved.shape[3]
-    f_re = tab[0]
-    f_im = tab[1]
-    n_im = -f_im
-    homes = []
-    places = []
     for quota in range(slots):
-        home = lax.rem(strip + (strips - 1) + 4 * (strips - quota % quarter), strips)
-        homes.append(home)
-        places.append(ints.slot(home, quota))
         for side, (a_ref, level) in enumerate(((moved, near), (moved_far, far))):
             row = pl.multiple_of((depth if side == 0 else 1 - depth) * half, half)
             here = pl.ds(row, half)
@@ -186,46 +194,28 @@
             axis=0,
         ).astype(dtype)
 
-    def blocks(re, im, low):
-        return jnp.concatenate(
-            [jnp.concatenate([re, im], axis=1), jnp.concatenate([low, re], axis=1)], axis=0
-        )
-
-    ahead = blocks(f_re, f_im, n_im)
-    behind = blocks(f_re, n_im, f_im)
+    ahead = tab[0]
+    behind = tab[1]
     section = side_by_side(dot(waves[...], ahead))
     spectrum = dot(behind, section)
     p_re = probe[0].astype(F32)
     p_im = probe[1].astype(F32)
     residuals = []
     for quota in range(slots):
-        alive = jnp.logical_and(
-            homes[quota] <= strips - 3, ints.alive(homes[quota], places[quota])
-        )
-        alive = jnp.where(alive, 1.0, 0.0).astype(F32)
         s_re = spectrum[:frame, quota * frame : (quota + 1) * frame]
         s_im = spectrum[frame:, quota * frame : (quota + 1) * frame]
         magnitude = jnp.maximum(jnp.sqrt(s_re * s_re + s_im * s_im), 1.0)
-        factor = (1.0 - levels[quota].astype(F32) / magnitude) * alive
+        factor = (1.0 - levels[quota].astype(F32) / magnitude) * alive[quota, :1, :1]
         residuals.append(jnp.concatenate([s_re * factor, s_im * factor], axis=1).astype(BF))
     inverse = side_by_side(dot(jnp.concatenate(residuals, axis=0), behind))
     wave = dot(ahead, inverse)
-    share = window - MAX_SHEAR
     for quota in range(slots):
         b_re = wave[:frame, quota * frame : (quota + 1) * frame]
         b_im = wave[frame:, quota * frame : (quota + 1) * frame]
         back = jnp.concatenate(
             [p_re * b_re + p_im * b_im, p_re * b_im - p_im * b_re], axis=1
         ).astype(BF)
-        offset = ints.offset(homes[quota], places[quota])
-        picks = []
-        for shift in range(angles):
-            target = lax.rem(plane + shift, angles)
-            for kind in range(2):
-                reach = 2 * depth if kind == 0 else 1
-                first = reach * (share * angles) + share * target - offset - MAX_SHEAR
-                picks.append(band_matrix(window, frame, first))
-        cut = dot(jnp.concatenate(picks, axis=0), back).astype(BF)
+        cut = dot(picks[quota], back).astype(BF)
         for place, out in enumerate(outs):
             rows = cut[place * window : (place + 1) * window]
             held = out.shape[0]
@@ -240,45 +230,47 @@
                 out[quota % held, 1] = rows[:, frame:]
 
 
-def deposit_kernel(strips, slots, items, before, last, scale, *refs):
-    laps = sorted({lap for lap, _ in items})
-    tables = dict(zip(laps, refs))
-    refs = refs[len(laps) :]
-    blocks, refs = refs[: len(items)], refs[len(items) :]
-    sums = refs[0] if before else None
-    out = refs[1] if before else refs[0]
-    total, sems = refs[-2:] if last else (out, None)
-    layers, _, share, ny = out.shape
-    window, frame = blocks[0].shape[2:]
+def place_kernel(strips, slots, share, rounds, laps, *refs):
+    tables, refs = refs[:laps], refs[laps:]
     strip = lax.axis_index("strip")
     depth = lax.axis_index("depth")
-    rows = []
+    for (items, layers), left, columns in zip(rounds, refs[::2], refs[1::2]):
+        _, frame, ny = columns.shape
+        window = left.shape[1] // columns.shape[0]
+        entry = 0
+        for lap, kind, held in items:
+            ints = Table(tables[lap], strips, slots, layers)
+            reach = (2 * depth, 2 - 2 * depth, 1, 1)[kind]
+            home = clip(strip - reach, strips - 1)
+            for place in range(held):
+                quota = place
+                if held < slots:
+                    quota = place + held * (depth if kind == 2 else 1 - depth)
+                slot = ints.slot(home, quota)
+                for z, shear in enumerate(ints.shears(home, slot)):
+                    left[z * share : (z + 1) * share, entry * window : (entry + 1) * window] = (
+                        band_matrix(share, window, MAX_SHEAR - shear)
+                    )
+                columns[entry] = band_matrix(frame, ny, ints.column(home, slot))
+                entry += 1
+
+
+def deposit_kernel(before, last, scale, left, columns, *refs):
+    refs, total, sems = (refs[:-2], *refs[-2:]) if last else (refs, refs[-1], None)
+    refs, out = refs[:-1], refs[-1]
+    blocks, sums = (refs[:-1], refs[-1]) if before else (refs, None)
+    layers, _, share, ny = out.shape
+    window = blocks[0].shape[2]
     values = ([], [])
-    for (lap, kind), block in zip(items, blocks):
-        ints = Table(tables[lap], strips, slots, layers)
-        reach = (2 * depth, 2 - 2 * depth, 1, 1)[kind]
-        home = clip(strip - reach, strips - 1)
-        held = block.shape[0]
-        for place in range(held):
-            quota = place
-            if held < slots:
-                quota = place + held * (depth if kind == 2 else 1 - depth)
-            slot = ints.slot(home, quota)
-            rows.append(
-                jnp.concatenate(
-                    [
-                        band_matrix(share, window, MAX_SHEAR - shear)
-                        for shear in ints.shears(home, slot)
-                    ],
-                    axis=0,
-                )
-            )
-            columns = band_matrix(frame, ny, ints.column(home, slot))
+    entry = 0
+    for block in blocks:
+        for place in range(block.shape[0]):
             both = jnp.concatenate([block[place, 0], block[place, 1]], axis=0)
-            placed = dot(both, columns).astype(BF)
+            placed = dot(both, columns[entry]).astype(BF)
             values[0].append(placed[:window])
             values[1].append(placed[window:])
-    left = jnp.concatenate(rows, axis=1)
+            entry += 1
+    left = left[...]
     copies = []
     for part in range(2):
         grown = dot(left, jnp.concatenate(values[part], axis=0)) * scale
@@ -351,26 +343,32 @@
         return permute(x, move)
 
     amplitude_far = swap(amplitude)
-    flat = [jnp.swapaxes(x, 1, 2) for x in (scan_x, scan_y, slot_angle, owner_slot)]
-    ints = (shear, *flat, counts)
+    by_slot = [jnp.swapaxes(x, 1, 2) for x in (scan_x, scan_y, slot_angle, owner_slot)]
+    sources = (shear, *by_slot, counts)
     entries = shear.shape[0] * layers + 4 * strips * slots + strips
-    sent, table = pl.pallas_call(
-        functools.partial(project_kernel, strips, slots, False),
-        out_shape=[
-            jax.ShapeDtypeStruct((slots, 2, half, frame), BF),
-            jax.ShapeDtypeStruct((entries,), jnp.int32),
-        ],
-        in_specs=[smem] * 6 + [vmem],
-        out_specs=[vmem, smem],
-        compiler_params=params,
-        cost_estimate=cost(1.5),
-        name="project_far",
-    )(*ints, crystal)
-    arrived = swap(sent)
+    table = pl.pallas_call(
+        fill_kernel,
+        out_shape=jax.ShapeDtypeStruct((entries,), jnp.int32),
+        in_specs=[smem] * 6,
+        out_specs=smem,
+        compiler_params=pltpu.CompilerParams(vmem_limit_bytes=FILL_VMEM_BYTES),
+        cost_estimate=cost(3),
+        name="fill",
+    )(*sources)
     tables = [table] + [
         lax.ppermute(table, "angle", [(a, (a + t) % angles) for a in range(angles)])
         for t in range(1, angles)
     ]
+    sent = pl.pallas_call(
+        functools.partial(project_kernel, strips, slots, False),
+        out_shape=jax.ShapeDtypeStruct((slots, 2, half, frame), BF),
+        in_specs=[smem, vmem],
+        out_specs=vmem,
+        compiler_params=params,
+        cost_estimate=cost(1.5),
+        name="project_far",
+    )(table, crystal)
+    arrived = swap(sent)
     moving, middle = pl.pallas_call(
         functools.partial(project_kernel, strips, slots, True),
         out_shape=[
@@ -393,6 +391,8 @@
         name="add",
     )(moving, arrived)
 
+    moving, middle_table = lax.optimization_barrier((moving, table))
+
     def by_hops(x, near, beyond):
         if quarter == 1:
             return near(x)
@@ -405,17 +405,31 @@
     moved = by_hops(moving, lambda x: ring(x, 1, 0), lambda x, n: far(x, 1, 0, n, True))
     middle = by_hops(middle, lambda x: x, lambda x, n: far(x, 0, 0, n, True))
     middle_far = swap(middle)
-    moved, tables, amplitude_far = lax.optimization_barrier((moved, tables, amplitude_far))
+    picks, alive = pl.pallas_call(
+        functools.partial(cut_kernel, strips, angles, slots, layers, window),
+        out_shape=[
+            jax.ShapeDtypeStruct((slots, 2 * angles * window, frame), BF),
+            jax.ShapeDtypeStruct((slots, 8, 128), F32),
+        ],
+        in_specs=[smem],
+        out_specs=[vmem] * 2,
+        compiler_params=params,
+        cost_estimate=cost(0.5),
+        name="cut",
+    )(middle_table)
+    moved, tables, amplitude_far, picks, alive = lax.optimization_barrier(
+        (moved, tables, amplitude_far, picks, alive)
+    )
     moved_far = swap(moved)
     split = quarter == 1 and slots % depths == 0
     held = slots // depths if split else slots
     cuts = pl.pallas_call(
-        functools.partial(transform_kernel, strips, angles, slots, layers, window),
+        functools.partial(transform_kernel, angles, slots, window),
         out_shape=[
             jax.ShapeDtypeStruct((held if i > 1 and i % 2 else slots, 2, window, frame), BF)
             for i in range(2 * angles)
         ],
-        in_specs=[smem] + [vmem] * 8,
+        in_specs=[vmem] * 10,
         out_specs=[vmem] * (2 * angles),
         scratch_shapes=[
             pltpu.VMEM((slots * frame, 2 * frame), BF),
@@ -425,11 +439,13 @@
         cost_estimate=cost(3),
         name="transform",
     )(
-        table, moved, moved_far, middle, middle_far,
-        amplitude, amplitude_far, probe, jnp.asarray(dft_table(frame)),
+        moved, moved_far, middle, middle_far,
+        amplitude, amplitude_far, probe, jnp.asarray(dft_tables(frame)),
+        picks, alive,
     )
+    *cuts, tables = lax.optimization_barrier([*cuts, tables])
     blocks = {}
-    for lap in range(angles):
+    for lap in reversed(range(angles)):
         blocks[lap, 0] = by_hops(
             cuts[2 * lap],
             lambda x: ring(x, -1, lap),
@@ -444,14 +460,43 @@
         )
     scale = 1.0 / (shear.shape[0] * angles)
 
-    def deposit(items, sums, last):
-        laps = sorted({lap for lap, _ in items})
+    later = range(1, angles)
+    keys = [(lap, kind) for lap in later for kind in (0, 2)] + [(0, 0)]
+    shared = {0: 1, 2: 3} if split else {0: 1}
+    rounds = [
+        [(lap, kind, blocks[lap, kind].shape[0]) for lap, kind in keys + [(0, 2)]],
+        [(lap, shared[kind], blocks[lap, kind].shape[0]) for lap, kind in keys if kind in shared],
+    ]
+    shapes = []
+    for items in rounds:
+        entries = sum(held for _, _, held in items)
+        shapes.append(jax.ShapeDtypeStruct((layers * share, entries * window), BF))
+        shapes.append(jax.ShapeDtypeStruct((entries, frame, ny), BF))
+    places = pl.pallas_call(
+        functools.partial(
+            place_kernel, strips, slots, share, [(items, layers) for items in rounds], angles
+        ),
+        out_shape=shapes,
+        in_specs=[smem] * angles,
+        out_specs=[vmem] * len(shapes),
+        compiler_params=params,
+        cost_estimate=cost(1.5),
+        name="place",
+    )(*tables)
+    arrivals = lax.optimization_barrier([blocks[key] for key in keys] + list(places))
+    blocks.update(zip(keys, arrivals))
+    places = arrivals[len(keys) :]
+    others = [(lap, shared[kind]) for lap, kind in keys if kind in shared]
+    own = keys + [(0, 2)]
+    blocks.update({(lap, shared[kind]): swap(blocks[lap, kind]) for lap, kind in keys if kind in shared})
+
+    def deposit(items, places, sums, last):
         sums = [] if sums is None else [sums]
         shape = (layers, 2, share, ny)
         return pl.pallas_call(
-            functools.partial(deposit_kernel, strips, slots, items, bool(sums), last, scale),
+            functools.partial(deposit_kernel, bool(sums), last, scale),
             out_shape=jax.ShapeDtypeStruct(shape, F32),
-            in_specs=[smem] * len(laps) + [vmem] * (len(items) + len(sums)),
+            in_specs=[vmem] * (2 + len(items) + len(sums)),
             out_specs=pl.BlockSpec(memory_space=pltpu.HBM) if last else vmem,
             scratch_shapes=[pltpu.VMEM(shape, F32), pltpu.SemaphoreType.DMA((layers, 2))]
             if last
@@ -459,15 +504,9 @@
             compiler_params=params,
             cost_estimate=cost(0.05),
             name="deposit",
-        )(*(tables[lap] for lap in laps), *(blocks[item] for item in items), *sums)
-
-    later = range(1, angles)
-    keys = [(lap, 0) for lap in range(angles)] + [(lap, 2) for lap in later]
-    blocks.update(zip(keys, lax.optimization_barrier([blocks[key] for key in keys])))
-    shared = {0: 1, 2: 3} if split else {0: 1}
-    others = [(lap, shared[kind]) for lap, kind in keys if kind in shared]
-    blocks.update({(lap, shared[kind]): swap(blocks[lap, kind]) for lap, kind in keys if kind in shared})
-    return deposit(others, deposit(keys + [(0, 2)], None, False), True)
+        )(*places, *(blocks[item] for item in items), *sums)
+
+    return deposit(others, places[2:], deposit(own, places[:2], None, False), True)
 
 
 def solution(mesh):

time: 31.1 us -> 28.5 us (0.916)
  waiting for transfers between devices: 11 us -> 7.88 us
  Pallas kernels: 9.75 us -> 11.3 us
  local copies, waits for them, and re-layouts: 1.87 us -> 0.68 us
    ppermute x1, waiting for transfers between devices: 7.14 us -> 4.56 us  [body(): lax.ppermute(x, 'angle', [(a, (a + lap) % angles) for a in range(angles)])]
    pallas_call x3 -> x6, Pallas kernels: 6.35 us -> 8.11 us  [the longest x1 2.32 us: body(): pl.pallas_call(functools.partial(transform_kernel, angles, slots, window)...]
    unnamed x22 -> x12, local copies, waits for them, and re-layouts: 1.87 us -> 0.68 us
    ppermute x1, waiting for transfers between devices: 1.47 us -> 0.82 us  [body(): lax.ppermute(table, 'angle', [(a, (a + t) % angles) for a in range(angles)])]
    ppermute x1, starting transfers between devices: 0.26 us -> 0.63 us  [body(): lax.ppermute(x, 'angle', [(a, (a + lap) % angles) for a in range(angles)])]
  transfers between devices with their start and end apart: 12 -> 12, of which waited for: 4 -> 5; matrix products, arithmetic and copies ran while one was open for 0% -> 0% of each run, Pallas kernels for 11% -> 17%
where the time goes in v3:
time: 28.5 us; the launch traced here: 28.3 us
  Pallas kernels  11.3 us (40%)
  starting transfers between devices  8.33 us (29%)
  waiting for transfers between devices  7.88 us (28%)
  local copies, waits for them, and re-layouts  0.68 us (2%)
    ppermute x1, waiting for transfers between devices, body(): lax.ppermute(x, 'angle', [(a, (a + lap) % angles) for a in range(angles)])  4.56 us
    ppermute x7, starting transfers between devices, swap(): lax.ppermute(x, 'depth', [(d, (d + 1) % depths) for d in range(depths)])  3.92 us
    ppermute x3, starting transfers between devices, permute(): return lax.ppermute(x, axes, pairs)  2.48 us
    pallas_call x1, Pallas kernels, body(): pl.pallas_call(functools.partial(transform_kernel, angles, slots, window)...  2.32 us
    pallas_call x2, Pallas kernels, deposit(): pl.pallas_call(functools.partial(deposit_kernel, bool(sums), last, scale)...  2.3 us
    pallas_call x1, Pallas kernels, body(): pl.pallas_call(functools.partial(project_kernel, strips, slots, True), ou...  1.95 us
    pallas_call x1, Pallas kernels, body(): pl.pallas_call(fill_kernel, out_shape=jax.ShapeDtypeStruct((entries,), jn...  1.45 us
    pallas_call x1, Pallas kernels, body(): pl.pallas_call(functools.partial(place_kernel, strips, slots, share, [(it...  1.41 us
  transfers between devices with their start and end apart: 12, of which 5 were waited for; matrix products, arithmetic and copies ran while one was open for 0% of the time, Pallas kernels for 17%

profile of v3, /device:TPU:17, one launch (start us, length us, event | category | flops | bytes accessed | tf_op | source)
XLA Modules:
  0.0 28.3 jit_solution(3314092393413672920)
XLA Ops:
  0.0 0.0 copy-start
  0.0 1.5 %fill.1.refs_0_.table = s32[52]{0:T(128)} custom-call(s32[4,4]{1,0:T(4,128)} %shear.1, s32[1,2,4]{2,1,0:T(2,128)} %bitcast.4, s32[1,2,4]{2,1,0:T(2,128)} %bitcast.5, s32[1,2,4]{2,1,0:T(2,128)} %bitcast.6, s32[1,2,4]{2,1,0:T(2,128)} %bitcast.7, s32[1,4]{1,0:T(1,128)} %counts.1), custom_call_target="tpu_custom_call" | custom-call | flops 2400000000 | tf_op jit(solution)/shard_map/fill/pallas_call | solution.py:349
  1.5 0.0 copy-done
  1.5 0.0 copy-start.3
  1.5 0.6 %copy-done.3 = s32[52]{0:T(128)S(1)} copy-done((s32[52]{0:T(128)S(1)}, s32[52]{0:T(128)}, u32[]{:S(2)}) %copy-start.3) | copy-done | bytes 232
  2.1 1.2 %project_far.1 = bf16[2,2,128,256]{3,2,1,0:T(8,128)(2,1)S(1)} custom-call(s32[52]{0:T(128)S(1)} %copy-done.3, bf16[4,2,128,384]{3,2,1,0:T(8,128)(2,1)S(1)} %copy-done), custom_call_target="tpu_custom_call" | custom-call | flops 1200000000 | tf_op jit(solution)/shard_map/project_far/pallas_call | solution.py:362
  3.3 0.7 %collective-permute-start = (bf16[2,2,128,256]{3,2,1,0:T(8,128)(2,1)S(1)}, bf16[2,2,128,256]{3,2,1,0:T(8,128)(2,1)S(1)}, u32[]{:S(2)}, u32[]{:S(2)}) collective-permute-start(bf16[2,2,128,256]{3,2,1,0:T(8,128)(2,1)S(1)} %project_far.1), channel_id=1, source_target_pairs={{0,1},{1,0},{2,3},{3,2},{4,5},{5,4},{6,7},{7,6},{8,9},{9,8},{10,11... | collective-permute-start | bytes 786440 | tf_op jit(solution)/shard_map/ppermute | solution.py:308
  4.0 1.9 %project_near.1 = (f32[2,2,128,256]{3,2,1,0:T(8,128)S(1)}, bf16[2,2,256,256]{3,2,1,0:T(8,128)(2,1)S(1)}) custom-call(s32[52]{0:T(128)S(1)} %copy-done.3, bf16[4,2,128,384]{3,2,1,0:T(8,128)(2,1)S(1)} %copy-done), custom_call_target="tpu_custom_call" | custom-call | flops 2000000000 | tf_op jit(solution)/shard_map/project_near/pallas_call | solution.py:372
  6.0 0.0 copy-start.2
  6.0 0.0 copy-start.4
  6.0 0.0 collective-permute-done.far
  6.0 0.0 copy-start.1
  6.0 0.0 copy-start.5
  6.1 0.2 collective-permute-start.1
  6.3 1.4 %collective-permute-start.5 = (bf16[2,2,256,256]{3,2,1,0:T(8,128)(2,1)S(1)}, bf16[2,2,256,256]{3,2,1,0:T(8,128)(2,1)S(1)}, u32[]{:S(2)}, u32[]{:S(2)}) collective-permute-start(bf16[2,2,256,256]{3,2,1,0:T(8,128)(2,1)S(1)} %get-tuple-element.44.refs_2_), channel_id=1, source_target_pairs={{0,1},{1,0},{2,3},{3,2},{4,5},{5,4},{6,7},{7,6},{8,9},{9,8},{10,11... | collective-permute-start | bytes 1572872 | tf_op jit(solution)/shard_map/ppermute | solution.py:308
  7.7 0.0 copy-done.2
  7.7 0.0 collective-permute-start.3
  7.7 0.0 copy-done.4
  7.7 1.3 %collective-permute-start.2 = (s32[52]{0:T(128)S(1)}, s32[52]{0:T(128)S(1)}, u32[]{:S(2)}, u32[]{:S(2)}) collective-permute-start(s32[52]{0:T(128)S(1)} %copy-done.4), channel_id=1, source_target_pairs={{0,2},{2,0},{1,3},{3,1},{4,6},{6,4},{5,7},{7,5},{8,10},{10,8},{9,1... | collective-permute-start | bytes 632 | tf_op jit(solution)/shard_map/ppermute | solution.py:359
  9.0 0.6 %cut.1 = (bf16[2,320,256]{2,1,0:T(8,128)(2,1)S(1)}, f32[2,8,128]{2,1,0:T(8,128)S(1)}) custom-call(s32[52]{0:T(128)S(1)} %copy-done.4), custom_call_target="tpu_custom_call" | custom-call | flops 400000000 | tf_op jit(solution)/shard_map/cut/pallas_call | solution.py:408
  9.6 0.8 %collective-permute-done.2.refs_1_ = s32[52]{0:T(128)S(1)} collective-permute-done((s32[52]{0:T(128)S(1)}, s32[52]{0:T(128)S(1)}, u32[]{:S(2)}, u32[]{:S(2)}) %collective-permute-start.2) | collective-permute-done | bytes 240 | tf_op jit(solution)/shard_map/ppermute | solution.py:359
  10.5 0.0 collective-permute-done.3.refs_5_
  10.5 1.2 %collective-permute-done.1.refs_0_ = bf16[2,2,128,256]{3,2,1,0:T(8,128)(2,1)S(1)} collective-permute-done((bf16[2,2,128,256]{3,2,1,0:T(8,128)(2,1)S(1)}, bf16[2,2,128,256]{3,2,1,0:T(8,128)(2,1)S(1)}, u32[]{:S(2)}, u32[]{:S(2)}) %collective-permute-start.1) | collective-permute-done | bytes 262176 | tf_op jit(solution)/shard_map/ppermute | solution.py:323
  11.6 0.9 %collective-permute-start.4 = (bf16[2,2,128,256]{3,2,1,0:T(8,128)(2,1)S(1)}, bf16[2,2,128,256]{3,2,1,0:T(8,128)(2,1)S(1)}, u32[]{:S(2)}, u32[]{:S(2)}) collective-permute-start(bf16[2,2,128,256]{3,2,1,0:T(8,128)(2,1)S(1)} %collective-permute-done.1.refs_0_), channel_id=1, source_target_pairs={{0,1},{1,0},{2,3},{3,2},{4,5},{5,4},{6,7},{7,6},{8,9},{9,8},{10,11... | collective-permute-start | bytes 786440 | tf_op jit(solution)/shard_map/ppermute | solution.py:308
  12.5 0.0 collective-permute-done.5.refs_3_
  12.5 1.2 %collective-permute-done.4.refs_1_ = bf16[2,2,128,256]{3,2,1,0:T(8,128)(2,1)S(1)} collective-permute-done((bf16[2,2,128,256]{3,2,1,0:T(8,128)(2,1)S(1)}, bf16[2,2,128,256]{3,2,1,0:T(8,128)(2,1)S(1)}, u32[]{:S(2)}, u32[]{:S(2)}) %collective-permute-start.4) | collective-permute-done | bytes 262176 | tf_op jit(solution)/shard_map/ppermute | solution.py:308
  13.7 0.0 copy-done.1
  13.7 0.0 copy-done.5
  13.7 2.3 %transform.1 = (bf16[2,2,80,256]{3,2,1,0:T(8,128)(2,1)S(1)}, bf16[2,2,80,256]{3,2,1,0:T(8,128)(2,1)S(1)}, bf16[2,2,80,256]{3,2,1,0:T(8,128)(2,1)S(1)}, bf16[1,2,80,256]{3,2,1,0:T(8,128)(2,1)S(1)}) custom-call(bf16[2,2,128,256]{3,2,1,0:T(8,128)(2,1)S(1)} %collective-permute-done.1.refs_0_, bf16[2,2,128,256]{3,2,1,0:T(8,128)(2,1)S(1)} %collective-permute-done.4.refs_1_, ...), custom_call_target="tpu_custom_call" | custom-call | flops 2400000000 | tf_op jit(solution)/shard_map/transform/pallas_call | solution.py:426
  16.0 2.3 %collective-permute-start.6 = (bf16[2,2,80,256]{3,2,1,0:T(8,128)(2,1)S(1)}, bf16[2,2,80,256]{3,2,1,0:T(8,128)(2,1)S(1)}, u32[]{:S(2)}, u32[]{:S(2)}) collective-permute-start(bf16[2,2,80,256]{3,2,1,0:T(8,128)(2,1)S(1)} %get-tuple-element.54), channel_id=1, source_target_pairs={{0,1},{1,7},{2,3},{3,5},{4,2},{5,11},{6,0},{7,9},{8,6},{9,15},{10,... | collective-permute-start | bytes 491528 | tf_op jit(solution)/shard_map/ppermute | solution.py:323
  18.3 0.0 collective-permute-start.8
  18.3 0.6 %collective-permute-start.7 = (bf16[1,2,80,256]{3,2,1,0:T(8,128)(2,1)S(1)}, bf16[1,2,80,256]{3,2,1,0:T(8,128)(2,1)S(1)}, u32[]{:S(2)}, u32[]{:S(2)}) collective-permute-start(bf16[1,2,80,256]{3,2,1,0:T(8,128)(2,1)S(1)} %get-tuple-element.55), channel_id=1, source_target_pairs={{0,2},{2,0},{1,3},{3,1},{4,6},{6,4},{5,7},{7,5},{8,10},{10,8},{9,1... | collective-permute-start | bytes 245768 | tf_op jit(solution)/shard_map/ppermute | solution.py:458
  18.9 1.4 %place.1 = (bf16[256,560]{1,0:T(8,128)(2,1)S(1)}, bf16[7,256,384]{2,1,0:T(8,128)(2,1)S(1)}, bf16[256,400]{1,0:T(8,128)(2,1)S(1)}, bf16[5,256,384]{2,1,0:T(8,128)(2,1)S(1)}) custom-call(s32[52]{0:T(128)S(1)} %copy-done.4, s32[52]{0:T(128)S(1)} %collective-permute-done.2.refs_1_), custom_call_target="tpu_custom_call" | custom-call | flops 1200000000 | tf_op jit(solution)/shard_map/place/pallas_call | solution.py:475
  20.4 4.6 %collective-permute-done.7.refs_1_ = bf16[1,2,80,256]{3,2,1,0:T(8,128)(2,1)S(1)} collective-permute-done((bf16[1,2,80,256]{3,2,1,0:T(8,128)(2,1)S(1)}, bf16[1,2,80,256]{3,2,1,0:T(8,128)(2,1)S(1)}, u32[]{:S(2)}, u32[]{:S(2)}) %collective-permute-start.7) | collective-permute-done | bytes 81952 | tf_op jit(solution)/shard_map/ppermute | solution.py:458
  24.9 0.0 collective-permute-done.6.refs_0_
  24.9 0.0 collective-permute-done.8.refs_2_
  24.9 0.4 %collective-permute-start.11 = (bf16[2,2,80,256]{3,2,1,0:T(8,128)(2,1)S(1)}, bf16[2,2,80,256]{3,2,1,0:T(8,128)(2,1)S(1)}, u32[]{:S(2)}, u32[]{:S(2)}) collective-permute-start(bf16[2,2,80,256]{3,2,1,0:T(8,128)(2,1)S(1)} %collective-permute-done.8.refs_2_), channel_id=1, source_target_pairs={{0,1},{1,0},{2,3},{3,2},{4,5},{5,4},{6,7},{7,6},{8,9},{9,8},{10,11... | collective-permute-start | bytes 491528 | tf_op jit(solution)/shard_map/ppermute | solution.py:308
  25.3 0.1 collective-permute-start.9
  25.4 0.4 %collective-permute-start.10 = (bf16[1,2,80,256]{3,2,1,0:T(8,128)(2,1)S(1)}, bf16[1,2,80,256]{3,2,1,0:T(8,128)(2,1)S(1)}, u32[]{:S(2)}, u32[]{:S(2)}) collective-permute-start(bf16[1,2,80,256]{3,2,1,0:T(8,128)(2,1)S(1)} %collective-permute-done.7.refs_1_), channel_id=1, source_target_pairs={{0,1},{1,0},{2,3},{3,2},{4,5},{5,4},{6,7},{7,6},{8,9},{9,8},{10,11... | collective-permute-start | bytes 245768 | tf_op jit(solution)/shard_map/ppermute | solution.py:308
  25.8 0.9 %deposit.2.refs_3_ = f32[4,2,64,384]{3,2,1,0:T(8,128)S(1)} custom-call(bf16[256,560]{1,0:T(8,128)(2,1)S(1)} %get-tuple-element.68.left, bf16[7,256,384]{2,1,0:T(8,128)(2,1)S(1)} %get-tuple-element.69.columns, bf16[2,2,80,256]{3,2,1,0:T(8,128)(2,1)S(1)} %collective-permute-done.6.refs_0_, bf16[1,2,80,256]{3,2,1,0:T(8,128)(2,1)S(1)} %collective-permute-done.7.refs_1_, ...), custom_call_target="tpu_custom_call" | custom-call | flops 40000000 | tf_op jit(solution)/shard_map/deposit/pallas_call | solution.py:496
  26.7 0.1 collective-permute-done.10.refs_1_
  26.8 0.0 collective-permute-done.11.refs_2_
  26.8 0.0 collective-permute-done.9.refs_0_
  26.8 1.4 %deposit.3 = f32[4,2,64,384]{3,2,1,0:T(8,128)} custom-call(bf16[256,400]{1,0:T(8,128)(2,1)S(1)} %get-tuple-element.63.left, bf16[5,256,384]{2,1,0:T(8,128)(2,1)S(1)} %get-tuple-element.64.columns, bf16[2,2,80,256]{3,2,1,0:T(8,128)(2,1)S(1)} %collective-permute-done.9.refs_0_, bf16[1,2,80,256]{3,2,1,0:T(8,128)(2,1)S(1)} %collective-permute-done.10.refs_1_, ...), custom_call_target="tpu_custom_call" | custom-call | flops 40000000 | tf_op jit(solution)/shard_map/deposit/pallas_call | solution.py:496
  (1 shorter events, 0.0 us)
Async XLA Ops:
  0.0 1.5 %copy-start = (bf16[4,2,128,384]{3,2,1,0:T(8,128)(2,1)S(1)}, bf16[4,2,128,384]{3,2,1,0:T(8,128)(2,1)}, u32[]{:S(2)}) copy-start(bf16[4,2,128,384]{3,2,1,0:T(8,128)(2,1)} %refs_1_.3) | copy-start | bytes 2359300
  1.5 0.7 %copy-start.3 = (s32[52]{0:T(128)S(1)}, s32[52]{0:T(128)}, u32[]{:S(2)}) copy-start(s32[52]{0:T(128)} %fill.1.refs_0_.table) | copy-start | bytes 628
  3.3 2.7 %collective-permute-start = (bf16[2,2,128,256]{3,2,1,0:T(8,128)(2,1)S(1)}, bf16[2,2,128,256]{3,2,1,0:T(8,128)(2,1)S(1)}, u32[]{:S(2)}, u32[]{:S(2)}) collective-permute-start(bf16[2,2,128,256]{3,2,1,0:T(8,128)(2,1)S(1)} %project_far.1), channel_id=1, source_target_pairs={{0,1},{1,0},{2,3},{3,2},{4,5},{5,4},{6,7},{7,6},{8,9},{9,8},{10,11... | collective-permute-start | bytes 786440 | tf_op jit(solution)/shard_map/ppermute | solution.py:308
  6.0 1.7 %copy-start.2 = (bf16[2,128,256]{2,1,0:T(8,128)(2,1)S(1)}, bf16[2,128,256]{2,1,0:T(8,128)(2,1)}, u32[]{:S(2)}) copy-start(bf16[2,128,256]{2,1,0:T(8,128)(2,1)} %refs_4_.1) | copy-start | bytes 393220
  6.0 1.7 %copy-start.4 = (s32[52]{0:T(128)S(1)}, s32[52]{0:T(128)}, u32[]{:S(2)}) copy-start(s32[52]{0:T(128)} %fill.1.refs_0_.table) | copy-start | bytes 628
  6.0 7.6 %copy-start.1 = (bf16[2,256,256]{2,1,0:T(8,128)(2,1)S(1)}, bf16[2,256,256]{2,1,0:T(8,128)(2,1)}, u32[]{:S(2)}) copy-start(bf16[2,256,256]{2,1,0:T(8,128)(2,1)} %refs_6_.1) | copy-start | bytes 786436
  6.0 7.6 %copy-start.5 = (bf16[2,512,512]{2,1,0:T(8,128)(2,1)S(1)}, bf16[2,512,512]{2,1,0:T(8,128)(2,1)}, u32[]{:S(2)}) copy-start(bf16[2,512,512]{2,1,0:T(8,128)(2,1)} %constant.2.clone.refs_7_) | copy-start | bytes 3145732
  6.1 5.5 %collective-permute-start.1 = (bf16[2,2,128,256]{3,2,1,0:T(8,128)(2,1)S(1)}, bf16[2,2,128,256]{3,2,1,0:T(8,128)(2,1)S(1)}, u32[]{:S(2)}, u32[]{:S(2)}) collective-permute-start(bf16[2,2,128,256]{3,2,1,0:T(8,128)(2,1)S(1)} %add.1), channel_id=1, source_target_pairs={{0,4},{1,0},{2,6},{3,2},{4,8},{5,1},{6,10},{7,3},{8,12},{9,5},{10,... | collective-permute-start | bytes 786440 | tf_op jit(solution)/shard_map/ppermute | solution.py:323
  6.3 6.2 %collective-permute-start.5 = (bf16[2,2,256,256]{3,2,1,0:T(8,128)(2,1)S(1)}, bf16[2,2,256,256]{3,2,1,0:T(8,128)(2,1)S(1)}, u32[]{:S(2)}, u32[]{:S(2)}) collective-permute-start(bf16[2,2,256,256]{3,2,1,0:T(8,128)(2,1)S(1)} %get-tuple-element.44.refs_2_), channel_id=1, source_target_pairs={{0,1},{1,0},{2,3},{3,2},{4,5},{5,4},{6,7},{7,6},{8,9},{9,8},{10,11... | collective-permute-start | bytes 1572872 | tf_op jit(solution)/shard_map/ppermute | solution.py:308
  7.7 2.8 %collective-permute-start.3 = (bf16[2,128,256]{2,1,0:T(8,128)(2,1)S(1)}, bf16[2,128,256]{2,1,0:T(8,128)(2,1)S(1)}, u32[]{:S(2)}, u32[]{:S(2)}) collective-permute-start(bf16[2,128,256]{2,1,0:T(8,128)(2,1)S(1)} %copy-done.2), channel_id=1, source_target_pairs={{0,1},{1,0},{2,3},{3,2},{4,5},{5,4},{6,7},{7,6},{8,9},{9,8},{10,11... | collective-permute-start | bytes 393224 | tf_op jit(solution)/shard_map/ppermute | solution.py:308
  7.7 2.8 %collective-permute-start.2 = (s32[52]{0:T(128)S(1)}, s32[52]{0:T(128)S(1)}, u32[]{:S(2)}, u32[]{:S(2)}) collective-permute-start(s32[52]{0:T(128)S(1)} %copy-done.4), channel_id=1, source_target_pairs={{0,2},{2,0},{1,3},{3,1},{4,6},{6,4},{5,7},{7,5},{8,10},{10,8},{9,1... | collective-permute-start | bytes 632 | tf_op jit(solution)/shard_map/ppermute | solution.py:359
  11.6 2.0 %collective-permute-start.4 = (bf16[2,2,128,256]{3,2,1,0:T(8,128)(2,1)S(1)}, bf16[2,2,128,256]{3,2,1,0:T(8,128)(2,1)S(1)}, u32[]{:S(2)}, u32[]{:S(2)}) collective-permute-start(bf16[2,2,128,256]{3,2,1,0:T(8,128)(2,1)S(1)} %collective-permute-done.1.refs_0_), channel_id=1, source_target_pairs={{0,1},{1,0},{2,3},{3,2},{4,5},{5,4},{6,7},{7,6},{8,9},{9,8},{10,11... | collective-permute-start | bytes 786440 | tf_op jit(solution)/shard_map/ppermute | solution.py:308
  16.0 8.9 %collective-permute-start.6 = (bf16[2,2,80,256]{3,2,1,0:T(8,128)(2,1)S(1)}, bf16[2,2,80,256]{3,2,1,0:T(8,128)(2,1)S(1)}, u32[]{:S(2)}, u32[]{:S(2)}) collective-permute-start(bf16[2,2,80,256]{3,2,1,0:T(8,128)(2,1)S(1)} %get-tuple-element.54), channel_id=1, source_target_pairs={{0,1},{1,7},{2,3},{3,5},{4,2},{5,11},{6,0},{7,9},{8,6},{9,15},{10,... | collective-permute-start | bytes 491528 | tf_op jit(solution)/shard_map/ppermute | solution.py:323
  18.3 6.6 %collective-permute-start.8 = (bf16[2,2,80,256]{3,2,1,0:T(8,128)(2,1)S(1)}, bf16[2,2,80,256]{3,2,1,0:T(8,128)(2,1)S(1)}, u32[]{:S(2)}, u32[]{:S(2)}) collective-permute-start(bf16[2,2,80,256]{3,2,1,0:T(8,128)(2,1)S(1)} %get-tuple-element.56), channel_id=1, source_target_pairs={{0,1},{1,5},{2,3},{3,7},{4,0},{5,9},{6,2},{7,11},{8,4},{9,13},{10,... | collective-permute-start | bytes 491528 | tf_op jit(solution)/shard_map/ppermute | solution.py:323
  18.3 6.6 %collective-permute-start.7 = (bf16[1,2,80,256]{3,2,1,0:T(8,128)(2,1)S(1)}, bf16[1,2,80,256]{3,2,1,0:T(8,128)(2,1)S(1)}, u32[]{:S(2)}, u32[]{:S(2)}) collective-permute-start(bf16[1,2,80,256]{3,2,1,0:T(8,128)(2,1)S(1)} %get-tuple-element.55), channel_id=1, source_target_pairs={{0,2},{2,0},{1,3},{3,1},{4,6},{6,4},{5,7},{7,5},{8,10},{10,8},{9,1... | collective-permute-start | bytes 245768 | tf_op jit(solution)/shard_map/ppermute | solution.py:458
  24.9 1.9 %collective-permute-start.11 = (bf16[2,2,80,256]{3,2,1,0:T(8,128)(2,1)S(1)}, bf16[2,2,80,256]{3,2,1,0:T(8,128)(2,1)S(1)}, u32[]{:S(2)}, u32[]{:S(2)}) collective-permute-start(bf16[2,2,80,256]{3,2,1,0:T(8,128)(2,1)S(1)} %collective-permute-done.8.refs_2_), channel_id=1, source_target_pairs={{0,1},{1,0},{2,3},{3,2},{4,5},{5,4},{6,7},{7,6},{8,9},{9,8},{10,11... | collective-permute-start | bytes 491528 | tf_op jit(solution)/shard_map/ppermute | solution.py:308
  25.3 1.5 %collective-permute-start.9 = (bf16[2,2,80,256]{3,2,1,0:T(8,128)(2,1)S(1)}, bf16[2,2,80,256]{3,2,1,0:T(8,128)(2,1)S(1)}, u32[]{:S(2)}, u32[]{:S(2)}) collective-permute-start(bf16[2,2,80,256]{3,2,1,0:T(8,128)(2,1)S(1)} %collective-permute-done.6.refs_0_), channel_id=1, source_target_pairs={{0,1},{1,0},{2,3},{3,2},{4,5},{5,4},{6,7},{7,6},{8,9},{9,8},{10,11... | collective-permute-start | bytes 491528 | tf_op jit(solution)/shard_map/ppermute | solution.py:308
  25.4 1.4 %collective-permute-start.10 = (bf16[1,2,80,256]{3,2,1,0:T(8,128)(2,1)S(1)}, bf16[1,2,80,256]{3,2,1,0:T(8,128)(2,1)S(1)}, u32[]{:S(2)}, u32[]{:S(2)}) collective-permute-start(bf16[1,2,80,256]{3,2,1,0:T(8,128)(2,1)S(1)} %collective-permute-done.7.refs_1_), channel_id=1, source_target_pairs={{0,1},{1,0},{2,3},{3,2},{4,5},{5,4},{6,7},{7,6},{8,9},{9,8},{10,11... | collective-permute-start | bytes 245768 | tf_op jit(solution)/shard_map/ppermute | solution.py:308

commit v4 on v3

--- a/solution.py
+++ b/solution.py
@@ -87,7 +87,7 @@
         place += 1
 
 
-def project_kernel(strips, slots, mine, *refs):
+def project_kernel(strips, slots, mine, kinds, *refs):
     strip = lax.axis_index("strip")
     depth = lax.axis_index("depth")
     half = depth if mine else 1 - depth
@@ -97,9 +97,9 @@
     frame = parts[0].shape[-1]
     rows = []
     columns = []
-    for kind, out in enumerate(parts):
+    for kind, out in zip(kinds, parts):
         home = clip(strip - (2 * half if kind == 0 else 1), strips - 1)
-        back = wx * half if kind == 0 else wx
+        back = wx * (1 - half if kind == 1 else half)
         for quota in range(slots):
             slot = ints.slot(home, quota)
             start = ints.offset(home, slot) - back
@@ -119,11 +119,11 @@
         for part in range(2)
     ]
     place = 0
-    for kind, out in enumerate(parts):
+    for entry, out in enumerate(parts):
         tall = out.shape[2]
         for quota in range(slots):
             both = jnp.concatenate([x[place : place + tall] for x in lifted], axis=0)
-            band = dot(both, columns[kind * slots + quota]).astype(out.dtype)
+            band = dot(both, columns[entry * slots + quota]).astype(out.dtype)
             out[quota, 0] = band[:tall]
             out[quota, 1] = band[tall:]
             place += tall
@@ -155,29 +155,35 @@
                 picks[quota, place : place + window] = band_matrix(window, picks.shape[2], first)
 
 
+def section_kernel(moved, middle, middle_far, probe, tab, out, waves):
+    slots, _, half, frame = moved.shape
+    here = pl.ds(pl.multiple_of(lax.axis_index("depth") * half, half), half)
+    p_re = probe[0, here].astype(F32)
+    p_im = probe[1, here].astype(F32)
+    for quota in range(slots):
+        w_re, w_im = (
+            moved[quota, part].astype(F32)
+            + middle[quota, part].astype(F32)
+            + middle_far[quota, part].astype(F32)
+            for part in range(2)
+        )
+        to = slice(quota * half, (quota + 1) * half)
+        waves[to, :frame] = (p_re * w_re - p_im * w_im).astype(BF)
+        waves[to, frame:] = (p_re * w_im + p_im * w_re).astype(BF)
+    out[...] = dot(waves[...], tab[0]).astype(BF)
+
+
 def transform_kernel(angles, slots, window, *refs):
-    moved, moved_far, middle, middle_far, near, far, probe, tab, picks, alive = refs[:10]
-    outs = refs[10 : 10 + 2 * angles]
-    waves, levels = refs[10 + 2 * angles :]
+    section_near, section_far, near, far, probe, tab, picks, alive = refs[:8]
+    outs = refs[8 : 8 + 2 * angles]
+    sections, levels = refs[8 + 2 * angles :]
     depth = lax.axis_index("depth")
-    half = moved.shape[2]
-    frame = moved.shape[3]
+    half, frame = near.shape[1:]
+    row = pl.multiple_of(depth * half, half)
+    row_far = pl.multiple_of((1 - depth) * half, half)
     for quota in range(slots):
-        for side, (a_ref, level) in enumerate(((moved, near), (moved_far, far))):
-            row = pl.multiple_of((depth if side == 0 else 1 - depth) * half, half)
-            here = pl.ds(row, half)
-            w_re, w_im = (
-                a_ref[quota, part].astype(F32)
-                + middle[quota, part, here].astype(F32)
-                + middle_far[quota, part, here].astype(F32)
-                for part in range(2)
-            )
-            p_re = probe[0, here].astype(F32)
-            p_im = probe[1, here].astype(F32)
-            to = pl.ds(row + quota * frame, half)
-            waves[to, :frame] = (p_re * w_re - p_im * w_im).astype(BF)
-            waves[to, frame:] = (p_re * w_im + p_im * w_re).astype(BF)
-            levels[quota, here] = level[quota]
+        levels[quota, pl.ds(row, half)] = near[quota]
+        levels[quota, pl.ds(row_far, half)] = far[quota]
 
     def side_by_side(x, dtype=BF):
         return jnp.concatenate(
@@ -196,7 +202,13 @@
 
     ahead = tab[0]
     behind = tab[1]
-    section = side_by_side(dot(waves[...], ahead))
+    for first, x in ((row, section_near), (row_far, section_far)):
+        for quota in range(slots):
+            for part in range(2):
+                sections[
+                    pl.ds(part * frame + first, half), quota * frame : (quota + 1) * frame
+                ] = x[quota * half : (quota + 1) * half, part * frame : (part + 1) * frame]
+    section = sections[...]
     spectrum = dot(behind, section)
     p_re = probe[0].astype(F32)
     p_im = probe[1].astype(F32)
@@ -355,12 +367,8 @@
         cost_estimate=cost(3),
         name="fill",
     )(*sources)
-    tables = [table] + [
-        lax.ppermute(table, "angle", [(a, (a + t) % angles) for a in range(angles)])
-        for t in range(1, angles)
-    ]
     sent = pl.pallas_call(
-        functools.partial(project_kernel, strips, slots, False),
+        functools.partial(project_kernel, strips, slots, False, (0,)),
         out_shape=jax.ShapeDtypeStruct((slots, 2, half, frame), BF),
         in_specs=[smem, vmem],
         out_specs=vmem,
@@ -369,18 +377,19 @@
         name="project_far",
     )(table, crystal)
     arrived = swap(sent)
-    moving, middle = pl.pallas_call(
-        functools.partial(project_kernel, strips, slots, True),
-        out_shape=[
-            jax.ShapeDtypeStruct((slots, 2, half, frame), F32),
-            jax.ShapeDtypeStruct((slots, 2, frame, frame), BF),
-        ],
-        in_specs=[smem, vmem],
-        out_specs=[vmem, vmem],
-        compiler_params=params,
-        cost_estimate=cost(2.5),
-        name="project_near",
-    )(table, crystal)
+
+    def project(kinds, dtype, micros, name):
+        return pl.pallas_call(
+            functools.partial(project_kernel, strips, slots, True, kinds),
+            out_shape=[jax.ShapeDtypeStruct((slots, 2, half, frame), dtype)] * len(kinds),
+            in_specs=[smem, vmem],
+            out_specs=[vmem] * len(kinds),
+            compiler_params=params,
+            cost_estimate=cost(micros),
+            name=name,
+        )
+
+    (moving,) = project((0,), F32, 1.5, "project_near")(table, crystal)
     moving = pl.pallas_call(
         add_kernel,
         out_shape=jax.ShapeDtypeStruct(moving.shape, BF),
@@ -392,6 +401,7 @@
     )(moving, arrived)
 
     moving, middle_table = lax.optimization_barrier((moving, table))
+    middle, middle_sent = project((1, 2), BF, 1.5, "project_middle")(middle_table, crystal)
 
     def by_hops(x, near, beyond):
         if quarter == 1:
@@ -403,8 +413,10 @@
         return jnp.stack(pieces, axis=1).reshape(x.shape)
 
     moved = by_hops(moving, lambda x: ring(x, 1, 0), lambda x, n: far(x, 1, 0, n, True))
-    middle = by_hops(middle, lambda x: x, lambda x, n: far(x, 0, 0, n, True))
-    middle_far = swap(middle)
+    middle, middle_sent = (
+        by_hops(x, lambda x: x, lambda x, n: far(x, 0, 0, n, True)) for x in (middle, middle_sent)
+    )
+    middle_far = swap(middle_sent)
     picks, alive = pl.pallas_call(
         functools.partial(cut_kernel, strips, angles, slots, layers, window),
         out_shape=[
@@ -417,10 +429,24 @@
         cost_estimate=cost(0.5),
         name="cut",
     )(middle_table)
-    moved, tables, amplitude_far, picks, alive = lax.optimization_barrier(
-        (moved, tables, amplitude_far, picks, alive)
+    moved, amplitude_far, picks, alive, table = lax.optimization_barrier(
+        (moved, amplitude_far, picks, alive, middle_table)
     )
-    moved_far = swap(moved)
+    tables = [table] + [
+        lax.ppermute(table, "angle", [(a, (a + t) % angles) for a in range(angles)])
+        for t in range(1, angles)
+    ]
+    tab = jnp.asarray(dft_tables(frame))
+    section_near = pl.pallas_call(
+        section_kernel,
+        out_shape=jax.ShapeDtypeStruct((slots * half, 2 * frame), BF),
+        in_specs=[vmem] * 5,
+        out_specs=vmem,
+        scratch_shapes=[pltpu.VMEM((slots * half, 2 * frame), BF)],
+        compiler_params=params,
+        cost_estimate=cost(0.7),
+        name="section",
+    )(moved, middle, middle_far, probe, tab)
     split = quarter == 1 and slots % depths == 0
     held = slots // depths if split else slots
     cuts = pl.pallas_call(
@@ -429,18 +455,18 @@
             jax.ShapeDtypeStruct((held if i > 1 and i % 2 else slots, 2, window, frame), BF)
             for i in range(2 * angles)
         ],
-        in_specs=[vmem] * 10,
+        in_specs=[vmem] * 8,
         out_specs=[vmem] * (2 * angles),
         scratch_shapes=[
-            pltpu.VMEM((slots * frame, 2 * frame), BF),
+            pltpu.VMEM((2 * frame, slots * frame), BF),
             pltpu.VMEM((slots, frame, frame), BF),
         ],
         compiler_params=params,
         cost_estimate=cost(3),
         name="transform",
     )(
-        moved, moved_far, middle, middle_far,
-        amplitude, amplitude_far, probe, jnp.asarray(dft_tables(frame)),
+        section_near, swap(section_near),
+        amplitude, amplitude_far, probe, tab,
         picks, alive,
     )
     *cuts, tables = lax.optimization_barrier([*cuts, tables])

time: 28.5 us -> 28 us (0.982)
  waiting for transfers between devices: 7.88 us -> 5.9 us
  Pallas kernels: 11.3 us -> 11.9 us
  starting transfers between devices: 8.33 us -> 8.87 us
  local copies, waits for them, and re-layouts: 0.68 us -> 1.06 us
    pallas_call x2 -> x4, Pallas kernels: 3.11 us -> 4.2 us  [the longest x1 1.52 us: body(): project((1, 2), BF, 1.5, 'project_middle')(middle_table, crystal)]
    ppermute x1, waiting for transfers between devices: 0.82 us -> 0.01 us  [body(): lax.ppermute(table, 'angle', [(a, (a + t) % angles) for a in range(angles)])]
    ppermute x3, waiting for transfers between devices: 1.19 us -> 0.63 us  [permute(): return lax.ppermute(x, axes, pairs)]
    ppermute x7, waiting for transfers between devices: 1.31 us -> 0.8 us  [swap(): lax.ppermute(x, 'depth', [(d, (d + 1) % depths) for d in range(depths)])]
    ppermute x7, starting transfers between devices: 3.92 us -> 4.43 us  [swap(): lax.ppermute(x, 'depth', [(d, (d + 1) % depths) for d in range(depths)])]
    pallas_call x1, Pallas kernels: 2.32 us -> 1.85 us  [body(): pl.pallas_call(functools.partial(transform_kernel, angles, slots, window)...]
    unnamed x12, local copies, waits for them, and re-layouts: 0.68 us -> 1.06 us
  transfers between devices with their start and end apart: 12 -> 12, of which waited for: 5 -> 4; matrix products, arithmetic and copies ran while one was open for 0% -> 0% of each run, Pallas kernels for 17% -> 27%
where the time goes in v4:
time: 28 us; the launch traced here: 27.9 us
  Pallas kernels  11.9 us (42%)
  starting transfers between devices  8.87 us (32%)
  waiting for transfers between devices  5.9 us (21%)
  local copies, waits for them, and re-layouts  1.06 us (4%)
    ppermute x1, waiting for transfers between devices, body(): lax.ppermute(x, 'angle', [(a, (a + lap) % angles) for a in range(angles)])  4.47 us
    ppermute x7, starting transfers between devices, swap(): lax.ppermute(x, 'depth', [(d, (d + 1) % depths) for d in range(depths)])  4.43 us
    ppermute x3, starting transfers between devices, permute(): return lax.ppermute(x, axes, pairs)  2.4 us
    pallas_call x2, Pallas kernels, deposit(): pl.pallas_call(functools.partial(deposit_kernel, bool(sums), last, scale)...  2.3 us
    pallas_call x1, Pallas kernels, body(): pl.pallas_call(functools.partial(transform_kernel, angles, slots, window)...  1.85 us
    pallas_call x1, Pallas kernels, body(): project((1, 2), BF, 1.5, 'project_middle')(middle_table, crystal)  1.52 us
    pallas_call x1, Pallas kernels, body(): pl.pallas_call(fill_kernel, out_shape=jax.ShapeDtypeStruct((entries,), jn...  1.45 us
    pallas_call x1, Pallas kernels, body(): pl.pallas_call(functools.partial(place_kernel, strips, slots, share, [(it...  1.41 us
  transfers between devices with their start and end apart: 12, of which 4 were waited for; matrix products, arithmetic and copies ran while one was open for 0% of the time, Pallas kernels for 27%

profile of v4, /device:TPU:17, one launch (start us, length us, event | category | flops | bytes accessed | tf_op | source)
XLA Modules:
  0.0 27.9 jit_solution(3277791414834825300)
XLA Ops:
  0.0 0.0 copy-start.2
  0.0 1.5 %fill.1.refs_0_.table = s32[52]{0:T(128)} custom-call(s32[4,4]{1,0:T(4,128)} %shear.1, s32[1,2,4]{2,1,0:T(2,128)} %bitcast.4, s32[1,2,4]{2,1,0:T(2,128)} %bitcast.5, s32[1,2,4]{2,1,0:T(2,128)} %bitcast.6, s32[1,2,4]{2,1,0:T(2,128)} %bitcast.7, s32[1,4]{1,0:T(1,128)} %counts.1), custom_call_target="tpu_custom_call" | custom-call | flops 2400000000 | tf_op jit(solution)/shard_map/fill/pallas_call | solution.py:361
  1.5 0.0 copy-done.2
  1.5 0.0 copy-start.4
  1.5 0.6 %copy-done.4 = s32[52]{0:T(128)S(1)} copy-done((s32[52]{0:T(128)S(1)}, s32[52]{0:T(128)}, u32[]{:S(2)}) %copy-start.4) | copy-done | bytes 232
  2.1 1.2 %project_far.1 = bf16[2,2,128,256]{3,2,1,0:T(8,128)(2,1)S(1)} custom-call(s32[52]{0:T(128)S(1)} %copy-done.4, bf16[4,2,128,384]{3,2,1,0:T(8,128)(2,1)S(1)} %copy-done.2), custom_call_target="tpu_custom_call" | custom-call | flops 1200000000 | tf_op jit(solution)/shard_map/project_far/pallas_call | solution.py:370
  3.3 0.7 %collective-permute-start = (bf16[2,2,128,256]{3,2,1,0:T(8,128)(2,1)S(1)}, bf16[2,2,128,256]{3,2,1,0:T(8,128)(2,1)S(1)}, u32[]{:S(2)}, u32[]{:S(2)}) collective-permute-start(bf16[2,2,128,256]{3,2,1,0:T(8,128)(2,1)S(1)} %project_far.1), channel_id=1, source_target_pairs={{0,1},{1,0},{2,3},{3,2},{4,5},{5,4},{6,7},{7,6},{8,9},{9,8},{10,11... | collective-permute-start | bytes 786440 | tf_op jit(solution)/shard_map/ppermute | solution.py:320
  4.0 1.2 %project_near.1.near = f32[2,2,128,256]{3,2,1,0:T(8,128)S(1)} custom-call(s32[52]{0:T(128)S(1)} %copy-done.4, bf16[4,2,128,384]{3,2,1,0:T(8,128)(2,1)S(1)} %copy-done.2), custom_call_target="tpu_custom_call" | custom-call | flops 1200000000 | tf_op jit(solution)/shard_map/project_near/pallas_call | solution.py:392
  5.2 0.0 copy-start.5
  5.2 0.0 collective-permute-done.far
  5.3 0.0 copy-start.3
  5.3 0.2 collective-permute-start.1
  5.5 0.4 %copy-done.5 = s32[52]{0:T(128)S(1)} copy-done((s32[52]{0:T(128)S(1)}, s32[52]{0:T(128)}, u32[]{:S(2)}) %copy-start.5) | copy-done | bytes 232
  5.9 1.5 %project_middle.1 = (bf16[2,2,128,256]{3,2,1,0:T(8,128)(2,1)S(1)}, bf16[2,2,128,256]{3,2,1,0:T(8,128)(2,1)S(1)}) custom-call(s32[52]{0:T(128)S(1)} %copy-done.5, bf16[4,2,128,384]{3,2,1,0:T(8,128)(2,1)S(1)} %copy-done.2), custom_call_target="tpu_custom_call" | custom-call | flops 1200000000 | tf_op jit(solution)/shard_map/project_middle/pallas_call | solution.py:404
  7.4 0.0 copy-start
  7.4 0.0 copy-start.1
  7.4 1.4 %collective-permute-start.3 = (bf16[2,2,128,256]{3,2,1,0:T(8,128)(2,1)S(1)}, bf16[2,2,128,256]{3,2,1,0:T(8,128)(2,1)S(1)}, u32[]{:S(2)}, u32[]{:S(2)}) collective-permute-start(bf16[2,2,128,256]{3,2,1,0:T(8,128)(2,1)S(1)} %get-tuple-element.43), channel_id=1, source_target_pairs={{0,1},{1,0},{2,3},{3,2},{4,5},{5,4},{6,7},{7,6},{8,9},{9,8},{10,11... | collective-permute-start | bytes 786440 | tf_op jit(solution)/shard_map/ppermute | solution.py:320
  8.9 0.0 copy-done.3
  8.9 0.1 collective-permute-start.2
  8.9 0.6 %cut.1 = (bf16[2,320,256]{2,1,0:T(8,128)(2,1)S(1)}, f32[2,8,128]{2,1,0:T(8,128)S(1)}) custom-call(s32[52]{0:T(128)S(1)} %copy-done.5), custom_call_target="tpu_custom_call" | custom-call | flops 400000000 | tf_op jit(solution)/shard_map/cut/pallas_call | solution.py:420
  9.6 0.6 %collective-permute-done.2.refs_3_ = bf16[2,128,256]{2,1,0:T(8,128)(2,1)S(1)} collective-permute-done((bf16[2,128,256]{2,1,0:T(8,128)(2,1)S(1)}, bf16[2,128,256]{2,1,0:T(8,128)(2,1)S(1)}, u32[]{:S(2)}, u32[]{:S(2)}) %collective-permute-start.2) | collective-permute-done | bytes 131104 | tf_op jit(solution)/shard_map/ppermute | solution.py:320
  10.2 0.6 %collective-permute-done.1.moved = bf16[2,2,128,256]{3,2,1,0:T(8,128)(2,1)S(1)} collective-permute-done((bf16[2,2,128,256]{3,2,1,0:T(8,128)(2,1)S(1)}, bf16[2,2,128,256]{3,2,1,0:T(8,128)(2,1)S(1)}, u32[]{:S(2)}, u32[]{:S(2)}) %collective-permute-start.1) | collective-permute-done | bytes 262176 | tf_op jit(solution)/shard_map/ppermute | solution.py:335
  10.8 0.0 collective-permute-done.3.middle_far
  10.8 0.0 copy-done
  10.8 0.0 copy-done.1
  10.9 0.3 %section.1.refs_0_ = bf16[256,512]{1,0:T(8,128)(2,1)S(1)} custom-call(bf16[2,2,128,256]{3,2,1,0:T(8,128)(2,1)S(1)} %collective-permute-done.1.moved, bf16[2,2,128,256]{3,2,1,0:T(8,128)(2,1)S(1)} %get-tuple-element.42.middle, bf16[2,2,128,256]{3,2,1,0:T(8,128)(2,1)S(1)} %collective-permute-done.3.middle_far, bf16[2,256,256]{2,1,0:T(8,128)(2,1)S(1)} %copy-done.1, ...), custom_call_target="tpu_custom_call" | custom-call | flops 560000000 | tf_op jit(solution)/shard_map/section/pallas_call | solution.py:440
  11.2 1.3 %collective-permute-start.4 = (bf16[256,512]{1,0:T(8,128)(2,1)S(1)}, bf16[256,512]{1,0:T(8,128)(2,1)S(1)}, u32[]{:S(2)}, u32[]{:S(2)}) collective-permute-start(bf16[256,512]{1,0:T(8,128)(2,1)S(1)} %section.1.refs_0_), channel_id=1, source_target_pairs={{0,1},{1,0},{2,3},{3,2},{4,5},{5,4},{6,7},{7,6},{8,9},{9,8},{10,11... | collective-permute-start | bytes 786440 | tf_op jit(solution)/shard_map/ppermute | solution.py:320
  12.5 1.2 %collective-permute-start.5 = (s32[52]{0:T(128)S(1)}, s32[52]{0:T(128)S(1)}, u32[]{:S(2)}, u32[]{:S(2)}) collective-permute-start(s32[52]{0:T(128)S(1)} %copy-done.5), channel_id=1, source_target_pairs={{0,2},{2,0},{1,3},{3,1},{4,6},{6,4},{5,7},{7,5},{8,10},{10,8},{9,1... | collective-permute-start | bytes 632 | tf_op jit(solution)/shard_map/ppermute | solution.py:436
  13.7 0.0 collective-permute-done.4.refs_1_
  13.7 1.9 %transform.1 = (bf16[2,2,80,256]{3,2,1,0:T(8,128)(2,1)S(1)}, bf16[2,2,80,256]{3,2,1,0:T(8,128)(2,1)S(1)}, bf16[2,2,80,256]{3,2,1,0:T(8,128)(2,1)S(1)}, bf16[1,2,80,256]{3,2,1,0:T(8,128)(2,1)S(1)}) custom-call(bf16[256,512]{1,0:T(8,128)(2,1)S(1)} %section.1.refs_0_, bf16[256,512]{1,0:T(8,128)(2,1)S(1)} %collective-permute-done.4.refs_1_, ...), custom_call_target="tpu_custom_call" | custom-call | flops 2400000000 | tf_op jit(solution)/shard_map/transform/pallas_call | solution.py:452
  15.6 0.0 collective-permute-done.5.refs_1_
  15.6 2.2 %collective-permute-start.6 = (bf16[2,2,80,256]{3,2,1,0:T(8,128)(2,1)S(1)}, bf16[2,2,80,256]{3,2,1,0:T(8,128)(2,1)S(1)}, u32[]{:S(2)}, u32[]{:S(2)}) collective-permute-start(bf16[2,2,80,256]{3,2,1,0:T(8,128)(2,1)S(1)} %get-tuple-element.52), channel_id=1, source_target_pairs={{0,1},{1,7},{2,3},{3,5},{4,2},{5,11},{6,0},{7,9},{8,6},{9,15},{10,... | collective-permute-start | bytes 491528 | tf_op jit(solution)/shard_map/ppermute | solution.py:335
  17.8 0.0 collective-permute-start.8
  17.8 0.8 %collective-permute-start.7 = (bf16[1,2,80,256]{3,2,1,0:T(8,128)(2,1)S(1)}, bf16[1,2,80,256]{3,2,1,0:T(8,128)(2,1)S(1)}, u32[]{:S(2)}, u32[]{:S(2)}) collective-permute-start(bf16[1,2,80,256]{3,2,1,0:T(8,128)(2,1)S(1)} %get-tuple-element.53), channel_id=1, source_target_pairs={{0,2},{2,0},{1,3},{3,1},{4,6},{6,4},{5,7},{7,5},{8,10},{10,8},{9,1... | collective-permute-start | bytes 245768 | tf_op jit(solution)/shard_map/ppermute | solution.py:484
  18.6 1.4 %place.1 = (bf16[256,560]{1,0:T(8,128)(2,1)S(1)}, bf16[7,256,384]{2,1,0:T(8,128)(2,1)S(1)}, bf16[256,400]{1,0:T(8,128)(2,1)S(1)}, bf16[5,256,384]{2,1,0:T(8,128)(2,1)S(1)}) custom-call(s32[52]{0:T(128)S(1)} %copy-done.5, s32[52]{0:T(128)S(1)} %collective-permute-done.5.refs_1_), custom_call_target="tpu_custom_call" | custom-call | flops 1200000000 | tf_op jit(solution)/shard_map/place/pallas_call | solution.py:501
  20.0 4.5 %collective-permute-done.7.refs_1_ = bf16[1,2,80,256]{3,2,1,0:T(8,128)(2,1)S(1)} collective-permute-done((bf16[1,2,80,256]{3,2,1,0:T(8,128)(2,1)S(1)}, bf16[1,2,80,256]{3,2,1,0:T(8,128)(2,1)S(1)}, u32[]{:S(2)}, u32[]{:S(2)}) %collective-permute-start.7) | collective-permute-done | bytes 81952 | tf_op jit(solution)/shard_map/ppermute | solution.py:484
  24.5 0.0 collective-permute-done.6.refs_0_
  24.5 0.0 collective-permute-done.8.refs_2_
  24.5 0.4 %collective-permute-start.11 = (bf16[2,2,80,256]{3,2,1,0:T(8,128)(2,1)S(1)}, bf16[2,2,80,256]{3,2,1,0:T(8,128)(2,1)S(1)}, u32[]{:S(2)}, u32[]{:S(2)}) collective-permute-start(bf16[2,2,80,256]{3,2,1,0:T(8,128)(2,1)S(1)} %collective-permute-done.8.refs_2_), channel_id=1, source_target_pairs={{0,1},{1,0},{2,3},{3,2},{4,5},{5,4},{6,7},{7,6},{8,9},{9,8},{10,11... | collective-permute-start | bytes 491528 | tf_op jit(solution)/shard_map/ppermute | solution.py:320
  24.9 0.1 collective-permute-start.9
  25.0 0.4 %collective-permute-start.10 = (bf16[1,2,80,256]{3,2,1,0:T(8,128)(2,1)S(1)}, bf16[1,2,80,256]{3,2,1,0:T(8,128)(2,1)S(1)}, u32[]{:S(2)}, u32[]{:S(2)}) collective-permute-start(bf16[1,2,80,256]{3,2,1,0:T(8,128)(2,1)S(1)} %collective-permute-done.7.refs_1_), channel_id=1, source_target_pairs={{0,1},{1,0},{2,3},{3,2},{4,5},{5,4},{6,7},{7,6},{8,9},{9,8},{10,11... | collective-permute-start | bytes 245768 | tf_op jit(solution)/shard_map/ppermute | solution.py:320
  25.4 0.8 %deposit.2.refs_3_ = f32[4,2,64,384]{3,2,1,0:T(8,128)S(1)} custom-call(bf16[256,560]{1,0:T(8,128)(2,1)S(1)} %get-tuple-element.66.left, bf16[7,256,384]{2,1,0:T(8,128)(2,1)S(1)} %get-tuple-element.67.columns, bf16[2,2,80,256]{3,2,1,0:T(8,128)(2,1)S(1)} %collective-permute-done.6.refs_0_, bf16[1,2,80,256]{3,2,1,0:T(8,128)(2,1)S(1)} %collective-permute-done.7.refs_1_, ...), custom_call_target="tpu_custom_call" | custom-call | flops 40000000 | tf_op jit(solution)/shard_map/deposit/pallas_call | solution.py:522
  26.3 0.1 collective-permute-done.10.refs_1_
  26.4 0.0 collective-permute-done.11.refs_2_
  26.4 0.0 collective-permute-done.9.refs_0_
  26.4 1.5 %deposit.3 = f32[4,2,64,384]{3,2,1,0:T(8,128)} custom-call(bf16[256,400]{1,0:T(8,128)(2,1)S(1)} %get-tuple-element.61.left, bf16[5,256,384]{2,1,0:T(8,128)(2,1)S(1)} %get-tuple-element.62.columns, bf16[2,2,80,256]{3,2,1,0:T(8,128)(2,1)S(1)} %collective-permute-done.9.refs_0_, bf16[1,2,80,256]{3,2,1,0:T(8,128)(2,1)S(1)} %collective-permute-done.10.refs_1_, ...), custom_call_target="tpu_custom_call" | custom-call | flops 40000000 | tf_op jit(solution)/shard_map/deposit/pallas_call | solution.py:522
  (1 shorter events, 0.0 us)
Async XLA Ops:
  0.0 1.5 %copy-start.2 = (bf16[4,2,128,384]{3,2,1,0:T(8,128)(2,1)S(1)}, bf16[4,2,128,384]{3,2,1,0:T(8,128)(2,1)}, u32[]{:S(2)}) copy-start(bf16[4,2,128,384]{3,2,1,0:T(8,128)(2,1)} %refs_1_.5) | copy-start | bytes 2359300
  1.5 0.7 %copy-start.4 = (s32[52]{0:T(128)S(1)}, s32[52]{0:T(128)}, u32[]{:S(2)}) copy-start(s32[52]{0:T(128)} %fill.1.refs_0_.table) | copy-start | bytes 628
  3.3 1.9 %collective-permute-start = (bf16[2,2,128,256]{3,2,1,0:T(8,128)(2,1)S(1)}, bf16[2,2,128,256]{3,2,1,0:T(8,128)(2,1)S(1)}, u32[]{:S(2)}, u32[]{:S(2)}) collective-permute-start(bf16[2,2,128,256]{3,2,1,0:T(8,128)(2,1)S(1)} %project_far.1), channel_id=1, source_target_pairs={{0,1},{1,0},{2,3},{3,2},{4,5},{5,4},{6,7},{7,6},{8,9},{9,8},{10,11... | collective-permute-start | bytes 786440 | tf_op jit(solution)/shard_map/ppermute | solution.py:320
  5.2 0.7 %copy-start.5 = (s32[52]{0:T(128)S(1)}, s32[52]{0:T(128)}, u32[]{:S(2)}) copy-start(s32[52]{0:T(128)} %fill.1.refs_0_.table) | copy-start | bytes 628
  5.3 3.6 %copy-start.3 = (bf16[2,128,256]{2,1,0:T(8,128)(2,1)S(1)}, bf16[2,128,256]{2,1,0:T(8,128)(2,1)}, u32[]{:S(2)}) copy-start(bf16[2,128,256]{2,1,0:T(8,128)(2,1)} %refs_2_.1) | copy-start | bytes 393220
  5.3 5.5 %collective-permute-start.1 = (bf16[2,2,128,256]{3,2,1,0:T(8,128)(2,1)S(1)}, bf16[2,2,128,256]{3,2,1,0:T(8,128)(2,1)S(1)}, u32[]{:S(2)}, u32[]{:S(2)}) collective-permute-start(bf16[2,2,128,256]{3,2,1,0:T(8,128)(2,1)S(1)} %add.1), channel_id=1, source_target_pairs={{0,4},{1,0},{2,6},{3,2},{4,8},{5,1},{6,10},{7,3},{8,12},{9,5},{10,... | collective-permute-start | bytes 786440 | tf_op jit(solution)/shard_map/ppermute | solution.py:335
  7.4 3.4 %copy-start = (bf16[2,512,512]{2,1,0:T(8,128)(2,1)S(1)}, bf16[2,512,512]{2,1,0:T(8,128)(2,1)}, u32[]{:S(2)}) copy-start(bf16[2,512,512]{2,1,0:T(8,128)(2,1)} %constant.2.clone.tab.refs_5_) | copy-start | bytes 3145732
  7.4 3.4 %copy-start.1 = (bf16[2,256,256]{2,1,0:T(8,128)(2,1)S(1)}, bf16[2,256,256]{2,1,0:T(8,128)(2,1)}, u32[]{:S(2)}) copy-start(bf16[2,256,256]{2,1,0:T(8,128)(2,1)} %refs_4_.1) | copy-start | bytes 786436
  7.4 3.4 %collective-permute-start.3 = (bf16[2,2,128,256]{3,2,1,0:T(8,128)(2,1)S(1)}, bf16[2,2,128,256]{3,2,1,0:T(8,128)(2,1)S(1)}, u32[]{:S(2)}, u32[]{:S(2)}) collective-permute-start(bf16[2,2,128,256]{3,2,1,0:T(8,128)(2,1)S(1)} %get-tuple-element.43), channel_id=1, source_target_pairs={{0,1},{1,0},{2,3},{3,2},{4,5},{5,4},{6,7},{7,6},{8,9},{9,8},{10,11... | collective-permute-start | bytes 786440 | tf_op jit(solution)/shard_map/ppermute | solution.py:320
  8.9 1.3 %collective-permute-start.2 = (bf16[2,128,256]{2,1,0:T(8,128)(2,1)S(1)}, bf16[2,128,256]{2,1,0:T(8,128)(2,1)S(1)}, u32[]{:S(2)}, u32[]{:S(2)}) collective-permute-start(bf16[2,128,256]{2,1,0:T(8,128)(2,1)S(1)} %copy-done.3), channel_id=1, source_target_pairs={{0,1},{1,0},{2,3},{3,2},{4,5},{5,4},{6,7},{7,6},{8,9},{9,8},{10,11... | collective-permute-start | bytes 393224 | tf_op jit(solution)/shard_map/ppermute | solution.py:320
  11.2 2.5 %collective-permute-start.4 = (bf16[256,512]{1,0:T(8,128)(2,1)S(1)}, bf16[256,512]{1,0:T(8,128)(2,1)S(1)}, u32[]{:S(2)}, u32[]{:S(2)}) collective-permute-start(bf16[256,512]{1,0:T(8,128)(2,1)S(1)} %section.1.refs_0_), channel_id=1, source_target_pairs={{0,1},{1,0},{2,3},{3,2},{4,5},{5,4},{6,7},{7,6},{8,9},{9,8},{10,11... | collective-permute-start | bytes 786440 | tf_op jit(solution)/shard_map/ppermute | solution.py:320
  12.5 3.1 %collective-permute-start.5 = (s32[52]{0:T(128)S(1)}, s32[52]{0:T(128)S(1)}, u32[]{:S(2)}, u32[]{:S(2)}) collective-permute-start(s32[52]{0:T(128)S(1)} %copy-done.5), channel_id=1, source_target_pairs={{0,2},{2,0},{1,3},{3,1},{4,6},{6,4},{5,7},{7,5},{8,10},{10,8},{9,1... | collective-permute-start | bytes 632 | tf_op jit(solution)/shard_map/ppermute | solution.py:436
  15.6 8.9 %collective-permute-start.6 = (bf16[2,2,80,256]{3,2,1,0:T(8,128)(2,1)S(1)}, bf16[2,2,80,256]{3,2,1,0:T(8,128)(2,1)S(1)}, u32[]{:S(2)}, u32[]{:S(2)}) collective-permute-start(bf16[2,2,80,256]{3,2,1,0:T(8,128)(2,1)S(1)} %get-tuple-element.52), channel_id=1, source_target_pairs={{0,1},{1,7},{2,3},{3,5},{4,2},{5,11},{6,0},{7,9},{8,6},{9,15},{10,... | collective-permute-start | bytes 491528 | tf_op jit(solution)/shard_map/ppermute | solution.py:335
  17.8 6.7 %collective-permute-start.8 = (bf16[2,2,80,256]{3,2,1,0:T(8,128)(2,1)S(1)}, bf16[2,2,80,256]{3,2,1,0:T(8,128)(2,1)S(1)}, u32[]{:S(2)}, u32[]{:S(2)}) collective-permute-start(bf16[2,2,80,256]{3,2,1,0:T(8,128)(2,1)S(1)} %get-tuple-element.54), channel_id=1, source_target_pairs={{0,1},{1,5},{2,3},{3,7},{4,0},{5,9},{6,2},{7,11},{8,4},{9,13},{10,... | collective-permute-start | bytes 491528 | tf_op jit(solution)/shard_map/ppermute | solution.py:335
  17.8 6.7 %collective-permute-start.7 = (bf16[1,2,80,256]{3,2,1,0:T(8,128)(2,1)S(1)}, bf16[1,2,80,256]{3,2,1,0:T(8,128)(2,1)S(1)}, u32[]{:S(2)}, u32[]{:S(2)}) collective-permute-start(bf16[1,2,80,256]{3,2,1,0:T(8,128)(2,1)S(1)} %get-tuple-element.53), channel_id=1, source_target_pairs={{0,2},{2,0},{1,3},{3,1},{4,6},{6,4},{5,7},{7,5},{8,10},{10,8},{9,1... | collective-permute-start | bytes 245768 | tf_op jit(solution)/shard_map/ppermute | solution.py:484
  24.5 1.9 %collective-permute-start.11 = (bf16[2,2,80,256]{3,2,1,0:T(8,128)(2,1)S(1)}, bf16[2,2,80,256]{3,2,1,0:T(8,128)(2,1)S(1)}, u32[]{:S(2)}, u32[]{:S(2)}) collective-permute-start(bf16[2,2,80,256]{3,2,1,0:T(8,128)(2,1)S(1)} %collective-permute-done.8.refs_2_), channel_id=1, source_target_pairs={{0,1},{1,0},{2,3},{3,2},{4,5},{5,4},{6,7},{7,6},{8,9},{9,8},{10,11... | collective-permute-start | bytes 491528 | tf_op jit(solution)/shard_map/ppermute | solution.py:320
  24.9 1.5 %collective-permute-start.9 = (bf16[2,2,80,256]{3,2,1,0:T(8,128)(2,1)S(1)}, bf16[2,2,80,256]{3,2,1,0:T(8,128)(2,1)S(1)}, u32[]{:S(2)}, u32[]{:S(2)}) collective-permute-start(bf16[2,2,80,256]{3,2,1,0:T(8,128)(2,1)S(1)} %collective-permute-done.6.refs_0_), channel_id=1, source_target_pairs={{0,1},{1,0},{2,3},{3,2},{4,5},{5,4},{6,7},{7,6},{8,9},{9,8},{10,11... | collective-permute-start | bytes 491528 | tf_op jit(solution)/shard_map/ppermute | solution.py:320
  25.0 1.4 %collective-permute-start.10 = (bf16[1,2,80,256]{3,2,1,0:T(8,128)(2,1)S(1)}, bf16[1,2,80,256]{3,2,1,0:T(8,128)(2,1)S(1)}, u32[]{:S(2)}, u32[]{:S(2)}) collective-permute-start(bf16[1,2,80,256]{3,2,1,0:T(8,128)(2,1)S(1)} %collective-permute-done.7.refs_1_), channel_id=1, source_target_pairs={{0,1},{1,0},{2,3},{3,2},{4,5},{5,4},{6,7},{7,6},{8,9},{9,8},{10,11... | collective-permute-start | bytes 245768 | tf_op jit(solution)/shard_map/ppermute | solution.py:320

commit v5 on v4

--- a/solution.py
+++ b/solution.py
@@ -216,8 +216,8 @@
     for quota in range(slots):
         s_re = spectrum[:frame, quota * frame : (quota + 1) * frame]
         s_im = spectrum[frame:, quota * frame : (quota + 1) * frame]
-        magnitude = jnp.maximum(jnp.sqrt(s_re * s_re + s_im * s_im), 1.0)
-        factor = (1.0 - levels[quota].astype(F32) / magnitude) * alive[quota, :1, :1]
+        inverse_size = jnp.minimum(lax.rsqrt(s_re * s_re + s_im * s_im), 1.0)
+        factor = (1.0 - levels[quota].astype(F32) * inverse_size) * alive[quota, :1, :1]
         residuals.append(jnp.concatenate([s_re * factor, s_im * factor], axis=1).astype(BF))
     inverse = side_by_side(dot(jnp.concatenate(residuals, axis=0), behind))
     wave = dot(ahead, inverse)
@@ -285,10 +285,12 @@
     left = left[...]
     copies = []
     for part in range(2):
-        grown = dot(left, jnp.concatenate(values[part], axis=0)) * scale
+        grown = dot(left, jnp.concatenate(values[part], axis=0))
         for z in range(layers):
             piece = grown[z * share : (z + 1) * share]
-            total[z, part] = piece if sums is None else piece + sums[z, part]
+            if before:
+                piece = piece + sums[z, part]
+            total[z, part] = piece * scale if last else piece
             if last:
                 copies.append(
                     pltpu.make_async_copy(total.at[z, part], out.at[z, part], sems.at[z, part])

time: 28 us -> 27.9 us (level)
  transfers between devices with their start and end apart: 12 -> 12, of which waited for: 4 -> 4; matrix products, arithmetic and copies ran while one was open for 0% -> 0% of each run, Pallas kernels for 27% -> 26%
where the time goes in v5:
time: 27.9 us; the launch traced here: 27.7 us
  Pallas kernels  11.8 us (42%)
  starting transfers between devices  9 us (32%)
  waiting for transfers between devices  5.78 us (21%)
  local copies, waits for them, and re-layouts  1.06 us (4%)
    ppermute x7, starting transfers between devices, swap(): lax.ppermute(x, 'depth', [(d, (d + 1) % depths) for d in range(depths)])  4.44 us
    ppermute x1, waiting for transfers between devices, body(): lax.ppermute(x, 'angle', [(a, (a + lap) % angles) for a in range(angles)])  4.34 us
    ppermute x3, starting transfers between devices, permute(): return lax.ppermute(x, axes, pairs)  2.4 us
    pallas_call x2, Pallas kernels, deposit(): pl.pallas_call(functools.partial(deposit_kernel, bool(sums), last, scale)...  2.3 us
    pallas_call x1, Pallas kernels, body(): pl.pallas_call(functools.partial(transform_kernel, angles, slots, window)...  1.73 us
    pallas_call x1, Pallas kernels, body(): project((1, 2), BF, 1.5, 'project_middle')(middle_table, crystal)  1.52 us
    pallas_call x1, Pallas kernels, body(): pl.pallas_call(fill_kernel, out_shape=jax.ShapeDtypeStruct((entries,), jn...  1.45 us
    pallas_call x1, Pallas kernels, body(): pl.pallas_call(functools.partial(place_kernel, strips, slots, share, [(it...  1.41 us
  transfers between devices with their start and end apart: 12, of which 4 were waited for; matrix products, arithmetic and copies ran while one was open for 0% of the time, Pallas kernels for 26%

profile of v5, /device:TPU:17, one launch (start us, length us, event | category | flops | bytes accessed | tf_op | source)
XLA Modules:
  0.0 27.7 jit_solution(1268029303456642698)
XLA Ops:
  0.0 0.0 copy-start.2
  0.0 1.5 %fill.1.refs_0_.table = s32[52]{0:T(128)} custom-call(s32[4,4]{1,0:T(4,128)} %shear.1, s32[1,2,4]{2,1,0:T(2,128)} %bitcast.4, s32[1,2,4]{2,1,0:T(2,128)} %bitcast.5, s32[1,2,4]{2,1,0:T(2,128)} %bitcast.6, s32[1,2,4]{2,1,0:T(2,128)} %bitcast.7, s32[1,4]{1,0:T(1,128)} %counts.1), custom_call_target="tpu_custom_call" | custom-call | flops 2400000000 | tf_op jit(solution)/shard_map/fill/pallas_call | solution.py:363
  1.5 0.0 copy-done.2
  1.5 0.0 copy-start.4
  1.5 0.6 %copy-done.4 = s32[52]{0:T(128)S(1)} copy-done((s32[52]{0:T(128)S(1)}, s32[52]{0:T(128)}, u32[]{:S(2)}) %copy-start.4) | copy-done | bytes 232
  2.1 1.2 %project_far.1 = bf16[2,2,128,256]{3,2,1,0:T(8,128)(2,1)S(1)} custom-call(s32[52]{0:T(128)S(1)} %copy-done.4, bf16[4,2,128,384]{3,2,1,0:T(8,128)(2,1)S(1)} %copy-done.2), custom_call_target="tpu_custom_call" | custom-call | flops 1200000000 | tf_op jit(solution)/shard_map/project_far/pallas_call | solution.py:372
  3.3 0.7 %collective-permute-start = (bf16[2,2,128,256]{3,2,1,0:T(8,128)(2,1)S(1)}, bf16[2,2,128,256]{3,2,1,0:T(8,128)(2,1)S(1)}, u32[]{:S(2)}, u32[]{:S(2)}) collective-permute-start(bf16[2,2,128,256]{3,2,1,0:T(8,128)(2,1)S(1)} %project_far.1), channel_id=1, source_target_pairs={{0,1},{1,0},{2,3},{3,2},{4,5},{5,4},{6,7},{7,6},{8,9},{9,8},{10,11... | collective-permute-start | bytes 786440 | tf_op jit(solution)/shard_map/ppermute | solution.py:322
  4.0 1.2 %project_near.1.near = f32[2,2,128,256]{3,2,1,0:T(8,128)S(1)} custom-call(s32[52]{0:T(128)S(1)} %copy-done.4, bf16[4,2,128,384]{3,2,1,0:T(8,128)(2,1)S(1)} %copy-done.2), custom_call_target="tpu_custom_call" | custom-call | flops 1200000000 | tf_op jit(solution)/shard_map/project_near/pallas_call | solution.py:394
  5.2 0.0 copy-start.5
  5.2 0.0 collective-permute-done.far
  5.3 0.0 copy-start.3
  5.3 0.2 collective-permute-start.1
  5.5 0.4 %copy-done.5 = s32[52]{0:T(128)S(1)} copy-done((s32[52]{0:T(128)S(1)}, s32[52]{0:T(128)}, u32[]{:S(2)}) %copy-start.5) | copy-done | bytes 232
  5.9 1.5 %project_middle.1 = (bf16[2,2,128,256]{3,2,1,0:T(8,128)(2,1)S(1)}, bf16[2,2,128,256]{3,2,1,0:T(8,128)(2,1)S(1)}) custom-call(s32[52]{0:T(128)S(1)} %copy-done.5, bf16[4,2,128,384]{3,2,1,0:T(8,128)(2,1)S(1)} %copy-done.2), custom_call_target="tpu_custom_call" | custom-call | flops 1200000000 | tf_op jit(solution)/shard_map/project_middle/pallas_call | solution.py:406
  7.4 0.0 copy-start
  7.4 0.0 copy-start.1
  7.4 1.4 %collective-permute-start.3 = (bf16[2,2,128,256]{3,2,1,0:T(8,128)(2,1)S(1)}, bf16[2,2,128,256]{3,2,1,0:T(8,128)(2,1)S(1)}, u32[]{:S(2)}, u32[]{:S(2)}) collective-permute-start(bf16[2,2,128,256]{3,2,1,0:T(8,128)(2,1)S(1)} %get-tuple-element.43), channel_id=1, source_target_pairs={{0,1},{1,0},{2,3},{3,2},{4,5},{5,4},{6,7},{7,6},{8,9},{9,8},{10,11... | collective-permute-start | bytes 786440 | tf_op jit(solution)/shard_map/ppermute | solution.py:322
  8.9 0.0 copy-done.3
  8.9 0.1 collective-permute-start.2
  8.9 0.6 %cut.1 = (bf16[2,320,256]{2,1,0:T(8,128)(2,1)S(1)}, f32[2,8,128]{2,1,0:T(8,128)S(1)}) custom-call(s32[52]{0:T(128)S(1)} %copy-done.5), custom_call_target="tpu_custom_call" | custom-call | flops 400000000 | tf_op jit(solution)/shard_map/cut/pallas_call | solution.py:422
  9.6 0.6 %collective-permute-done.2.refs_3_ = bf16[2,128,256]{2,1,0:T(8,128)(2,1)S(1)} collective-permute-done((bf16[2,128,256]{2,1,0:T(8,128)(2,1)S(1)}, bf16[2,128,256]{2,1,0:T(8,128)(2,1)S(1)}, u32[]{:S(2)}, u32[]{:S(2)}) %collective-permute-start.2) | collective-permute-done | bytes 131104 | tf_op jit(solution)/shard_map/ppermute | solution.py:322
  10.2 0.6 %collective-permute-done.1.moved = bf16[2,2,128,256]{3,2,1,0:T(8,128)(2,1)S(1)} collective-permute-done((bf16[2,2,128,256]{3,2,1,0:T(8,128)(2,1)S(1)}, bf16[2,2,128,256]{3,2,1,0:T(8,128)(2,1)S(1)}, u32[]{:S(2)}, u32[]{:S(2)}) %collective-permute-start.1) | collective-permute-done | bytes 262176 | tf_op jit(solution)/shard_map/ppermute | solution.py:337
  10.8 0.0 collective-permute-done.3.middle_far
  10.8 0.0 copy-done
  10.8 0.0 copy-done.1
  10.9 0.3 %section.1.refs_0_ = bf16[256,512]{1,0:T(8,128)(2,1)S(1)} custom-call(bf16[2,2,128,256]{3,2,1,0:T(8,128)(2,1)S(1)} %collective-permute-done.1.moved, bf16[2,2,128,256]{3,2,1,0:T(8,128)(2,1)S(1)} %get-tuple-element.42.middle, bf16[2,2,128,256]{3,2,1,0:T(8,128)(2,1)S(1)} %collective-permute-done.3.middle_far, bf16[2,256,256]{2,1,0:T(8,128)(2,1)S(1)} %copy-done.1, ...), custom_call_target="tpu_custom_call" | custom-call | flops 560000000 | tf_op jit(solution)/shard_map/section/pallas_call | solution.py:442
  11.2 1.3 %collective-permute-start.4 = (bf16[256,512]{1,0:T(8,128)(2,1)S(1)}, bf16[256,512]{1,0:T(8,128)(2,1)S(1)}, u32[]{:S(2)}, u32[]{:S(2)}) collective-permute-start(bf16[256,512]{1,0:T(8,128)(2,1)S(1)} %section.1.refs_0_), channel_id=1, source_target_pairs={{0,1},{1,0},{2,3},{3,2},{4,5},{5,4},{6,7},{7,6},{8,9},{9,8},{10,11... | collective-permute-start | bytes 786440 | tf_op jit(solution)/shard_map/ppermute | solution.py:322
  12.5 1.2 %collective-permute-start.5 = (s32[52]{0:T(128)S(1)}, s32[52]{0:T(128)S(1)}, u32[]{:S(2)}, u32[]{:S(2)}) collective-permute-start(s32[52]{0:T(128)S(1)} %copy-done.5), channel_id=1, source_target_pairs={{0,2},{2,0},{1,3},{3,1},{4,6},{6,4},{5,7},{7,5},{8,10},{10,8},{9,1... | collective-permute-start | bytes 632 | tf_op jit(solution)/shard_map/ppermute | solution.py:438
  13.7 0.0 collective-permute-done.4.refs_1_
  13.7 1.7 %transform.1 = (bf16[2,2,80,256]{3,2,1,0:T(8,128)(2,1)S(1)}, bf16[2,2,80,256]{3,2,1,0:T(8,128)(2,1)S(1)}, bf16[2,2,80,256]{3,2,1,0:T(8,128)(2,1)S(1)}, bf16[1,2,80,256]{3,2,1,0:T(8,128)(2,1)S(1)}) custom-call(bf16[256,512]{1,0:T(8,128)(2,1)S(1)} %section.1.refs_0_, bf16[256,512]{1,0:T(8,128)(2,1)S(1)} %collective-permute-done.4.refs_1_, ...), custom_call_target="tpu_custom_call" | custom-call | flops 2400000000 | tf_op jit(solution)/shard_map/transform/pallas_call | solution.py:454
  15.4 0.0 collective-permute-done.5.refs_1_
  15.4 2.2 %collective-permute-start.6 = (bf16[2,2,80,256]{3,2,1,0:T(8,128)(2,1)S(1)}, bf16[2,2,80,256]{3,2,1,0:T(8,128)(2,1)S(1)}, u32[]{:S(2)}, u32[]{:S(2)}) collective-permute-start(bf16[2,2,80,256]{3,2,1,0:T(8,128)(2,1)S(1)} %get-tuple-element.52), channel_id=1, source_target_pairs={{0,1},{1,7},{2,3},{3,5},{4,2},{5,11},{6,0},{7,9},{8,6},{9,15},{10,... | collective-permute-start | bytes 491528 | tf_op jit(solution)/shard_map/ppermute | solution.py:337
  17.7 0.0 collective-permute-start.8
  17.7 0.9 %collective-permute-start.7 = (bf16[1,2,80,256]{3,2,1,0:T(8,128)(2,1)S(1)}, bf16[1,2,80,256]{3,2,1,0:T(8,128)(2,1)S(1)}, u32[]{:S(2)}, u32[]{:S(2)}) collective-permute-start(bf16[1,2,80,256]{3,2,1,0:T(8,128)(2,1)S(1)} %get-tuple-element.53), channel_id=1, source_target_pairs={{0,2},{2,0},{1,3},{3,1},{4,6},{6,4},{5,7},{7,5},{8,10},{10,8},{9,1... | collective-permute-start | bytes 245768 | tf_op jit(solution)/shard_map/ppermute | solution.py:486
  18.6 1.4 %place.1 = (bf16[256,560]{1,0:T(8,128)(2,1)S(1)}, bf16[7,256,384]{2,1,0:T(8,128)(2,1)S(1)}, bf16[256,400]{1,0:T(8,128)(2,1)S(1)}, bf16[5,256,384]{2,1,0:T(8,128)(2,1)S(1)}) custom-call(s32[52]{0:T(128)S(1)} %copy-done.5, s32[52]{0:T(128)S(1)} %collective-permute-done.5.refs_1_), custom_call_target="tpu_custom_call" | custom-call | flops 1200000000 | tf_op jit(solution)/shard_map/place/pallas_call | solution.py:503
  20.0 4.3 %collective-permute-done.7.refs_1_ = bf16[1,2,80,256]{3,2,1,0:T(8,128)(2,1)S(1)} collective-permute-done((bf16[1,2,80,256]{3,2,1,0:T(8,128)(2,1)S(1)}, bf16[1,2,80,256]{3,2,1,0:T(8,128)(2,1)S(1)}, u32[]{:S(2)}, u32[]{:S(2)}) %collective-permute-start.7) | collective-permute-done | bytes 81952 | tf_op jit(solution)/shard_map/ppermute | solution.py:486
  24.4 0.0 collective-permute-done.6.refs_0_
  24.4 0.0 collective-permute-done.8.refs_2_
  24.4 0.4 %collective-permute-start.11 = (bf16[2,2,80,256]{3,2,1,0:T(8,128)(2,1)S(1)}, bf16[2,2,80,256]{3,2,1,0:T(8,128)(2,1)S(1)}, u32[]{:S(2)}, u32[]{:S(2)}) collective-permute-start(bf16[2,2,80,256]{3,2,1,0:T(8,128)(2,1)S(1)} %collective-permute-done.8.refs_2_), channel_id=1, source_target_pairs={{0,1},{1,0},{2,3},{3,2},{4,5},{5,4},{6,7},{7,6},{8,9},{9,8},{10,11... | collective-permute-start | bytes 491528 | tf_op jit(solution)/shard_map/ppermute | solution.py:322
  24.8 0.1 collective-permute-start.9
  24.9 0.4 %collective-permute-start.10 = (bf16[1,2,80,256]{3,2,1,0:T(8,128)(2,1)S(1)}, bf16[1,2,80,256]{3,2,1,0:T(8,128)(2,1)S(1)}, u32[]{:S(2)}, u32[]{:S(2)}) collective-permute-start(bf16[1,2,80,256]{3,2,1,0:T(8,128)(2,1)S(1)} %collective-permute-done.7.refs_1_), channel_id=1, source_target_pairs={{0,1},{1,0},{2,3},{3,2},{4,5},{5,4},{6,7},{7,6},{8,9},{9,8},{10,11... | collective-permute-start | bytes 245768 | tf_op jit(solution)/shard_map/ppermute | solution.py:322
  25.3 0.8 %deposit.2.refs_3_ = f32[4,2,64,384]{3,2,1,0:T(8,128)S(1)} custom-call(bf16[256,560]{1,0:T(8,128)(2,1)S(1)} %get-tuple-element.66.left, bf16[7,256,384]{2,1,0:T(8,128)(2,1)S(1)} %get-tuple-element.67.columns, bf16[2,2,80,256]{3,2,1,0:T(8,128)(2,1)S(1)} %collective-permute-done.6.refs_0_, bf16[1,2,80,256]{3,2,1,0:T(8,128)(2,1)S(1)} %collective-permute-done.7.refs_1_, ...), custom_call_target="tpu_custom_call" | custom-call | flops 40000000 | tf_op jit(solution)/shard_map/deposit/pallas_call | solution.py:524
  26.1 0.2 collective-permute-done.10.refs_1_
  26.3 0.0 collective-permute-done.11.refs_2_
  26.3 0.0 collective-permute-done.9.refs_0_
  26.3 1.5 %deposit.3 = f32[4,2,64,384]{3,2,1,0:T(8,128)} custom-call(bf16[256,400]{1,0:T(8,128)(2,1)S(1)} %get-tuple-element.61.left, bf16[5,256,384]{2,1,0:T(8,128)(2,1)S(1)} %get-tuple-element.62.columns, bf16[2,2,80,256]{3,2,1,0:T(8,128)(2,1)S(1)} %collective-permute-done.9.refs_0_, bf16[1,2,80,256]{3,2,1,0:T(8,128)(2,1)S(1)} %collective-permute-done.10.refs_1_, ...), custom_call_target="tpu_custom_call" | custom-call | flops 40000000 | tf_op jit(solution)/shard_map/deposit/pallas_call | solution.py:524
  (1 shorter events, 0.0 us)
Async XLA Ops:
  0.0 1.5 %copy-start.2 = (bf16[4,2,128,384]{3,2,1,0:T(8,128)(2,1)S(1)}, bf16[4,2,128,384]{3,2,1,0:T(8,128)(2,1)}, u32[]{:S(2)}) copy-start(bf16[4,2,128,384]{3,2,1,0:T(8,128)(2,1)} %refs_1_.5) | copy-start | bytes 2359300
  1.5 0.7 %copy-start.4 = (s32[52]{0:T(128)S(1)}, s32[52]{0:T(128)}, u32[]{:S(2)}) copy-start(s32[52]{0:T(128)} %fill.1.refs_0_.table) | copy-start | bytes 628
  3.3 1.9 %collective-permute-start = (bf16[2,2,128,256]{3,2,1,0:T(8,128)(2,1)S(1)}, bf16[2,2,128,256]{3,2,1,0:T(8,128)(2,1)S(1)}, u32[]{:S(2)}, u32[]{:S(2)}) collective-permute-start(bf16[2,2,128,256]{3,2,1,0:T(8,128)(2,1)S(1)} %project_far.1), channel_id=1, source_target_pairs={{0,1},{1,0},{2,3},{3,2},{4,5},{5,4},{6,7},{7,6},{8,9},{9,8},{10,11... | collective-permute-start | bytes 786440 | tf_op jit(solution)/shard_map/ppermute | solution.py:322
  5.2 0.7 %copy-start.5 = (s32[52]{0:T(128)S(1)}, s32[52]{0:T(128)}, u32[]{:S(2)}) copy-start(s32[52]{0:T(128)} %fill.1.refs_0_.table) | copy-start | bytes 628
  5.3 3.6 %copy-start.3 = (bf16[2,128,256]{2,1,0:T(8,128)(2,1)S(1)}, bf16[2,128,256]{2,1,0:T(8,128)(2,1)}, u32[]{:S(2)}) copy-start(bf16[2,128,256]{2,1,0:T(8,128)(2,1)} %refs_2_.1) | copy-start | bytes 393220
  5.3 5.5 %collective-permute-start.1 = (bf16[2,2,128,256]{3,2,1,0:T(8,128)(2,1)S(1)}, bf16[2,2,128,256]{3,2,1,0:T(8,128)(2,1)S(1)}, u32[]{:S(2)}, u32[]{:S(2)}) collective-permute-start(bf16[2,2,128,256]{3,2,1,0:T(8,128)(2,1)S(1)} %add.1), channel_id=1, source_target_pairs={{0,4},{1,0},{2,6},{3,2},{4,8},{5,1},{6,10},{7,3},{8,12},{9,5},{10,... | collective-permute-start | bytes 786440 | tf_op jit(solution)/shard_map/ppermute | solution.py:337
  7.4 3.4 %copy-start = (bf16[2,512,512]{2,1,0:T(8,128)(2,1)S(1)}, bf16[2,512,512]{2,1,0:T(8,128)(2,1)}, u32[]{:S(2)}) copy-start(bf16[2,512,512]{2,1,0:T(8,128)(2,1)} %constant.2.clone.tab.refs_5_) | copy-start | bytes 3145732
  7.4 3.4 %copy-start.1 = (bf16[2,256,256]{2,1,0:T(8,128)(2,1)S(1)}, bf16[2,256,256]{2,1,0:T(8,128)(2,1)}, u32[]{:S(2)}) copy-start(bf16[2,256,256]{2,1,0:T(8,128)(2,1)} %refs_4_.1) | copy-start | bytes 786436
  7.4 3.4 %collective-permute-start.3 = (bf16[2,2,128,256]{3,2,1,0:T(8,128)(2,1)S(1)}, bf16[2,2,128,256]{3,2,1,0:T(8,128)(2,1)S(1)}, u32[]{:S(2)}, u32[]{:S(2)}) collective-permute-start(bf16[2,2,128,256]{3,2,1,0:T(8,128)(2,1)S(1)} %get-tuple-element.43), channel_id=1, source_target_pairs={{0,1},{1,0},{2,3},{3,2},{4,5},{5,4},{6,7},{7,6},{8,9},{9,8},{10,11... | collective-permute-start | bytes 786440 | tf_op jit(solution)/shard_map/ppermute | solution.py:322
  8.9 1.3 %collective-permute-start.2 = (bf16[2,128,256]{2,1,0:T(8,128)(2,1)S(1)}, bf16[2,128,256]{2,1,0:T(8,128)(2,1)S(1)}, u32[]{:S(2)}, u32[]{:S(2)}) collective-permute-start(bf16[2,128,256]{2,1,0:T(8,128)(2,1)S(1)} %copy-done.3), channel_id=1, source_target_pairs={{0,1},{1,0},{2,3},{3,2},{4,5},{5,4},{6,7},{7,6},{8,9},{9,8},{10,11... | collective-permute-start | bytes 393224 | tf_op jit(solution)/shard_map/ppermute | solution.py:322
  11.2 2.5 %collective-permute-start.4 = (bf16[256,512]{1,0:T(8,128)(2,1)S(1)}, bf16[256,512]{1,0:T(8,128)(2,1)S(1)}, u32[]{:S(2)}, u32[]{:S(2)}) collective-permute-start(bf16[256,512]{1,0:T(8,128)(2,1)S(1)} %section.1.refs_0_), channel_id=1, source_target_pairs={{0,1},{1,0},{2,3},{3,2},{4,5},{5,4},{6,7},{7,6},{8,9},{9,8},{10,11... | collective-permute-start | bytes 786440 | tf_op jit(solution)/shard_map/ppermute | solution.py:322
  12.5 3.0 %collective-permute-start.5 = (s32[52]{0:T(128)S(1)}, s32[52]{0:T(128)S(1)}, u32[]{:S(2)}, u32[]{:S(2)}) collective-permute-start(s32[52]{0:T(128)S(1)} %copy-done.5), channel_id=1, source_target_pairs={{0,2},{2,0},{1,3},{3,1},{4,6},{6,4},{5,7},{7,5},{8,10},{10,8},{9,1... | collective-permute-start | bytes 632 | tf_op jit(solution)/shard_map/ppermute | solution.py:438
  15.4 8.9 %collective-permute-start.6 = (bf16[2,2,80,256]{3,2,1,0:T(8,128)(2,1)S(1)}, bf16[2,2,80,256]{3,2,1,0:T(8,128)(2,1)S(1)}, u32[]{:S(2)}, u32[]{:S(2)}) collective-permute-start(bf16[2,2,80,256]{3,2,1,0:T(8,128)(2,1)S(1)} %get-tuple-element.52), channel_id=1, source_target_pairs={{0,1},{1,7},{2,3},{3,5},{4,2},{5,11},{6,0},{7,9},{8,6},{9,15},{10,... | collective-permute-start | bytes 491528 | tf_op jit(solution)/shard_map/ppermute | solution.py:337
  17.7 6.7 %collective-permute-start.8 = (bf16[2,2,80,256]{3,2,1,0:T(8,128)(2,1)S(1)}, bf16[2,2,80,256]{3,2,1,0:T(8,128)(2,1)S(1)}, u32[]{:S(2)}, u32[]{:S(2)}) collective-permute-start(bf16[2,2,80,256]{3,2,1,0:T(8,128)(2,1)S(1)} %get-tuple-element.54), channel_id=1, source_target_pairs={{0,1},{1,5},{2,3},{3,7},{4,0},{5,9},{6,2},{7,11},{8,4},{9,13},{10,... | collective-permute-start | bytes 491528 | tf_op jit(solution)/shard_map/ppermute | solution.py:337
  17.7 6.7 %collective-permute-start.7 = (bf16[1,2,80,256]{3,2,1,0:T(8,128)(2,1)S(1)}, bf16[1,2,80,256]{3,2,1,0:T(8,128)(2,1)S(1)}, u32[]{:S(2)}, u32[]{:S(2)}) collective-permute-start(bf16[1,2,80,256]{3,2,1,0:T(8,128)(2,1)S(1)} %get-tuple-element.53), channel_id=1, source_target_pairs={{0,2},{2,0},{1,3},{3,1},{4,6},{6,4},{5,7},{7,5},{8,10},{10,8},{9,1... | collective-permute-start | bytes 245768 | tf_op jit(solution)/shard_map/ppermute | solution.py:486
  24.4 1.9 %collective-permute-start.11 = (bf16[2,2,80,256]{3,2,1,0:T(8,128)(2,1)S(1)}, bf16[2,2,80,256]{3,2,1,0:T(8,128)(2,1)S(1)}, u32[]{:S(2)}, u32[]{:S(2)}) collective-permute-start(bf16[2,2,80,256]{3,2,1,0:T(8,128)(2,1)S(1)} %collective-permute-done.8.refs_2_), channel_id=1, source_target_pairs={{0,1},{1,0},{2,3},{3,2},{4,5},{5,4},{6,7},{7,6},{8,9},{9,8},{10,11... | collective-permute-start | bytes 491528 | tf_op jit(solution)/shard_map/ppermute | solution.py:322
  24.8 1.5 %collective-permute-start.9 = (bf16[2,2,80,256]{3,2,1,0:T(8,128)(2,1)S(1)}, bf16[2,2,80,256]{3,2,1,0:T(8,128)(2,1)S(1)}, u32[]{:S(2)}, u32[]{:S(2)}) collective-permute-start(bf16[2,2,80,256]{3,2,1,0:T(8,128)(2,1)S(1)} %collective-permute-done.6.refs_0_), channel_id=1, source_target_pairs={{0,1},{1,0},{2,3},{3,2},{4,5},{5,4},{6,7},{7,6},{8,9},{9,8},{10,11... | collective-permute-start | bytes 491528 | tf_op jit(solution)/shard_map/ppermute | solution.py:322
  24.9 1.4 %collective-permute-start.10 = (bf16[1,2,80,256]{3,2,1,0:T(8,128)(2,1)S(1)}, bf16[1,2,80,256]{3,2,1,0:T(8,128)(2,1)S(1)}, u32[]{:S(2)}, u32[]{:S(2)}) collective-permute-start(bf16[1,2,80,256]{3,2,1,0:T(8,128)(2,1)S(1)} %collective-permute-done.7.refs_1_), channel_id=1, source_target_pairs={{0,1},{1,0},{2,3},{3,2},{4,5},{5,4},{6,7},{7,6},{8,9},{9,8},{10,11... | collective-permute-start | bytes 245768 | tf_op jit(solution)/shard_map/ppermute | solution.py:322

commit v6 on v5

--- a/solution.py
+++ b/solution.py
@@ -471,7 +471,6 @@
         amplitude, amplitude_far, probe, tab,
         picks, alive,
     )
-    *cuts, tables = lax.optimization_barrier([*cuts, tables])
     blocks = {}
     for lap in reversed(range(angles)):
         blocks[lap, 0] = by_hops(
@@ -508,7 +507,7 @@
         in_specs=[smem] * angles,
         out_specs=[vmem] * len(shapes),
         compiler_params=params,
-        cost_estimate=cost(1.5),
+        cost_estimate=cost(0.05),
         name="place",
     )(*tables)
     arrivals = lax.optimization_barrier([blocks[key] for key in keys] + list(places))

time: 27.9 us -> 29.4 us (1.054)
  waiting for transfers between devices: 5.78 us -> 7.73 us
  starting transfers between devices: 9 us -> 8.52 us
    ppermute x1, waiting for transfers between devices: 0.01 us -> 5.14 us  [body(): lax.ppermute(table, 'angle', [(a, (a + t) % angles) for a in range(angles)])]
    ppermute x1, waiting for transfers between devices: 4.34 us -> 0.01 us  [body(): lax.ppermute(x, 'angle', [(a, (a + lap) % angles) for a in range(angles)])]
    ppermute x7, waiting for transfers between devices: 0.8 us -> 1.95 us  [swap(): lax.ppermute(x, 'depth', [(d, (d + 1) % depths) for d in range(depths)])]
    ppermute x1, starting transfers between devices: 1.23 us -> 0.85 us  [body(): lax.ppermute(table, 'angle', [(a, (a + t) % angles) for a in range(angles)])]
  transfers between devices with their start and end apart: 12 -> 12, of which waited for: 4 -> 5; matrix products, arithmetic and copies ran while one was open for 0% -> 0% of each run, Pallas kernels for 26% -> 19%
where the time goes in v6:
time: 29.4 us; the launch traced here: 29.2 us
  Pallas kernels  11.8 us (40%)
  starting transfers between devices  8.52 us (29%)
  waiting for transfers between devices  7.73 us (26%)
  local copies, waits for them, and re-layouts  1.06 us (4%)
    ppermute x1, waiting for transfers between devices, body(): lax.ppermute(table, 'angle', [(a, (a + t) % angles) for a in range(angles)])  5.14 us
    ppermute x7, starting transfers between devices, swap(): lax.ppermute(x, 'depth', [(d, (d + 1) % depths) for d in range(depths)])  4.55 us
    ppermute x3, starting transfers between devices, permute(): return lax.ppermute(x, axes, pairs)  2.47 us
    pallas_call x2, Pallas kernels, deposit(): pl.pallas_call(functools.partial(deposit_kernel, bool(sums), last, scale)...  2.3 us
    ppermute x7, waiting for transfers between devices, swap(): lax.ppermute(x, 'depth', [(d, (d + 1) % depths) for d in range(depths)])  1.95 us
    pallas_call x1, Pallas kernels, body(): pl.pallas_call(functools.partial(transform_kernel, angles, slots, window)...  1.73 us
    pallas_call x1, Pallas kernels, body(): project((1, 2), BF, 1.5, 'project_middle')(middle_table, crystal)  1.52 us
    pallas_call x1, Pallas kernels, body(): pl.pallas_call(fill_kernel, out_shape=jax.ShapeDtypeStruct((entries,), jn...  1.45 us
  transfers between devices with their start and end apart: 12, of which 5 were waited for; matrix products, arithmetic and copies ran while one was open for 0% of the time, Pallas kernels for 19%

profile of v6, /device:TPU:17, one launch (start us, length us, event | category | flops | bytes accessed | tf_op | source)
XLA Modules:
  0.0 29.2 jit_solution(8725384266827834121)
XLA Ops:
  0.0 0.0 copy-start.2
  0.0 1.5 %fill.1.refs_0_.table = s32[52]{0:T(128)} custom-call(s32[4,4]{1,0:T(4,128)} %shear.1, s32[1,2,4]{2,1,0:T(2,128)} %bitcast.4, s32[1,2,4]{2,1,0:T(2,128)} %bitcast.5, s32[1,2,4]{2,1,0:T(2,128)} %bitcast.6, s32[1,2,4]{2,1,0:T(2,128)} %bitcast.7, s32[1,4]{1,0:T(1,128)} %counts.1), custom_call_target="tpu_custom_call" | custom-call | flops 2400000000 | tf_op jit(solution)/shard_map/fill/pallas_call | solution.py:363
  1.5 0.0 copy-done.2
  1.5 0.0 copy-start.4
  1.5 0.6 %copy-done.4 = s32[52]{0:T(128)S(1)} copy-done((s32[52]{0:T(128)S(1)}, s32[52]{0:T(128)}, u32[]{:S(2)}) %copy-start.4) | copy-done | bytes 232
  2.1 1.2 %project_far.1 = bf16[2,2,128,256]{3,2,1,0:T(8,128)(2,1)S(1)} custom-call(s32[52]{0:T(128)S(1)} %copy-done.4, bf16[4,2,128,384]{3,2,1,0:T(8,128)(2,1)S(1)} %copy-done.2), custom_call_target="tpu_custom_call" | custom-call | flops 1200000000 | tf_op jit(solution)/shard_map/project_far/pallas_call | solution.py:372
  3.3 0.7 %collective-permute-start = (bf16[2,2,128,256]{3,2,1,0:T(8,128)(2,1)S(1)}, bf16[2,2,128,256]{3,2,1,0:T(8,128)(2,1)S(1)}, u32[]{:S(2)}, u32[]{:S(2)}) collective-permute-start(bf16[2,2,128,256]{3,2,1,0:T(8,128)(2,1)S(1)} %project_far.1), channel_id=1, source_target_pairs={{0,1},{1,0},{2,3},{3,2},{4,5},{5,4},{6,7},{7,6},{8,9},{9,8},{10,11... | collective-permute-start | bytes 786440 | tf_op jit(solution)/shard_map/ppermute | solution.py:322
  4.0 1.2 %project_near.1.near = f32[2,2,128,256]{3,2,1,0:T(8,128)S(1)} custom-call(s32[52]{0:T(128)S(1)} %copy-done.4, bf16[4,2,128,384]{3,2,1,0:T(8,128)(2,1)S(1)} %copy-done.2), custom_call_target="tpu_custom_call" | custom-call | flops 1200000000 | tf_op jit(solution)/shard_map/project_near/pallas_call | solution.py:394
  5.2 0.0 copy-start.5
  5.2 0.0 collective-permute-done.far
  5.3 0.0 copy-start.3
  5.3 0.2 collective-permute-start.1
  5.5 0.4 %copy-done.5 = s32[52]{0:T(128)S(1)} copy-done((s32[52]{0:T(128)S(1)}, s32[52]{0:T(128)}, u32[]{:S(2)}) %copy-start.5) | copy-done | bytes 232
  5.9 1.5 %project_middle.1 = (bf16[2,2,128,256]{3,2,1,0:T(8,128)(2,1)S(1)}, bf16[2,2,128,256]{3,2,1,0:T(8,128)(2,1)S(1)}) custom-call(s32[52]{0:T(128)S(1)} %copy-done.5, bf16[4,2,128,384]{3,2,1,0:T(8,128)(2,1)S(1)} %copy-done.2), custom_call_target="tpu_custom_call" | custom-call | flops 1200000000 | tf_op jit(solution)/shard_map/project_middle/pallas_call | solution.py:406
  7.4 0.0 copy-start
  7.4 0.0 copy-start.1
  7.4 1.4 %collective-permute-start.3 = (bf16[2,2,128,256]{3,2,1,0:T(8,128)(2,1)S(1)}, bf16[2,2,128,256]{3,2,1,0:T(8,128)(2,1)S(1)}, u32[]{:S(2)}, u32[]{:S(2)}) collective-permute-start(bf16[2,2,128,256]{3,2,1,0:T(8,128)(2,1)S(1)} %get-tuple-element.37), channel_id=1, source_target_pairs={{0,1},{1,0},{2,3},{3,2},{4,5},{5,4},{6,7},{7,6},{8,9},{9,8},{10,11... | collective-permute-start | bytes 786440 | tf_op jit(solution)/shard_map/ppermute | solution.py:322
  8.9 0.0 copy-done.3
  8.9 0.1 collective-permute-start.2
  8.9 0.6 %cut.1 = (bf16[2,320,256]{2,1,0:T(8,128)(2,1)S(1)}, f32[2,8,128]{2,1,0:T(8,128)S(1)}) custom-call(s32[52]{0:T(128)S(1)} %copy-done.5), custom_call_target="tpu_custom_call" | custom-call | flops 400000000 | tf_op jit(solution)/shard_map/cut/pallas_call | solution.py:422
  9.6 0.6 %collective-permute-done.2.refs_3_ = bf16[2,128,256]{2,1,0:T(8,128)(2,1)S(1)} collective-permute-done((bf16[2,128,256]{2,1,0:T(8,128)(2,1)S(1)}, bf16[2,128,256]{2,1,0:T(8,128)(2,1)S(1)}, u32[]{:S(2)}, u32[]{:S(2)}) %collective-permute-start.2) | collective-permute-done | bytes 131104 | tf_op jit(solution)/shard_map/ppermute | solution.py:322
  10.2 0.6 %collective-permute-done.1.moved = bf16[2,2,128,256]{3,2,1,0:T(8,128)(2,1)S(1)} collective-permute-done((bf16[2,2,128,256]{3,2,1,0:T(8,128)(2,1)S(1)}, bf16[2,2,128,256]{3,2,1,0:T(8,128)(2,1)S(1)}, u32[]{:S(2)}, u32[]{:S(2)}) %collective-permute-start.1) | collective-permute-done | bytes 262176 | tf_op jit(solution)/shard_map/ppermute | solution.py:337
  10.8 0.0 collective-permute-done.3.middle_far
  10.8 0.0 copy-done
  10.8 0.0 copy-done.1
  10.9 0.3 %section.1.refs_0_ = bf16[256,512]{1,0:T(8,128)(2,1)S(1)} custom-call(bf16[2,2,128,256]{3,2,1,0:T(8,128)(2,1)S(1)} %collective-permute-done.1.moved, bf16[2,2,128,256]{3,2,1,0:T(8,128)(2,1)S(1)} %get-tuple-element.36.middle, bf16[2,2,128,256]{3,2,1,0:T(8,128)(2,1)S(1)} %collective-permute-done.3.middle_far, bf16[2,256,256]{2,1,0:T(8,128)(2,1)S(1)} %copy-done.1, ...), custom_call_target="tpu_custom_call" | custom-call | flops 560000000 | tf_op jit(solution)/shard_map/section/pallas_call | solution.py:442
  11.2 1.3 %collective-permute-start.4 = (bf16[256,512]{1,0:T(8,128)(2,1)S(1)}, bf16[256,512]{1,0:T(8,128)(2,1)S(1)}, u32[]{:S(2)}, u32[]{:S(2)}) collective-permute-start(bf16[256,512]{1,0:T(8,128)(2,1)S(1)} %section.1.refs_0_), channel_id=1, source_target_pairs={{0,1},{1,0},{2,3},{3,2},{4,5},{5,4},{6,7},{7,6},{8,9},{9,8},{10,11... | collective-permute-start | bytes 786440 | tf_op jit(solution)/shard_map/ppermute | solution.py:322
  12.5 1.2 %collective-permute-done.4.refs_1_ = bf16[256,512]{1,0:T(8,128)(2,1)S(1)} collective-permute-done((bf16[256,512]{1,0:T(8,128)(2,1)S(1)}, bf16[256,512]{1,0:T(8,128)(2,1)S(1)}, u32[]{:S(2)}, u32[]{:S(2)}) %collective-permute-start.4) | collective-permute-done | bytes 262176 | tf_op jit(solution)/shard_map/ppermute | solution.py:322
  13.6 1.7 %transform.1 = (bf16[2,2,80,256]{3,2,1,0:T(8,128)(2,1)S(1)}, bf16[2,2,80,256]{3,2,1,0:T(8,128)(2,1)S(1)}, bf16[2,2,80,256]{3,2,1,0:T(8,128)(2,1)S(1)}, bf16[1,2,80,256]{3,2,1,0:T(8,128)(2,1)S(1)}) custom-call(bf16[256,512]{1,0:T(8,128)(2,1)S(1)} %section.1.refs_0_, bf16[256,512]{1,0:T(8,128)(2,1)S(1)} %collective-permute-done.4.refs_1_, ...), custom_call_target="tpu_custom_call" | custom-call | flops 2400000000 | tf_op jit(solution)/shard_map/transform/pallas_call | solution.py:454
  15.4 2.3 %collective-permute-start.5 = (bf16[2,2,80,256]{3,2,1,0:T(8,128)(2,1)S(1)}, bf16[2,2,80,256]{3,2,1,0:T(8,128)(2,1)S(1)}, u32[]{:S(2)}, u32[]{:S(2)}) collective-permute-start(bf16[2,2,80,256]{3,2,1,0:T(8,128)(2,1)S(1)} %get-tuple-element.41), channel_id=1, source_target_pairs={{0,1},{1,7},{2,3},{3,5},{4,2},{5,11},{6,0},{7,9},{8,6},{9,15},{10,... | collective-permute-start | bytes 491528 | tf_op jit(solution)/shard_map/ppermute | solution.py:337
  17.6 0.0 collective-permute-start.7
  17.6 0.7 %collective-permute-start.6 = (bf16[1,2,80,256]{3,2,1,0:T(8,128)(2,1)S(1)}, bf16[1,2,80,256]{3,2,1,0:T(8,128)(2,1)S(1)}, u32[]{:S(2)}, u32[]{:S(2)}) collective-permute-start(bf16[1,2,80,256]{3,2,1,0:T(8,128)(2,1)S(1)} %get-tuple-element.42), channel_id=1, source_target_pairs={{0,2},{2,0},{1,3},{3,1},{4,6},{6,4},{5,7},{7,5},{8,10},{10,8},{9,1... | collective-permute-start | bytes 245768 | tf_op jit(solution)/shard_map/ppermute | solution.py:485
  18.3 0.8 %collective-permute-start.8 = (s32[52]{0:T(128)S(1)}, s32[52]{0:T(128)S(1)}, u32[]{:S(2)}, u32[]{:S(2)}) collective-permute-start(s32[52]{0:T(128)S(1)} %copy-done.5), channel_id=1, source_target_pairs={{0,2},{2,0},{1,3},{3,1},{4,6},{6,4},{5,7},{7,5},{8,10},{10,8},{9,1... | collective-permute-start | bytes 632 | tf_op jit(solution)/shard_map/ppermute | solution.py:438
  19.1 5.1 %collective-permute-done.8.refs_1_ = s32[52]{0:T(128)S(1)} collective-permute-done((s32[52]{0:T(128)S(1)}, s32[52]{0:T(128)S(1)}, u32[]{:S(2)}, u32[]{:S(2)}) %collective-permute-start.8) | collective-permute-done | bytes 240 | tf_op jit(solution)/shard_map/ppermute | solution.py:438
  24.3 1.4 %place.1 = (bf16[256,560]{1,0:T(8,128)(2,1)S(1)}, bf16[7,256,384]{2,1,0:T(8,128)(2,1)S(1)}, bf16[256,400]{1,0:T(8,128)(2,1)S(1)}, bf16[5,256,384]{2,1,0:T(8,128)(2,1)S(1)}) custom-call(s32[52]{0:T(128)S(1)} %copy-done.5, s32[52]{0:T(128)S(1)} %collective-permute-done.8.refs_1_), custom_call_target="tpu_custom_call" | custom-call | flops 40000000 | tf_op jit(solution)/shard_map/place/pallas_call | solution.py:502
  25.7 0.0 collective-permute-done.6.refs_1_
  25.7 0.0 collective-permute-done.5.refs_0_
  25.7 0.0 collective-permute-done.7.refs_2_
  25.7 0.5 %collective-permute-start.11 = (bf16[2,2,80,256]{3,2,1,0:T(8,128)(2,1)S(1)}, bf16[2,2,80,256]{3,2,1,0:T(8,128)(2,1)S(1)}, u32[]{:S(2)}, u32[]{:S(2)}) collective-permute-start(bf16[2,2,80,256]{3,2,1,0:T(8,128)(2,1)S(1)} %collective-permute-done.7.refs_2_), channel_id=1, source_target_pairs={{0,1},{1,0},{2,3},{3,2},{4,5},{5,4},{6,7},{7,6},{8,9},{9,8},{10,11... | collective-permute-start | bytes 491528 | tf_op jit(solution)/shard_map/ppermute | solution.py:322
  26.3 0.1 collective-permute-start.9
  26.4 0.4 %collective-permute-start.10 = (bf16[1,2,80,256]{3,2,1,0:T(8,128)(2,1)S(1)}, bf16[1,2,80,256]{3,2,1,0:T(8,128)(2,1)S(1)}, u32[]{:S(2)}, u32[]{:S(2)}) collective-permute-start(bf16[1,2,80,256]{3,2,1,0:T(8,128)(2,1)S(1)} %collective-permute-done.6.refs_1_), channel_id=1, source_target_pairs={{0,1},{1,0},{2,3},{3,2},{4,5},{5,4},{6,7},{7,6},{8,9},{9,8},{10,11... | collective-permute-start | bytes 245768 | tf_op jit(solution)/shard_map/ppermute | solution.py:322
  26.8 0.9 %deposit.2.refs_3_ = f32[4,2,64,384]{3,2,1,0:T(8,128)S(1)} custom-call(bf16[256,560]{1,0:T(8,128)(2,1)S(1)} %get-tuple-element.54.left, bf16[7,256,384]{2,1,0:T(8,128)(2,1)S(1)} %get-tuple-element.55.columns, bf16[2,2,80,256]{3,2,1,0:T(8,128)(2,1)S(1)} %collective-permute-done.5.refs_0_, bf16[1,2,80,256]{3,2,1,0:T(8,128)(2,1)S(1)} %collective-permute-done.6.refs_1_, ...), custom_call_target="tpu_custom_call" | custom-call | flops 40000000 | tf_op jit(solution)/shard_map/deposit/pallas_call | solution.py:523
  27.6 0.1 collective-permute-done.10.refs_1_
  27.8 0.0 collective-permute-done.11.refs_2_
  27.8 0.0 collective-permute-done.9.refs_0_
  27.8 1.4 %deposit.3 = f32[4,2,64,384]{3,2,1,0:T(8,128)} custom-call(bf16[256,400]{1,0:T(8,128)(2,1)S(1)} %get-tuple-element.49.left, bf16[5,256,384]{2,1,0:T(8,128)(2,1)S(1)} %get-tuple-element.50.columns, bf16[2,2,80,256]{3,2,1,0:T(8,128)(2,1)S(1)} %collective-permute-done.9.refs_0_, bf16[1,2,80,256]{3,2,1,0:T(8,128)(2,1)S(1)} %collective-permute-done.10.refs_1_, ...), custom_call_target="tpu_custom_call" | custom-call | flops 40000000 | tf_op jit(solution)/shard_map/deposit/pallas_call | solution.py:523
  (1 shorter events, 0.0 us)
Async XLA Ops:
  0.0 1.5 %copy-start.2 = (bf16[4,2,128,384]{3,2,1,0:T(8,128)(2,1)S(1)}, bf16[4,2,128,384]{3,2,1,0:T(8,128)(2,1)}, u32[]{:S(2)}) copy-start(bf16[4,2,128,384]{3,2,1,0:T(8,128)(2,1)} %refs_1_.5) | copy-start | bytes 2359300
  1.5 0.7 %copy-start.4 = (s32[52]{0:T(128)S(1)}, s32[52]{0:T(128)}, u32[]{:S(2)}) copy-start(s32[52]{0:T(128)} %fill.1.refs_0_.table) | copy-start | bytes 628
  3.3 1.9 %collective-permute-start = (bf16[2,2,128,256]{3,2,1,0:T(8,128)(2,1)S(1)}, bf16[2,2,128,256]{3,2,1,0:T(8,128)(2,1)S(1)}, u32[]{:S(2)}, u32[]{:S(2)}) collective-permute-start(bf16[2,2,128,256]{3,2,1,0:T(8,128)(2,1)S(1)} %project_far.1), channel_id=1, source_target_pairs={{0,1},{1,0},{2,3},{3,2},{4,5},{5,4},{6,7},{7,6},{8,9},{9,8},{10,11... | collective-permute-start | bytes 786440 | tf_op jit(solution)/shard_map/ppermute | solution.py:322
  5.2 0.7 %copy-start.5 = (s32[52]{0:T(128)S(1)}, s32[52]{0:T(128)}, u32[]{:S(2)}) copy-start(s32[52]{0:T(128)} %fill.1.refs_0_.table) | copy-start | bytes 628
  5.3 3.6 %copy-start.3 = (bf16[2,128,256]{2,1,0:T(8,128)(2,1)S(1)}, bf16[2,128,256]{2,1,0:T(8,128)(2,1)}, u32[]{:S(2)}) copy-start(bf16[2,128,256]{2,1,0:T(8,128)(2,1)} %refs_2_.1) | copy-start | bytes 393220
  5.3 5.5 %collective-permute-start.1 = (bf16[2,2,128,256]{3,2,1,0:T(8,128)(2,1)S(1)}, bf16[2,2,128,256]{3,2,1,0:T(8,128)(2,1)S(1)}, u32[]{:S(2)}, u32[]{:S(2)}) collective-permute-start(bf16[2,2,128,256]{3,2,1,0:T(8,128)(2,1)S(1)} %add.1), channel_id=1, source_target_pairs={{0,4},{1,0},{2,6},{3,2},{4,8},{5,1},{6,10},{7,3},{8,12},{9,5},{10,... | collective-permute-start | bytes 786440 | tf_op jit(solution)/shard_map/ppermute | solution.py:337
  7.4 3.4 %copy-start = (bf16[2,512,512]{2,1,0:T(8,128)(2,1)S(1)}, bf16[2,512,512]{2,1,0:T(8,128)(2,1)}, u32[]{:S(2)}) copy-start(bf16[2,512,512]{2,1,0:T(8,128)(2,1)} %constant.2.clone.tab.refs_5_) | copy-start | bytes 3145732
  7.4 3.4 %copy-start.1 = (bf16[2,256,256]{2,1,0:T(8,128)(2,1)S(1)}, bf16[2,256,256]{2,1,0:T(8,128)(2,1)}, u32[]{:S(2)}) copy-start(bf16[2,256,256]{2,1,0:T(8,128)(2,1)} %refs_4_.1) | copy-start | bytes 786436
  7.4 3.4 %collective-permute-start.3 = (bf16[2,2,128,256]{3,2,1,0:T(8,128)(2,1)S(1)}, bf16[2,2,128,256]{3,2,1,0:T(8,128)(2,1)S(1)}, u32[]{:S(2)}, u32[]{:S(2)}) collective-permute-start(bf16[2,2,128,256]{3,2,1,0:T(8,128)(2,1)S(1)} %get-tuple-element.37), channel_id=1, source_target_pairs={{0,1},{1,0},{2,3},{3,2},{4,5},{5,4},{6,7},{7,6},{8,9},{9,8},{10,11... | collective-permute-start | bytes 786440 | tf_op jit(solution)/shard_map/ppermute | solution.py:322
  8.9 1.3 %collective-permute-start.2 = (bf16[2,128,256]{2,1,0:T(8,128)(2,1)S(1)}, bf16[2,128,256]{2,1,0:T(8,128)(2,1)S(1)}, u32[]{:S(2)}, u32[]{:S(2)}) collective-permute-start(bf16[2,128,256]{2,1,0:T(8,128)(2,1)S(1)} %copy-done.3), channel_id=1, source_target_pairs={{0,1},{1,0},{2,3},{3,2},{4,5},{5,4},{6,7},{7,6},{8,9},{9,8},{10,11... | collective-permute-start | bytes 393224 | tf_op jit(solution)/shard_map/ppermute | solution.py:322
  11.2 2.4 %collective-permute-start.4 = (bf16[256,512]{1,0:T(8,128)(2,1)S(1)}, bf16[256,512]{1,0:T(8,128)(2,1)S(1)}, u32[]{:S(2)}, u32[]{:S(2)}) collective-permute-start(bf16[256,512]{1,0:T(8,128)(2,1)S(1)} %section.1.refs_0_), channel_id=1, source_target_pairs={{0,1},{1,0},{2,3},{3,2},{4,5},{5,4},{6,7},{7,6},{8,9},{9,8},{10,11... | collective-permute-start | bytes 786440 | tf_op jit(solution)/shard_map/ppermute | solution.py:322
  15.4 10.4 %collective-permute-start.5 = (bf16[2,2,80,256]{3,2,1,0:T(8,128)(2,1)S(1)}, bf16[2,2,80,256]{3,2,1,0:T(8,128)(2,1)S(1)}, u32[]{:S(2)}, u32[]{:S(2)}) collective-permute-start(bf16[2,2,80,256]{3,2,1,0:T(8,128)(2,1)S(1)} %get-tuple-element.41), channel_id=1, source_target_pairs={{0,1},{1,7},{2,3},{3,5},{4,2},{5,11},{6,0},{7,9},{8,6},{9,15},{10,... | collective-permute-start | bytes 491528 | tf_op jit(solution)/shard_map/ppermute | solution.py:337
  17.6 8.1 %collective-permute-start.7 = (bf16[2,2,80,256]{3,2,1,0:T(8,128)(2,1)S(1)}, bf16[2,2,80,256]{3,2,1,0:T(8,128)(2,1)S(1)}, u32[]{:S(2)}, u32[]{:S(2)}) collective-permute-start(bf16[2,2,80,256]{3,2,1,0:T(8,128)(2,1)S(1)} %get-tuple-element.43), channel_id=1, source_target_pairs={{0,1},{1,5},{2,3},{3,7},{4,0},{5,9},{6,2},{7,11},{8,4},{9,13},{10,... | collective-permute-start | bytes 491528 | tf_op jit(solution)/shard_map/ppermute | solution.py:337
  17.6 8.1 %collective-permute-start.6 = (bf16[1,2,80,256]{3,2,1,0:T(8,128)(2,1)S(1)}, bf16[1,2,80,256]{3,2,1,0:T(8,128)(2,1)S(1)}, u32[]{:S(2)}, u32[]{:S(2)}) collective-permute-start(bf16[1,2,80,256]{3,2,1,0:T(8,128)(2,1)S(1)} %get-tuple-element.42), channel_id=1, source_target_pairs={{0,2},{2,0},{1,3},{3,1},{4,6},{6,4},{5,7},{7,5},{8,10},{10,8},{9,1... | collective-permute-start | bytes 245768 | tf_op jit(solution)/shard_map/ppermute | solution.py:485
  18.3 6.0 %collective-permute-start.8 = (s32[52]{0:T(128)S(1)}, s32[52]{0:T(128)S(1)}, u32[]{:S(2)}, u32[]{:S(2)}) collective-permute-start(s32[52]{0:T(128)S(1)} %copy-done.5), channel_id=1, source_target_pairs={{0,2},{2,0},{1,3},{3,1},{4,6},{6,4},{5,7},{7,5},{8,10},{10,8},{9,1... | collective-permute-start | bytes 632 | tf_op jit(solution)/shard_map/ppermute | solution.py:438
  25.7 2.0 %collective-permute-start.11 = (bf16[2,2,80,256]{3,2,1,0:T(8,128)(2,1)S(1)}, bf16[2,2,80,256]{3,2,1,0:T(8,128)(2,1)S(1)}, u32[]{:S(2)}, u32[]{:S(2)}) collective-permute-start(bf16[2,2,80,256]{3,2,1,0:T(8,128)(2,1)S(1)} %collective-permute-done.7.refs_2_), channel_id=1, source_target_pairs={{0,1},{1,0},{2,3},{3,2},{4,5},{5,4},{6,7},{7,6},{8,9},{9,8},{10,11... | collective-permute-start | bytes 491528 | tf_op jit(solution)/shard_map/ppermute | solution.py:322
  26.3 1.5 %collective-permute-start.9 = (bf16[2,2,80,256]{3,2,1,0:T(8,128)(2,1)S(1)}, bf16[2,2,80,256]{3,2,1,0:T(8,128)(2,1)S(1)}, u32[]{:S(2)}, u32[]{:S(2)}) collective-permute-start(bf16[2,2,80,256]{3,2,1,0:T(8,128)(2,1)S(1)} %collective-permute-done.5.refs_0_), channel_id=1, source_target_pairs={{0,1},{1,0},{2,3},{3,2},{4,5},{5,4},{6,7},{7,6},{8,9},{9,8},{10,11... | collective-permute-start | bytes 491528 | tf_op jit(solution)/shard_map/ppermute | solution.py:322
  26.4 1.4 %collective-permute-start.10 = (bf16[1,2,80,256]{3,2,1,0:T(8,128)(2,1)S(1)}, bf16[1,2,80,256]{3,2,1,0:T(8,128)(2,1)S(1)}, u32[]{:S(2)}, u32[]{:S(2)}) collective-permute-start(bf16[1,2,80,256]{3,2,1,0:T(8,128)(2,1)S(1)} %collective-permute-done.6.refs_1_), channel_id=1, source_target_pairs={{0,1},{1,0},{2,3},{3,2},{4,5},{5,4},{6,7},{7,6},{8,9},{9,8},{10,11... | collective-permute-start | bytes 245768 | tf_op jit(solution)/shard_map/ppermute | solution.py:322
